TPU v7x, 128 devices: a whole 4x4x4 slice. The times are simulated.
128 devices in a mesh: col: 4 (over y), row: 32 (over z, x, core).
Axes of the slice: x: 4, y: 4, z: 4, core: 2. Of those that a mesh axis runs over, the one named last changes fastest.
Arguments:
- eigenvectors: float32 [256, 131072], P(('col', 'row')), may hold values from -6 to 6
- reflectors: float32 [32, 131072], P('row', 'col'), may hold values from -6 to 6
- sweep_ranges: int32 [32, 2], replicated, may hold values from 0 to 131072, as said below
Outputs:
- transformed: float32 [256, 131072], P('col', 'row')
Inputs may be any that keep to these rules, and one draw needn't show every extreme that they name: `sweep_ranges`: in every sweep the first entry is below the second by at least 65536 rows, and sweep 0 covers all 131072 rows.
All inputs are finite; a program needn't handle non-finite values.
Results may differ from a plain program's by a relative error of at most 0.0003.
Values sent between devices are 32-bit elements; how exact they have to be, the bound alone decides.
No kernel may reach another device: no remote copies, remote signals or barrier semaphores. Data moves between devices by JAX's collectives and lax.ppermute only.
A program may use at most 128 MiB of HBM per device.

v0:
```python
import jax
import jax.numpy as jnp
from jax import lax
from jax.sharding import PartitionSpec as P

NB = 128
SWEEPS = 32


def with_halo(block, sides, width):
    for axis, dim in sides:
        count = lax.axis_size(axis)
        forward = [(i, i + 1) for i in range(count - 1)]
        backward = [(target, source) for source, target in forward]
        low = lax.ppermute(
            lax.slice_in_dim(block, block.shape[dim] - width, None, axis=dim), axis, forward
        )
        high = lax.ppermute(lax.slice_in_dim(block, 0, width, axis=dim), axis, backward)
        block = jnp.concatenate([low, block, high], axis=dim)
    return block


def apply_blocks(window, reflector_window, first_start, lower_row, upper_row):
    block_count = reflector_window.shape[0] // NB
    blocks = window.reshape(window.shape[0], block_count, NB)
    vectors = reflector_window.reshape(block_count, NB)
    starts = first_start + NB * lax.iota(jnp.int32, block_count)
    active_mask = jnp.logical_and(starts >= lower_row, starts + NB <= upper_row).astype(jnp.float32)
    squares = jnp.sum(vectors * vectors, axis=1)
    factors = active_mask * 2.0 / (squares + 1.0 - active_mask)
    inner = jnp.einsum("cbi,bi->cb", blocks, vectors, precision=lax.Precision.HIGHEST)
    updated = blocks - (inner * factors[None, :])[:, :, None] * vectors[None, :, :]
    return updated.reshape(window.shape)


def receive_owned(eigenvectors, sweep_rows):
    vectors_in = lax.all_to_all(eigenvectors, "row", split_axis=1, concat_axis=0, tiled=True)
    local_rows = lax.all_to_all(sweep_rows, "row", split_axis=1, concat_axis=0, tiled=True)
    return (vectors_in, local_rows)


def per_device(eigenvectors, reflectors, sweep_ranges):
    sweep_rows = lax.all_gather(reflectors, "col", axis=1, tiled=True)
    vectors_in, local_rows = receive_owned(eigenvectors, sweep_rows)
    row_count = vectors_in.shape[1]
    extended_rows = with_halo(local_rows, (("row", 1),), NB)
    global_base = lax.axis_index("row") * row_count - NB

    def one_sweep(sweep_step, vectors_now):
        sweep_index = SWEEPS - 1 - sweep_step
        ranges_now = lax.dynamic_index_in_dim(sweep_ranges, sweep_index, 0, keepdims=False)
        block_phase = ranges_now[0] % NB
        extended = with_halo(vectors_now, (("row", 1),), NB)
        reflector_row = lax.dynamic_index_in_dim(extended_rows, sweep_index, 0, keepdims=False)
        window = lax.dynamic_slice_in_dim(extended, block_phase, row_count + NB, 1)
        reflector_window = lax.dynamic_slice_in_dim(reflector_row, block_phase, row_count + NB, 0)
        updated = apply_blocks(
            window, reflector_window, global_base + block_phase, ranges_now[0], ranges_now[1]
        )
        return lax.dynamic_slice_in_dim(updated, NB - block_phase, row_count, 1)

    result = lax.fori_loop(0, SWEEPS, one_sweep, vectors_in)
    return result


def solution(mesh):
    placed = (P(("col", "row"), None), P("row", "col"), P())
    return jax.shard_map(
        per_device, mesh=mesh, in_specs=placed, out_specs=P("col", "row"), check_vma=False
    )
```

profile of v0, /device:TPU:40, one launch (start us, length us, event | category | flops | bytes accessed | tf_op | source)
XLA Modules:
  0.0 562.1 jit_solution(6375301506774415678)
XLA Ops:
  0.0 13.9 %all_gather.3 = f32[1,131072]{1,0:T(1,128)S(1)} all-gather(f32[1,32768]{1,0:T(1,128)} %param.6), channel_id=1, replica_groups=mesh['col'=4,'row'=32] {'col'}, dimensions={1}, use_global_device_ids=true | all-gather | bytes 655360 | tf_op jit(solution)/shard_map/all_gather | solution.py:43
  13.9 17.5 %all_to_all.35 = f32[1,32,4096]{2,0,1:T(1,128)S(1)} all-to-all(f32[1,32,4096]{2,0,1:T(1,128)S(1)} %bitcast.57), channel_id=1, replica_groups=mesh['col'=4,'row'=32] {'row'}, dimensions={1} | all-to-all | bytes 1048576 | tf_op jit(solution)/shard_map/all_to_all | solution.py:38
  31.4 5.9 %all-to-all-start = ((f32[2,32,4096]{2,0,1:T(2,128)}), f32[2,32,4096]{2,0,1:T(2,128)S(1)}, u32[]{:S(2)}, u32[]{:S(2)}) async-start(f32[2,32,4096]{2,0,1:T(2,128)} %bitcast.5), calls=%async_computation | async-start | bytes 2097152 | tf_op jit(solution)/shard_map/all_to_all | solution.py:37
  45.4 6.9 %collective-permute-done.2 = f32[32,128]{1,0:T(8,128)S(1)} collective-permute-done((f32[32,128]{1,0:T(8,128)S(1)}, f32[32,128]{1,0:T(8,128)S(1)}, u32[]{:S(2)}, u32[]{:S(2)}) %collective-permute-start.2) | collective-permute-done | bytes 16416 | tf_op jit(solution)/shard_map/ppermute | solution.py:15
  53.1 508.0 %while.16 = (s32[]{:T(128)}, f32[64,4096]{1,0:T(8,128)S(1)}, s32[32,2]{0,1:T(2,128)S(1)}, f32[32,4352]{1,0:T(8,128)S(1)}, s32[]{:T(128)}, /*index=5*/s32[]{:T(12...) while((s32[]{:T(128)}, f32[64,4096]{1,0:T(8,128)S(1)}, ...), condition=%wide.region_2.3_spmd, body=%wide.region_0.2_spmd.sunk | while | flops 4319909 | bytes 10228280 | solution.py:62
  70.9 5.8 %collective-permute-start.1 = (f32[64,128]{1,0:T(8,128)S(1)}, f32[64,128]{1,0:T(8,128)S(1)}, u32[]{:S(2)}, u32[]{:S(2)}) collective-permute-start(f32[64,128]{1,0:T(8,128)S(1)} %get-tuple-element.219), channel_id=1, source_target_pairs={{1,0},{2,1},{3,2},{4,3},{5,4},{6,5},{7,6},{8,7},{9,8},{10,9},{11,1... | collective-permute-start | bytes 98312 | tf_op jit(solution)/shard_map/while/body/eval_jaxpr/ppermute | solution.py:18
  86.8 5.8 %collective-permute-start.1 = (f32[64,128]{1,0:T(8,128)S(1)}, f32[64,128]{1,0:T(8,128)S(1)}, u32[]{:S(2)}, u32[]{:S(2)}) collective-permute-start(f32[64,128]{1,0:T(8,128)S(1)} %get-tuple-element.219), channel_id=1, source_target_pairs={{1,0},{2,1},{3,2},{4,3},{5,4},{6,5},{7,6},{8,7},{9,8},{10,9},{11,1... | collective-permute-start | bytes 98312 | tf_op jit(solution)/shard_map/while/body/eval_jaxpr/ppermute | solution.py:18
  102.7 5.8 %collective-permute-start.1 = (f32[64,128]{1,0:T(8,128)S(1)}, f32[64,128]{1,0:T(8,128)S(1)}, u32[]{:S(2)}, u32[]{:S(2)}) collective-permute-start(f32[64,128]{1,0:T(8,128)S(1)} %get-tuple-element.219), channel_id=1, source_target_pairs={{1,0},{2,1},{3,2},{4,3},{5,4},{6,5},{7,6},{8,7},{9,8},{10,9},{11,1... | collective-permute-start | bytes 98312 | tf_op jit(solution)/shard_map/while/body/eval_jaxpr/ppermute | solution.py:18
  118.5 5.8 %collective-permute-start.1 = (f32[64,128]{1,0:T(8,128)S(1)}, f32[64,128]{1,0:T(8,128)S(1)}, u32[]{:S(2)}, u32[]{:S(2)}) collective-permute-start(f32[64,128]{1,0:T(8,128)S(1)} %get-tuple-element.219), channel_id=1, source_target_pairs={{1,0},{2,1},{3,2},{4,3},{5,4},{6,5},{7,6},{8,7},{9,8},{10,9},{11,1... | collective-permute-start | bytes 98312 | tf_op jit(solution)/shard_map/while/body/eval_jaxpr/ppermute | solution.py:18
  134.4 5.8 %collective-permute-start.1 = (f32[64,128]{1,0:T(8,128)S(1)}, f32[64,128]{1,0:T(8,128)S(1)}, u32[]{:S(2)}, u32[]{:S(2)}) collective-permute-start(f32[64,128]{1,0:T(8,128)S(1)} %get-tuple-element.219), channel_id=1, source_target_pairs={{1,0},{2,1},{3,2},{4,3},{5,4},{6,5},{7,6},{8,7},{9,8},{10,9},{11,1... | collective-permute-start | bytes 98312 | tf_op jit(solution)/shard_map/while/body/eval_jaxpr/ppermute | solution.py:18
  150.3 5.8 %collective-permute-start.1 = (f32[64,128]{1,0:T(8,128)S(1)}, f32[64,128]{1,0:T(8,128)S(1)}, u32[]{:S(2)}, u32[]{:S(2)}) collective-permute-start(f32[64,128]{1,0:T(8,128)S(1)} %get-tuple-element.219), channel_id=1, source_target_pairs={{1,0},{2,1},{3,2},{4,3},{5,4},{6,5},{7,6},{8,7},{9,8},{10,9},{11,1... | collective-permute-start | bytes 98312 | tf_op jit(solution)/shard_map/while/body/eval_jaxpr/ppermute | solution.py:18
  182.0 5.8 %collective-permute-start.1 = (f32[64,128]{1,0:T(8,128)S(1)}, f32[64,128]{1,0:T(8,128)S(1)}, u32[]{:S(2)}, u32[]{:S(2)}) collective-permute-start(f32[64,128]{1,0:T(8,128)S(1)} %get-tuple-element.219), channel_id=1, source_target_pairs={{1,0},{2,1},{3,2},{4,3},{5,4},{6,5},{7,6},{8,7},{9,8},{10,9},{11,1... | collective-permute-start | bytes 98312 | tf_op jit(solution)/shard_map/while/body/eval_jaxpr/ppermute | solution.py:18
  197.9 5.8 %collective-permute-start.1 = (f32[64,128]{1,0:T(8,128)S(1)}, f32[64,128]{1,0:T(8,128)S(1)}, u32[]{:S(2)}, u32[]{:S(2)}) collective-permute-start(f32[64,128]{1,0:T(8,128)S(1)} %get-tuple-element.219), channel_id=1, source_target_pairs={{1,0},{2,1},{3,2},{4,3},{5,4},{6,5},{7,6},{8,7},{9,8},{10,9},{11,1... | collective-permute-start | bytes 98312 | tf_op jit(solution)/shard_map/while/body/eval_jaxpr/ppermute | solution.py:18
  213.8 5.8 %collective-permute-start.1 = (f32[64,128]{1,0:T(8,128)S(1)}, f32[64,128]{1,0:T(8,128)S(1)}, u32[]{:S(2)}, u32[]{:S(2)}) collective-permute-start(f32[64,128]{1,0:T(8,128)S(1)} %get-tuple-element.219), channel_id=1, source_target_pairs={{1,0},{2,1},{3,2},{4,3},{5,4},{6,5},{7,6},{8,7},{9,8},{10,9},{11,1... | collective-permute-start | bytes 98312 | tf_op jit(solution)/shard_map/while/body/eval_jaxpr/ppermute | solution.py:18
  229.7 5.8 %collective-permute-start.1 = (f32[64,128]{1,0:T(8,128)S(1)}, f32[64,128]{1,0:T(8,128)S(1)}, u32[]{:S(2)}, u32[]{:S(2)}) collective-permute-start(f32[64,128]{1,0:T(8,128)S(1)} %get-tuple-element.219), channel_id=1, source_target_pairs={{1,0},{2,1},{3,2},{4,3},{5,4},{6,5},{7,6},{8,7},{9,8},{10,9},{11,1... | collective-permute-start | bytes 98312 | tf_op jit(solution)/shard_map/while/body/eval_jaxpr/ppermute | solution.py:18
  245.5 5.8 %collective-permute-start.1 = (f32[64,128]{1,0:T(8,128)S(1)}, f32[64,128]{1,0:T(8,128)S(1)}, u32[]{:S(2)}, u32[]{:S(2)}) collective-permute-start(f32[64,128]{1,0:T(8,128)S(1)} %get-tuple-element.219), channel_id=1, source_target_pairs={{1,0},{2,1},{3,2},{4,3},{5,4},{6,5},{7,6},{8,7},{9,8},{10,9},{11,1... | collective-permute-start | bytes 98312 | tf_op jit(solution)/shard_map/while/body/eval_jaxpr/ppermute | solution.py:18
  277.3 5.8 %collective-permute-start.1 = (f32[64,128]{1,0:T(8,128)S(1)}, f32[64,128]{1,0:T(8,128)S(1)}, u32[]{:S(2)}, u32[]{:S(2)}) collective-permute-start(f32[64,128]{1,0:T(8,128)S(1)} %get-tuple-element.219), channel_id=1, source_target_pairs={{1,0},{2,1},{3,2},{4,3},{5,4},{6,5},{7,6},{8,7},{9,8},{10,9},{11,1... | collective-permute-start | bytes 98312 | tf_op jit(solution)/shard_map/while/body/eval_jaxpr/ppermute | solution.py:18
  293.2 5.8 %collective-permute-start.1 = (f32[64,128]{1,0:T(8,128)S(1)}, f32[64,128]{1,0:T(8,128)S(1)}, u32[]{:S(2)}, u32[]{:S(2)}) collective-permute-start(f32[64,128]{1,0:T(8,128)S(1)} %get-tuple-element.219), channel_id=1, source_target_pairs={{1,0},{2,1},{3,2},{4,3},{5,4},{6,5},{7,6},{8,7},{9,8},{10,9},{11,1... | collective-permute-start | bytes 98312 | tf_op jit(solution)/shard_map/while/body/eval_jaxpr/ppermute | solution.py:18
  309.0 5.8 %collective-permute-start.1 = (f32[64,128]{1,0:T(8,128)S(1)}, f32[64,128]{1,0:T(8,128)S(1)}, u32[]{:S(2)}, u32[]{:S(2)}) collective-permute-start(f32[64,128]{1,0:T(8,128)S(1)} %get-tuple-element.219), channel_id=1, source_target_pairs={{1,0},{2,1},{3,2},{4,3},{5,4},{6,5},{7,6},{8,7},{9,8},{10,9},{11,1... | collective-permute-start | bytes 98312 | tf_op jit(solution)/shard_map/while/body/eval_jaxpr/ppermute | solution.py:18
  324.9 5.8 %collective-permute-start.1 = (f32[64,128]{1,0:T(8,128)S(1)}, f32[64,128]{1,0:T(8,128)S(1)}, u32[]{:S(2)}, u32[]{:S(2)}) collective-permute-start(f32[64,128]{1,0:T(8,128)S(1)} %get-tuple-element.219), channel_id=1, source_target_pairs={{1,0},{2,1},{3,2},{4,3},{5,4},{6,5},{7,6},{8,7},{9,8},{10,9},{11,1... | collective-permute-start | bytes 98312 | tf_op jit(solution)/shard_map/while/body/eval_jaxpr/ppermute | solution.py:18
  340.8 5.8 %collective-permute-start.1 = (f32[64,128]{1,0:T(8,128)S(1)}, f32[64,128]{1,0:T(8,128)S(1)}, u32[]{:S(2)}, u32[]{:S(2)}) collective-permute-start(f32[64,128]{1,0:T(8,128)S(1)} %get-tuple-element.219), channel_id=1, source_target_pairs={{1,0},{2,1},{3,2},{4,3},{5,4},{6,5},{7,6},{8,7},{9,8},{10,9},{11,1... | collective-permute-start | bytes 98312 | tf_op jit(solution)/shard_map/while/body/eval_jaxpr/ppermute | solution.py:18
  356.7 5.8 %collective-permute-start.1 = (f32[64,128]{1,0:T(8,128)S(1)}, f32[64,128]{1,0:T(8,128)S(1)}, u32[]{:S(2)}, u32[]{:S(2)}) collective-permute-start(f32[64,128]{1,0:T(8,128)S(1)} %get-tuple-element.219), channel_id=1, source_target_pairs={{1,0},{2,1},{3,2},{4,3},{5,4},{6,5},{7,6},{8,7},{9,8},{10,9},{11,1... | collective-permute-start | bytes 98312 | tf_op jit(solution)/shard_map/while/body/eval_jaxpr/ppermute | solution.py:18
  372.5 5.8 %collective-permute-start.1 = (f32[64,128]{1,0:T(8,128)S(1)}, f32[64,128]{1,0:T(8,128)S(1)}, u32[]{:S(2)}, u32[]{:S(2)}) collective-permute-start(f32[64,128]{1,0:T(8,128)S(1)} %get-tuple-element.219), channel_id=1, source_target_pairs={{1,0},{2,1},{3,2},{4,3},{5,4},{6,5},{7,6},{8,7},{9,8},{10,9},{11,1... | collective-permute-start | bytes 98312 | tf_op jit(solution)/shard_map/while/body/eval_jaxpr/ppermute | solution.py:18
  388.4 5.8 %collective-permute-start.1 = (f32[64,128]{1,0:T(8,128)S(1)}, f32[64,128]{1,0:T(8,128)S(1)}, u32[]{:S(2)}, u32[]{:S(2)}) collective-permute-start(f32[64,128]{1,0:T(8,128)S(1)} %get-tuple-element.219), channel_id=1, source_target_pairs={{1,0},{2,1},{3,2},{4,3},{5,4},{6,5},{7,6},{8,7},{9,8},{10,9},{11,1... | collective-permute-start | bytes 98312 | tf_op jit(solution)/shard_map/while/body/eval_jaxpr/ppermute | solution.py:18
  404.3 5.8 %collective-permute-start.1 = (f32[64,128]{1,0:T(8,128)S(1)}, f32[64,128]{1,0:T(8,128)S(1)}, u32[]{:S(2)}, u32[]{:S(2)}) collective-permute-start(f32[64,128]{1,0:T(8,128)S(1)} %get-tuple-element.219), channel_id=1, source_target_pairs={{1,0},{2,1},{3,2},{4,3},{5,4},{6,5},{7,6},{8,7},{9,8},{10,9},{11,1... | collective-permute-start | bytes 98312 | tf_op jit(solution)/shard_map/while/body/eval_jaxpr/ppermute | solution.py:18
  420.2 5.8 %collective-permute-start.1 = (f32[64,128]{1,0:T(8,128)S(1)}, f32[64,128]{1,0:T(8,128)S(1)}, u32[]{:S(2)}, u32[]{:S(2)}) collective-permute-start(f32[64,128]{1,0:T(8,128)S(1)} %get-tuple-element.219), channel_id=1, source_target_pairs={{1,0},{2,1},{3,2},{4,3},{5,4},{6,5},{7,6},{8,7},{9,8},{10,9},{11,1... | collective-permute-start | bytes 98312 | tf_op jit(solution)/shard_map/while/body/eval_jaxpr/ppermute | solution.py:18
  436.0 5.8 %collective-permute-start.1 = (f32[64,128]{1,0:T(8,128)S(1)}, f32[64,128]{1,0:T(8,128)S(1)}, u32[]{:S(2)}, u32[]{:S(2)}) collective-permute-start(f32[64,128]{1,0:T(8,128)S(1)} %get-tuple-element.219), channel_id=1, source_target_pairs={{1,0},{2,1},{3,2},{4,3},{5,4},{6,5},{7,6},{8,7},{9,8},{10,9},{11,1... | collective-permute-start | bytes 98312 | tf_op jit(solution)/shard_map/while/body/eval_jaxpr/ppermute | solution.py:18
  451.9 5.8 %collective-permute-start.1 = (f32[64,128]{1,0:T(8,128)S(1)}, f32[64,128]{1,0:T(8,128)S(1)}, u32[]{:S(2)}, u32[]{:S(2)}) collective-permute-start(f32[64,128]{1,0:T(8,128)S(1)} %get-tuple-element.219), channel_id=1, source_target_pairs={{1,0},{2,1},{3,2},{4,3},{5,4},{6,5},{7,6},{8,7},{9,8},{10,9},{11,1... | collective-permute-start | bytes 98312 | tf_op jit(solution)/shard_map/while/body/eval_jaxpr/ppermute | solution.py:18
  467.8 5.8 %collective-permute-start.1 = (f32[64,128]{1,0:T(8,128)S(1)}, f32[64,128]{1,0:T(8,128)S(1)}, u32[]{:S(2)}, u32[]{:S(2)}) collective-permute-start(f32[64,128]{1,0:T(8,128)S(1)} %get-tuple-element.219), channel_id=1, source_target_pairs={{1,0},{2,1},{3,2},{4,3},{5,4},{6,5},{7,6},{8,7},{9,8},{10,9},{11,1... | collective-permute-start | bytes 98312 | tf_op jit(solution)/shard_map/while/body/eval_jaxpr/ppermute | solution.py:18
  483.7 5.8 %collective-permute-start.1 = (f32[64,128]{1,0:T(8,128)S(1)}, f32[64,128]{1,0:T(8,128)S(1)}, u32[]{:S(2)}, u32[]{:S(2)}) collective-permute-start(f32[64,128]{1,0:T(8,128)S(1)} %get-tuple-element.219), channel_id=1, source_target_pairs={{1,0},{2,1},{3,2},{4,3},{5,4},{6,5},{7,6},{8,7},{9,8},{10,9},{11,1... | collective-permute-start | bytes 98312 | tf_op jit(solution)/shard_map/while/body/eval_jaxpr/ppermute | solution.py:18
  499.5 5.8 %collective-permute-start.1 = (f32[64,128]{1,0:T(8,128)S(1)}, f32[64,128]{1,0:T(8,128)S(1)}, u32[]{:S(2)}, u32[]{:S(2)}) collective-permute-start(f32[64,128]{1,0:T(8,128)S(1)} %get-tuple-element.219), channel_id=1, source_target_pairs={{1,0},{2,1},{3,2},{4,3},{5,4},{6,5},{7,6},{8,7},{9,8},{10,9},{11,1... | collective-permute-start | bytes 98312 | tf_op jit(solution)/shard_map/while/body/eval_jaxpr/ppermute | solution.py:18
  515.4 5.8 %collective-permute-start.1 = (f32[64,128]{1,0:T(8,128)S(1)}, f32[64,128]{1,0:T(8,128)S(1)}, u32[]{:S(2)}, u32[]{:S(2)}) collective-permute-start(f32[64,128]{1,0:T(8,128)S(1)} %get-tuple-element.219), channel_id=1, source_target_pairs={{1,0},{2,1},{3,2},{4,3},{5,4},{6,5},{7,6},{8,7},{9,8},{10,9},{11,1... | collective-permute-start | bytes 98312 | tf_op jit(solution)/shard_map/while/body/eval_jaxpr/ppermute | solution.py:18
  (561 shorter events, 292.9 us)
Async XLA Ops:
  31.4 20.9 %all-to-all-start = ((f32[2,32,4096]{2,0,1:T(2,128)}), f32[2,32,4096]{2,0,1:T(2,128)S(1)}, u32[]{:S(2)}, u32[]{:S(2)}) async-start(f32[2,32,4096]{2,0,1:T(2,128)} %bitcast.5), calls=%async_computation | async-start | bytes 2097152 | tf_op jit(solution)/shard_map/all_to_all | solution.py:37
  37.7 14.6 %collective-permute-start.2 = (f32[32,128]{1,0:T(8,128)S(1)}, f32[32,128]{1,0:T(8,128)S(1)}, u32[]{:S(2)}, u32[]{:S(2)}) collective-permute-start(f32[32,128]{1,0:T(8,128)S(1)} %get-tuple-element.180), channel_id=1, source_target_pairs={{0,1},{1,2},{2,3},{3,4},{4,5},{5,6},{6,7},{7,8},{8,9},{9,10},{10,1... | collective-permute-start | bytes 49160 | tf_op jit(solution)/shard_map/ppermute | solution.py:15
  39.7 12.5 %collective-permute-start.3 = (f32[32,128]{1,0:T(8,128)S(1)}, f32[32,128]{1,0:T(8,128)S(1)}, u32[]{:S(2)}, u32[]{:S(2)}) collective-permute-start(f32[32,128]{1,0:T(8,128)S(1)} %get-tuple-element.181), channel_id=1, source_target_pairs={{1,0},{2,1},{3,2},{4,3},{5,4},{6,5},{7,6},{8,7},{9,8},{10,9},{11,1... | collective-permute-start | bytes 49160 | tf_op jit(solution)/shard_map/ppermute | solution.py:18
  53.1 12.0 %collective-permute-start = (f32[64,128]{1,0:T(8,128)S(1)}, f32[64,128]{1,0:T(8,128)S(1)}, u32[]{:S(2)}, u32[]{:S(2)}) collective-permute-start(f32[64,128]{1,0:T(8,128)S(1)} %get-tuple-element.218), channel_id=1, source_target_pairs={{0,1},{1,2},{2,3},{3,4},{4,5},{5,6},{6,7},{7,8},{8,9},{9,10},{10,1... | collective-permute-start | bytes 98312 | tf_op jit(solution)/shard_map/while/body/eval_jaxpr/ppermute | solution.py:15
  69.0 12.0 %collective-permute-start = (f32[64,128]{1,0:T(8,128)S(1)}, f32[64,128]{1,0:T(8,128)S(1)}, u32[]{:S(2)}, u32[]{:S(2)}) collective-permute-start(f32[64,128]{1,0:T(8,128)S(1)} %get-tuple-element.218), channel_id=1, source_target_pairs={{0,1},{1,2},{2,3},{3,4},{4,5},{5,6},{6,7},{7,8},{8,9},{9,10},{10,1... | collective-permute-start | bytes 98312 | tf_op jit(solution)/shard_map/while/body/eval_jaxpr/ppermute | solution.py:15
  84.9 12.0 %collective-permute-start = (f32[64,128]{1,0:T(8,128)S(1)}, f32[64,128]{1,0:T(8,128)S(1)}, u32[]{:S(2)}, u32[]{:S(2)}) collective-permute-start(f32[64,128]{1,0:T(8,128)S(1)} %get-tuple-element.218), channel_id=1, source_target_pairs={{0,1},{1,2},{2,3},{3,4},{4,5},{5,6},{6,7},{7,8},{8,9},{9,10},{10,1... | collective-permute-start | bytes 98312 | tf_op jit(solution)/shard_map/while/body/eval_jaxpr/ppermute | solution.py:15
  100.7 12.0 %collective-permute-start = (f32[64,128]{1,0:T(8,128)S(1)}, f32[64,128]{1,0:T(8,128)S(1)}, u32[]{:S(2)}, u32[]{:S(2)}) collective-permute-start(f32[64,128]{1,0:T(8,128)S(1)} %get-tuple-element.218), channel_id=1, source_target_pairs={{0,1},{1,2},{2,3},{3,4},{4,5},{5,6},{6,7},{7,8},{8,9},{9,10},{10,1... | collective-permute-start | bytes 98312 | tf_op jit(solution)/shard_map/while/body/eval_jaxpr/ppermute | solution.py:15
  116.6 12.0 %collective-permute-start = (f32[64,128]{1,0:T(8,128)S(1)}, f32[64,128]{1,0:T(8,128)S(1)}, u32[]{:S(2)}, u32[]{:S(2)}) collective-permute-start(f32[64,128]{1,0:T(8,128)S(1)} %get-tuple-element.218), channel_id=1, source_target_pairs={{0,1},{1,2},{2,3},{3,4},{4,5},{5,6},{6,7},{7,8},{8,9},{9,10},{10,1... | collective-permute-start | bytes 98312 | tf_op jit(solution)/shard_map/while/body/eval_jaxpr/ppermute | solution.py:15
  132.5 12.0 %collective-permute-start = (f32[64,128]{1,0:T(8,128)S(1)}, f32[64,128]{1,0:T(8,128)S(1)}, u32[]{:S(2)}, u32[]{:S(2)}) collective-permute-start(f32[64,128]{1,0:T(8,128)S(1)} %get-tuple-element.218), channel_id=1, source_target_pairs={{0,1},{1,2},{2,3},{3,4},{4,5},{5,6},{6,7},{7,8},{8,9},{9,10},{10,1... | collective-permute-start | bytes 98312 | tf_op jit(solution)/shard_map/while/body/eval_jaxpr/ppermute | solution.py:15
  148.4 12.0 %collective-permute-start = (f32[64,128]{1,0:T(8,128)S(1)}, f32[64,128]{1,0:T(8,128)S(1)}, u32[]{:S(2)}, u32[]{:S(2)}) collective-permute-start(f32[64,128]{1,0:T(8,128)S(1)} %get-tuple-element.218), channel_id=1, source_target_pairs={{0,1},{1,2},{2,3},{3,4},{4,5},{5,6},{6,7},{7,8},{8,9},{9,10},{10,1... | collective-permute-start | bytes 98312 | tf_op jit(solution)/shard_map/while/body/eval_jaxpr/ppermute | solution.py:15
  164.2 12.0 %collective-permute-start = (f32[64,128]{1,0:T(8,128)S(1)}, f32[64,128]{1,0:T(8,128)S(1)}, u32[]{:S(2)}, u32[]{:S(2)}) collective-permute-start(f32[64,128]{1,0:T(8,128)S(1)} %get-tuple-element.218), channel_id=1, source_target_pairs={{0,1},{1,2},{2,3},{3,4},{4,5},{5,6},{6,7},{7,8},{8,9},{9,10},{10,1... | collective-permute-start | bytes 98312 | tf_op jit(solution)/shard_map/while/body/eval_jaxpr/ppermute | solution.py:15
  180.1 12.0 %collective-permute-start = (f32[64,128]{1,0:T(8,128)S(1)}, f32[64,128]{1,0:T(8,128)S(1)}, u32[]{:S(2)}, u32[]{:S(2)}) collective-permute-start(f32[64,128]{1,0:T(8,128)S(1)} %get-tuple-element.218), channel_id=1, source_target_pairs={{0,1},{1,2},{2,3},{3,4},{4,5},{5,6},{6,7},{7,8},{8,9},{9,10},{10,1... | collective-permute-start | bytes 98312 | tf_op jit(solution)/shard_map/while/body/eval_jaxpr/ppermute | solution.py:15
  196.0 12.0 %collective-permute-start = (f32[64,128]{1,0:T(8,128)S(1)}, f32[64,128]{1,0:T(8,128)S(1)}, u32[]{:S(2)}, u32[]{:S(2)}) collective-permute-start(f32[64,128]{1,0:T(8,128)S(1)} %get-tuple-element.218), channel_id=1, source_target_pairs={{0,1},{1,2},{2,3},{3,4},{4,5},{5,6},{6,7},{7,8},{8,9},{9,10},{10,1... | collective-permute-start | bytes 98312 | tf_op jit(solution)/shard_map/while/body/eval_jaxpr/ppermute | solution.py:15
  211.9 12.0 %collective-permute-start = (f32[64,128]{1,0:T(8,128)S(1)}, f32[64,128]{1,0:T(8,128)S(1)}, u32[]{:S(2)}, u32[]{:S(2)}) collective-permute-start(f32[64,128]{1,0:T(8,128)S(1)} %get-tuple-element.218), channel_id=1, source_target_pairs={{0,1},{1,2},{2,3},{3,4},{4,5},{5,6},{6,7},{7,8},{8,9},{9,10},{10,1... | collective-permute-start | bytes 98312 | tf_op jit(solution)/shard_map/while/body/eval_jaxpr/ppermute | solution.py:15
  227.7 12.0 %collective-permute-start = (f32[64,128]{1,0:T(8,128)S(1)}, f32[64,128]{1,0:T(8,128)S(1)}, u32[]{:S(2)}, u32[]{:S(2)}) collective-permute-start(f32[64,128]{1,0:T(8,128)S(1)} %get-tuple-element.218), channel_id=1, source_target_pairs={{0,1},{1,2},{2,3},{3,4},{4,5},{5,6},{6,7},{7,8},{8,9},{9,10},{10,1... | collective-permute-start | bytes 98312 | tf_op jit(solution)/shard_map/while/body/eval_jaxpr/ppermute | solution.py:15
  243.6 12.0 %collective-permute-start = (f32[64,128]{1,0:T(8,128)S(1)}, f32[64,128]{1,0:T(8,128)S(1)}, u32[]{:S(2)}, u32[]{:S(2)}) collective-permute-start(f32[64,128]{1,0:T(8,128)S(1)} %get-tuple-element.218), channel_id=1, source_target_pairs={{0,1},{1,2},{2,3},{3,4},{4,5},{5,6},{6,7},{7,8},{8,9},{9,10},{10,1... | collective-permute-start | bytes 98312 | tf_op jit(solution)/shard_map/while/body/eval_jaxpr/ppermute | solution.py:15
  259.5 12.0 %collective-permute-start = (f32[64,128]{1,0:T(8,128)S(1)}, f32[64,128]{1,0:T(8,128)S(1)}, u32[]{:S(2)}, u32[]{:S(2)}) collective-permute-start(f32[64,128]{1,0:T(8,128)S(1)} %get-tuple-element.218), channel_id=1, source_target_pairs={{0,1},{1,2},{2,3},{3,4},{4,5},{5,6},{6,7},{7,8},{8,9},{9,10},{10,1... | collective-permute-start | bytes 98312 | tf_op jit(solution)/shard_map/while/body/eval_jaxpr/ppermute | solution.py:15
  275.4 12.0 %collective-permute-start = (f32[64,128]{1,0:T(8,128)S(1)}, f32[64,128]{1,0:T(8,128)S(1)}, u32[]{:S(2)}, u32[]{:S(2)}) collective-permute-start(f32[64,128]{1,0:T(8,128)S(1)} %get-tuple-element.218), channel_id=1, source_target_pairs={{0,1},{1,2},{2,3},{3,4},{4,5},{5,6},{6,7},{7,8},{8,9},{9,10},{10,1... | collective-permute-start | bytes 98312 | tf_op jit(solution)/shard_map/while/body/eval_jaxpr/ppermute | solution.py:15
  291.2 12.0 %collective-permute-start = (f32[64,128]{1,0:T(8,128)S(1)}, f32[64,128]{1,0:T(8,128)S(1)}, u32[]{:S(2)}, u32[]{:S(2)}) collective-permute-start(f32[64,128]{1,0:T(8,128)S(1)} %get-tuple-element.218), channel_id=1, source_target_pairs={{0,1},{1,2},{2,3},{3,4},{4,5},{5,6},{6,7},{7,8},{8,9},{9,10},{10,1... | collective-permute-start | bytes 98312 | tf_op jit(solution)/shard_map/while/body/eval_jaxpr/ppermute | solution.py:15
  307.1 12.0 %collective-permute-start = (f32[64,128]{1,0:T(8,128)S(1)}, f32[64,128]{1,0:T(8,128)S(1)}, u32[]{:S(2)}, u32[]{:S(2)}) collective-permute-start(f32[64,128]{1,0:T(8,128)S(1)} %get-tuple-element.218), channel_id=1, source_target_pairs={{0,1},{1,2},{2,3},{3,4},{4,5},{5,6},{6,7},{7,8},{8,9},{9,10},{10,1... | collective-permute-start | bytes 98312 | tf_op jit(solution)/shard_map/while/body/eval_jaxpr/ppermute | solution.py:15
  323.0 12.0 %collective-permute-start = (f32[64,128]{1,0:T(8,128)S(1)}, f32[64,128]{1,0:T(8,128)S(1)}, u32[]{:S(2)}, u32[]{:S(2)}) collective-permute-start(f32[64,128]{1,0:T(8,128)S(1)} %get-tuple-element.218), channel_id=1, source_target_pairs={{0,1},{1,2},{2,3},{3,4},{4,5},{5,6},{6,7},{7,8},{8,9},{9,10},{10,1... | collective-permute-start | bytes 98312 | tf_op jit(solution)/shard_map/while/body/eval_jaxpr/ppermute | solution.py:15
  338.9 12.0 %collective-permute-start = (f32[64,128]{1,0:T(8,128)S(1)}, f32[64,128]{1,0:T(8,128)S(1)}, u32[]{:S(2)}, u32[]{:S(2)}) collective-permute-start(f32[64,128]{1,0:T(8,128)S(1)} %get-tuple-element.218), channel_id=1, source_target_pairs={{0,1},{1,2},{2,3},{3,4},{4,5},{5,6},{6,7},{7,8},{8,9},{9,10},{10,1... | collective-permute-start | bytes 98312 | tf_op jit(solution)/shard_map/while/body/eval_jaxpr/ppermute | solution.py:15
  354.7 12.0 %collective-permute-start = (f32[64,128]{1,0:T(8,128)S(1)}, f32[64,128]{1,0:T(8,128)S(1)}, u32[]{:S(2)}, u32[]{:S(2)}) collective-permute-start(f32[64,128]{1,0:T(8,128)S(1)} %get-tuple-element.218), channel_id=1, source_target_pairs={{0,1},{1,2},{2,3},{3,4},{4,5},{5,6},{6,7},{7,8},{8,9},{9,10},{10,1... | collective-permute-start | bytes 98312 | tf_op jit(solution)/shard_map/while/body/eval_jaxpr/ppermute | solution.py:15
  370.6 12.0 %collective-permute-start = (f32[64,128]{1,0:T(8,128)S(1)}, f32[64,128]{1,0:T(8,128)S(1)}, u32[]{:S(2)}, u32[]{:S(2)}) collective-permute-start(f32[64,128]{1,0:T(8,128)S(1)} %get-tuple-element.218), channel_id=1, source_target_pairs={{0,1},{1,2},{2,3},{3,4},{4,5},{5,6},{6,7},{7,8},{8,9},{9,10},{10,1... | collective-permute-start | bytes 98312 | tf_op jit(solution)/shard_map/while/body/eval_jaxpr/ppermute | solution.py:15
  386.5 12.0 %collective-permute-start = (f32[64,128]{1,0:T(8,128)S(1)}, f32[64,128]{1,0:T(8,128)S(1)}, u32[]{:S(2)}, u32[]{:S(2)}) collective-permute-start(f32[64,128]{1,0:T(8,128)S(1)} %get-tuple-element.218), channel_id=1, source_target_pairs={{0,1},{1,2},{2,3},{3,4},{4,5},{5,6},{6,7},{7,8},{8,9},{9,10},{10,1... | collective-permute-start | bytes 98312 | tf_op jit(solution)/shard_map/while/body/eval_jaxpr/ppermute | solution.py:15
  402.4 12.0 %collective-permute-start = (f32[64,128]{1,0:T(8,128)S(1)}, f32[64,128]{1,0:T(8,128)S(1)}, u32[]{:S(2)}, u32[]{:S(2)}) collective-permute-start(f32[64,128]{1,0:T(8,128)S(1)} %get-tuple-element.218), channel_id=1, source_target_pairs={{0,1},{1,2},{2,3},{3,4},{4,5},{5,6},{6,7},{7,8},{8,9},{9,10},{10,1... | collective-permute-start | bytes 98312 | tf_op jit(solution)/shard_map/while/body/eval_jaxpr/ppermute | solution.py:15
  418.2 12.0 %collective-permute-start = (f32[64,128]{1,0:T(8,128)S(1)}, f32[64,128]{1,0:T(8,128)S(1)}, u32[]{:S(2)}, u32[]{:S(2)}) collective-permute-start(f32[64,128]{1,0:T(8,128)S(1)} %get-tuple-element.218), channel_id=1, source_target_pairs={{0,1},{1,2},{2,3},{3,4},{4,5},{5,6},{6,7},{7,8},{8,9},{9,10},{10,1... | collective-permute-start | bytes 98312 | tf_op jit(solution)/shard_map/while/body/eval_jaxpr/ppermute | solution.py:15
  434.1 12.0 %collective-permute-start = (f32[64,128]{1,0:T(8,128)S(1)}, f32[64,128]{1,0:T(8,128)S(1)}, u32[]{:S(2)}, u32[]{:S(2)}) collective-permute-start(f32[64,128]{1,0:T(8,128)S(1)} %get-tuple-element.218), channel_id=1, source_target_pairs={{0,1},{1,2},{2,3},{3,4},{4,5},{5,6},{6,7},{7,8},{8,9},{9,10},{10,1... | collective-permute-start | bytes 98312 | tf_op jit(solution)/shard_map/while/body/eval_jaxpr/ppermute | solution.py:15
  450.0 12.0 %collective-permute-start = (f32[64,128]{1,0:T(8,128)S(1)}, f32[64,128]{1,0:T(8,128)S(1)}, u32[]{:S(2)}, u32[]{:S(2)}) collective-permute-start(f32[64,128]{1,0:T(8,128)S(1)} %get-tuple-element.218), channel_id=1, source_target_pairs={{0,1},{1,2},{2,3},{3,4},{4,5},{5,6},{6,7},{7,8},{8,9},{9,10},{10,1... | collective-permute-start | bytes 98312 | tf_op jit(solution)/shard_map/while/body/eval_jaxpr/ppermute | solution.py:15
  465.9 12.0 %collective-permute-start = (f32[64,128]{1,0:T(8,128)S(1)}, f32[64,128]{1,0:T(8,128)S(1)}, u32[]{:S(2)}, u32[]{:S(2)}) collective-permute-start(f32[64,128]{1,0:T(8,128)S(1)} %get-tuple-element.218), channel_id=1, source_target_pairs={{0,1},{1,2},{2,3},{3,4},{4,5},{5,6},{6,7},{7,8},{8,9},{9,10},{10,1... | collective-permute-start | bytes 98312 | tf_op jit(solution)/shard_map/while/body/eval_jaxpr/ppermute | solution.py:15
  529.4 12.0 %collective-permute-start = (f32[64,128]{1,0:T(8,128)S(1)}, f32[64,128]{1,0:T(8,128)S(1)}, u32[]{:S(2)}, u32[]{:S(2)}) collective-permute-start(f32[64,128]{1,0:T(8,128)S(1)} %get-tuple-element.218), channel_id=1, source_target_pairs={{0,1},{1,2},{2,3},{3,4},{4,5},{5,6},{6,7},{7,8},{8,9},{9,10},{10,1... | collective-permute-start | bytes 98312 | tf_op jit(solution)/shard_map/while/body/eval_jaxpr/ppermute | solution.py:15
  545.2 12.0 %collective-permute-start = (f32[64,128]{1,0:T(8,128)S(1)}, f32[64,128]{1,0:T(8,128)S(1)}, u32[]{:S(2)}, u32[]{:S(2)}) collective-permute-start(f32[64,128]{1,0:T(8,128)S(1)} %get-tuple-element.218), channel_id=1, source_target_pairs={{0,1},{1,2},{2,3},{3,4},{4,5},{5,6},{6,7},{7,8},{8,9},{9,10},{10,1... | collective-permute-start | bytes 98312 | tf_op jit(solution)/shard_map/while/body/eval_jaxpr/ppermute | solution.py:15
  (37 other events, 359.8 us)
where the time goes:
time: 566 us; the launch traced here: 562 us
  starting transfers between devices  259 us (46%)
  other arithmetic  84 us (15%)
  loops' own time  69.5 us (12%)
  matrix products  59.1 us (10%)
  local copies, waits for them, and re-layouts  51.8 us (9%)
  blocking collectives  31.4 us (6%)
  waiting for transfers between devices  7.07 us (1%)
    ppermute x33, starting transfers between devices, with_halo(): lax.ppermute(lax.slice_in_dim(block, 0, width, axis=dim), axis, backward)  189 us
    another operation x1, loops' own time, per_device(): result = lax.fori_loop(0, SWEEPS, one_sweep, vectors_in)  69.5 us
    ppermute x33, starting transfers between devices, with_halo(): lax.ppermute(lax.slice_in_dim(block, block.shape[dim] - width, None, axis...  64.4 us
    dot_general x32, matrix products, apply_blocks(): jnp.einsum('cbi,bi->cb', blocks, vectors, precision=lax.Precision.HIGHEST)  59.1 us
    div x32, other arithmetic, apply_blocks(): factors = active_mask * 2.0 / (squares + 1.0 - active_mask)  40.2 us
    concatenate x33, other arithmetic, with_halo(): block = jnp.concatenate([low, block, high], axis=dim)  20.4 us
    sub x32, other arithmetic, apply_blocks(): blocks - (inner * factors[None, :])[:, :, None] * vectors[None, :, :]  19.7 us
    slice x32, local copies, waits for them, and re-layouts, one_sweep(): ranges_now[1]  18.7 us
  transfers between devices with their start and end apart: 67, of which 1 were waited for; matrix products, arithmetic and copies ran while one was open for 13% of the time, Pallas kernels for 0%

commit v1 on v0

v1 whole, which is shorter than its diff:
```python
import jax
import jax.numpy as jnp
from jax import lax
from jax.experimental import pallas as pl
from jax.experimental.pallas import tpu as pltpu
from jax.sharding import PartitionSpec as P

NB = 128
SWEEPS = 32
OWN = 32
EIG = 64
HALO = 32
F32 = jnp.float32
BF16 = jnp.bfloat16
VMEM_LIMIT = 48 * 1024 * 1024


def split(x):
    high = x.astype(BF16)
    low = (x - high.astype(F32)).astype(BF16)
    return high, low


def dot3(left, right, contract):
    lh, ll = split(left)
    rh, rl = split(right)
    dims = (contract, ((), ()))
    def dot(a, b):
        return lax.dot_general(a, b, dims, preferred_element_type=F32)
    return dot(lh, rh) + (dot(lh, rl) + dot(ll, rh))


def lane_group(rows):
    return lax.broadcasted_iota(jnp.int32, (rows, NB), 1) // 32


def sweep_bounds(ranges_ref):
    lower = jnp.broadcast_to(ranges_ref[:, 0:1], (SWEEPS, NB))
    upper = jnp.broadcast_to(ranges_ref[:, 1:2], (SWEEPS, NB))
    phase = lower & (NB - 1)
    first = lower >> 7
    last = (upper - phase - NB) >> 7
    return phase, first, last


def heads_tails(rows, bounds, block):
    phase, first, last = bounds
    lane = lax.broadcasted_iota(jnp.int32, (SWEEPS, NB), 1)
    head_on = (lane >= phase) & (block >= first) & (block <= last)
    tail_on = (lane < phase) & (block - 1 >= first) & (block - 1 <= last)
    return jnp.where(head_on, rows, 0.0), jnp.where(tail_on, rows, 0.0)


def fold(x, rows):
    group = lane_group(rows)
    out = x[0:rows]
    for q in range(1, 4):
        out = jnp.where(group == q, x[q * rows:(q + 1) * rows], out)
    return out


def inner_kernel(base_ref, ranges_ref, x_ref, v_ref, out_ref):
    bounds = sweep_bounds(ranges_ref)
    row = lax.broadcasted_iota(jnp.int32, (SWEEPS, NB), 0)
    lane = lax.broadcasted_iota(jnp.int32, (SWEEPS, NB), 1)
    upper = row <= (lane & 31)
    base = base_ref[0]
    out_ref[0] = jnp.zeros((24, NB), F32)
    for a in range(OWN):
        cols = pl.ds(a * NB, NB)
        head, tail = heads_tails(v_ref[:, cols], bounds, base + a)
        left = jnp.concatenate([x_ref[:, cols], head, tail], axis=0)
        right = jnp.concatenate([head] * 4 + [tail] * 4, axis=0)
        prod = dot3(left, right, ((1,), (1,)))
        from_head, from_tail = prod[:, :NB], prod[:, NB:]
        gram_head = jnp.where(upper, from_head[64:96], from_head[96:128])
        gram_tail = jnp.where(upper, from_tail[96:128], from_tail[64:96])
        out_ref[a + 1, 0:16] = fold(from_head[:64], 16)
        out_ref[a + 1, 16:24] = fold(gram_head, 8)
        out_ref[a, 0:16] += fold(from_tail[:64], 16)
        out_ref[a, 16:24] += fold(gram_tail, 8)


def apply_kernel(base_ref, phase_ref, ranges_ref, own_ref, low_ref, high_ref, x_ref, v_ref,
                 out_ref, gather, coef, tau, inner, shifted, rows_t):
    gather[pl.ds(0, HALO * 24)] = low_ref[pl.ds(24, HALO * 24)]
    gather[pl.ds(HALO * 24, OWN * 24)] = own_ref[pl.ds(24, OWN * 24)]
    gather[pl.ds((HALO - 1) * 24, 24)] += own_ref[pl.ds(0, 24)]
    gather[pl.ds((HALO + OWN - 1) * 24, 24)] += high_ref[pl.ds(0, 24)]
    gather[pl.ds((HALO + OWN) * 24, (HALO - 1) * 24)] = high_ref[pl.ds(24, (HALO - 1) * 24)]
    gather[pl.ds((2 * HALO + OWN - 1) * 24, 33 * 24)] = jnp.zeros((33 * 24, NB), F32)

    for q in range(8):
        block = gather[pl.ds(16 + q, NB, stride=24), :].T
        for g in range(4):
            coef[pl.ds((g * 8 + q) * 32, 32)] = block[g * 32:(g + 1) * 32]
    for j in range(SWEEPS):
        square = coef[pl.ds(j * 33, 1), :]
        tau[pl.ds(j, 1)] = jnp.where(square > 0, 2.0 / jnp.where(square > 0, square, 1.0), 0.0)
    row = lax.broadcasted_iota(jnp.int32, (SWEEPS, NB), 0)
    all_tau = tau[...]
    for j in range(SWEEPS):
        mine = jnp.broadcast_to(all_tau[j:j + 1], (SWEEPS, NB))
        coef[pl.ds(j * 32, 32)] *= jnp.where(row < j, all_tau, mine)

    for q in range(16):
        block = gather[pl.ds(q, NB, stride=24), :].T
        for g in range(4):
            part = block[g * 32:(g + 1) * 32] * all_tau
            inner[pl.ds(g * 16 + q, 32, stride=64), :] = part

    for j in range(SWEEPS - 1, -1, -1):
        total = inner[pl.ds(j * EIG, EIG)]
        for i in range(SWEEPS - 1, j, -1):
            same = coef[pl.ds(j * 32 + i, 1), :]
            next_to = coef[pl.ds(i * 32 + j, 1), :]
            down = jnp.where(phase_ref[j] < phase_ref[i], 0, 1)
            start = pl.multiple_of((2 * i + down) * EIG, EIG)
            total = total - same * inner[pl.ds(i * EIG, EIG)] - next_to * shifted[pl.ds(start, EIG)]
        inner[pl.ds(j * EIG, EIG)] = total
        shifted[pl.ds((2 * j) * EIG, EIG)] = pltpu.roll(total, 1, 1)
        shifted[pl.ds((2 * j + 1) * EIG, EIG)] = pltpu.roll(total, NB - 1, 1)

    for q in range(16):
        parts = [inner[pl.ds(g * 16 + q, 32, stride=64), :] for g in range(4)]
        block = jnp.concatenate(parts, axis=0).T
        rows_t[pl.ds(q, 40, stride=16), :] = block[24:64]

    bounds = sweep_bounds(ranges_ref)
    group = lane_group(16)
    base = base_ref[0]
    for a in range(OWN):
        cols = pl.ds(a * NB, NB)
        head, tail = heads_tails(v_ref[:, cols], bounds, base + a)
        of_head = rows_t[pl.ds((a + 8) * 16, 16)]
        of_tail = rows_t[pl.ds((a + 7) * 16, 16)]
        spread = [jnp.concatenate([jnp.where(group == g, y, 0.0) for g in range(4)], axis=0)
                  for y in (of_head, of_tail)]
        left = jnp.concatenate(spread, axis=1)
        right = jnp.concatenate([head] * 4 + [tail] * 4, axis=0)
        out_ref[:, cols] = x_ref[:, cols] - dot3(left, right, ((1,), (0,)))


def back_transform(x, v, sweep_ranges):
    count = lax.axis_size("row")
    base = (lax.axis_index("row") * OWN).reshape(1).astype(jnp.int32)
    vmem = pl.BlockSpec(memory_space=pltpu.VMEM)
    smem = pl.BlockSpec(memory_space=pltpu.SMEM)
    params = pltpu.CompilerParams(vmem_limit_bytes=VMEM_LIMIT)
    own = pl.pallas_call(
        inner_kernel,
        out_shape=jax.ShapeDtypeStruct((OWN + 1, 24, NB), F32),
        in_specs=[smem, vmem, vmem, vmem],
        out_specs=vmem,
        compiler_params=params,
        name="inner_products",
    )(base, sweep_ranges, x, v)
    own = own.reshape((OWN + 1) * 24, NB)
    forward = [(i, i + 1) for i in range(count - 1)]
    backward = [(i + 1, i) for i in range(count - 1)]
    low = lax.ppermute(own, "row", forward)
    high = lax.ppermute(own, "row", backward)
    phase = sweep_ranges[:, 0] % NB
    return pl.pallas_call(
        apply_kernel,
        out_shape=jax.ShapeDtypeStruct((EIG, OWN * NB), F32),
        in_specs=[smem, smem, vmem, vmem, vmem, vmem, vmem, vmem],
        out_specs=vmem,
        scratch_shapes=[
            pltpu.VMEM((NB * 24, NB), F32),
            pltpu.VMEM((SWEEPS * 32, NB), F32),
            pltpu.VMEM((SWEEPS, NB), F32),
            pltpu.VMEM((SWEEPS * EIG, NB), F32),
            pltpu.VMEM((2 * SWEEPS * EIG, NB), F32),
            pltpu.VMEM((40 * 16, NB), F32),
        ],
        compiler_params=params,
        name="apply_sweeps",
    )(base, phase, sweep_ranges, own, low, high, x, v)


def per_device(eigenvectors, reflectors, sweep_ranges):
    sweep_rows = lax.all_gather(reflectors, "col", axis=1, tiled=True)
    x = lax.all_to_all(eigenvectors, "row", split_axis=1, concat_axis=0, tiled=True)
    v = lax.all_to_all(sweep_rows, "row", split_axis=1, concat_axis=0, tiled=True)
    return back_transform(x, v, sweep_ranges)


def solution(mesh):
    placed = (P(("col", "row"), None), P("row", "col"), P())
    return jax.shard_map(
        per_device, mesh=mesh, in_specs=placed, out_specs=P("col", "row"), check_vma=False
    )
```

time: 566 us -> 80.5 us (0.14)
  starting transfers between devices: 259 us -> 13.2 us
  other arithmetic: 84 us -> 0.01 us
  loops' own time: 69.5 us -> 0 us
  matrix products: 59.1 us -> 0 us
  local copies, waits for them, and re-layouts: 51.8 us -> 1.79 us
  waiting for transfers between devices: 7.07 us -> 23.2 us
  Pallas kernels: 0 us -> 10.5 us
    ppermute x66 -> x2, starting transfers between devices: 253 us -> 7.31 us  [the longest x1 5.38 us: back_transform(): high = lax.ppermute(own, 'row', backward)]
    another operation x1 -> x0, loops' own time: 69.5 us -> none  [per_device(): result = lax.fori_loop(0, SWEEPS, one_sweep, vectors_in)]
    dot_general x32 -> x0, matrix products: 59.1 us -> none  [apply_blocks(): jnp.einsum('cbi,bi->cb', blocks, vectors, precision=lax.Precision.HIGHEST)]
    div x32 -> x0, other arithmetic: 40.2 us -> none  [apply_blocks(): factors = active_mask * 2.0 / (squares + 1.0 - active_mask)]
    concatenate x33 -> x0, other arithmetic: 20.4 us -> none  [with_halo(): block = jnp.concatenate([low, block, high], axis=dim)]
    sub x32 -> x0, other arithmetic: 19.7 us -> none  [apply_blocks(): blocks - (inner * factors[None, :])[:, :, None] * vectors[None, :, :]]
    slice x65 -> x0, local copies, waits for them, and re-layouts: 18.9 us -> none  [the longest x32 18.7 us: one_sweep(): ranges_now[1]]
    all_to_all x1, waiting for transfers between devices: 0.01 us -> 13.8 us  [per_device(): lax.all_to_all(eigenvectors, 'row', split_axis=1, concat_axis=0, tiled=True)]
  transfers between devices with their start and end apart: 67 -> 3, of which waited for: 1 -> 3; matrix products, arithmetic and copies ran while one was open for 13% -> 1% of each run, Pallas kernels for 0% -> 0%
where the time goes in v1:
time: 80.5 us; the launch traced here: 80.2 us
  blocking collectives  31.4 us (39%)
  waiting for transfers between devices  23.2 us (29%)
  starting transfers between devices  13.2 us (16%)
  Pallas kernels  10.5 us (13%)
  local copies, waits for them, and re-layouts  1.79 us (2%)
    all_to_all x1, blocking collectives, per_device(): lax.all_to_all(sweep_rows, 'row', split_axis=1, concat_axis=0, tiled=True)  17.5 us
    all_gather x1, blocking collectives, per_device(): sweep_rows = lax.all_gather(reflectors, 'col', axis=1, tiled=True)  13.9 us
    all_to_all x1, waiting for transfers between devices, per_device(): lax.all_to_all(eigenvectors, 'row', split_axis=1, concat_axis=0, tiled=True)  13.8 us
    pallas_call x1, Pallas kernels, back_transform(): pl.pallas_call(apply_kernel, out_shape=jax.ShapeDtypeStruct((EIG, OWN * N...  8.61 us
    all_to_all x1, starting transfers between devices, per_device(): lax.all_to_all(eigenvectors, 'row', split_axis=1, concat_axis=0, tiled=True)  5.93 us
    ppermute x1, waiting for transfers between devices, back_transform(): low = lax.ppermute(own, 'row', forward)  5.93 us
    ppermute x1, starting transfers between devices, back_transform(): high = lax.ppermute(own, 'row', backward)  5.38 us
    ppermute x1, waiting for transfers between devices, back_transform(): high = lax.ppermute(own, 'row', backward)  3.46 us
  transfers between devices with their start and end apart: 3, of which 3 were waited for; matrix products, arithmetic and copies ran while one was open for 1% of the time, Pallas kernels for 0%

profile of v1, /device:TPU:40, one launch (start us, length us, event | category | flops | bytes accessed | tf_op | source)
XLA Modules:
  0.0 80.2 jit_solution(2984728118586824689)
XLA Ops:
  0.0 13.9 %all_gather.3 = f32[1,131072]{1,0:T(1,128)S(1)} all-gather(f32[1,32768]{1,0:T(1,128)} %param.4), channel_id=1, replica_groups=mesh['col'=4,'row'=32] {'col'}, dimensions={1}, use_global_device_ids=true | all-gather | bytes 655360 | tf_op jit(solution)/shard_map/all_gather | solution.py:183
  13.9 17.5 %all_to_all.35 = f32[1,32,4096]{2,0,1:T(1,128)S(1)} all-to-all(f32[1,32,4096]{2,0,1:T(1,128)S(1)} %bitcast.16), channel_id=1, replica_groups=mesh['col'=4,'row'=32] {'row'}, dimensions={1} | all-to-all | bytes 1048576 | tf_op jit(solution)/shard_map/all_to_all | solution.py:185
  31.4 5.9 %all-to-all-start = ((f32[2,32,4096]{2,0,1:T(2,128)}), f32[2,32,4096]{2,0,1:T(2,128)S(1)}, u32[]{:S(2)}, u32[]{:S(2)}) async-start(f32[2,32,4096]{2,0,1:T(2,128)} %bitcast.2), calls=%async_computation | async-start | bytes 2097152 | tf_op jit(solution)/shard_map/all_to_all | solution.py:184
  37.4 0.0 copy-start
  37.4 0.7 copy-done
  38.0 0.1 copy.9.ranges_ref
  38.1 0.3 copy.12
  38.4 13.8 %all-to-all-done = f32[2,32,4096]{2,0,1:T(2,128)S(1)} async-done(((f32[2,32,4096]{2,0,1:T(2,128)}), f32[2,32,4096]{2,0,1:T(2,128)S(1)}, u32[]{:S(2)}, u32[]{:S(2)}) %all-to-all-start) | async-done | bytes 1048608 | tf_op jit(solution)/shard_map/all_to_all | solution.py:184
  52.2 0.7 all_to_all.29.x_ref
  53.0 1.9 %inner_products.1 = f32[33,24,128]{2,1,0:T(8,128)S(1)} custom-call(s32[1]{0:T(128)} %bitcast.base_ref, s32[32,2]{1,0:T(8,128)S(1)} %copy.9.ranges_ref, f32[64,4096]{1,0:T(8,128)S(1)} %all_to_all.29.x_ref, f32[32,4096]{1,0:T(8,128)S(1)} %bitcast.10), custom_call_target="tpu_custom_call" | custom-call | tf_op jit(solution)/shard_map/inner_products/pallas_call | solution.py:150
  54.9 5.4 %collective-permute-start.1 = (f32[792,128]{1,0:T(8,128)S(1)}, f32[792,128]{1,0:T(8,128)S(1)}, u32[]{:S(2)}, u32[]{:S(2)}) collective-permute-start(f32[792,128]{1,0:T(8,128)S(1)} %bitcast.12), channel_id=1, source_target_pairs={{1,0},{2,1},{3,2},{4,3},{5,4},{6,5},{7,6},{8,7},{9,8},{10,9},{11,1... | collective-permute-start | bytes 1216520 | tf_op jit(solution)/shard_map/ppermute | solution.py:162
  60.2 1.9 %collective-permute-start = (f32[792,128]{1,0:T(8,128)S(1)}, f32[792,128]{1,0:T(8,128)S(1)}, u32[]{:S(2)}, u32[]{:S(2)}) collective-permute-start(f32[792,128]{1,0:T(8,128)S(1)} %bitcast.13), channel_id=1, source_target_pairs={{0,1},{1,2},{2,3},{3,4},{4,5},{5,6},{6,7},{7,8},{8,9},{9,10},{10,1... | collective-permute-start | bytes 1216520 | tf_op jit(solution)/shard_map/ppermute | solution.py:161
  62.2 3.5 %collective-permute-done.1.high_ref = f32[792,128]{1,0:T(8,128)S(1)} collective-permute-done((f32[792,128]{1,0:T(8,128)S(1)}, f32[792,128]{1,0:T(8,128)S(1)}, u32[]{:S(2)}, u32[]{:S(2)}) %collective-permute-start.1) | collective-permute-done | bytes 405536 | tf_op jit(solution)/shard_map/ppermute | solution.py:162
  65.7 5.9 %collective-permute-done.low_ref = f32[792,128]{1,0:T(8,128)S(1)} collective-permute-done((f32[792,128]{1,0:T(8,128)S(1)}, f32[792,128]{1,0:T(8,128)S(1)}, u32[]{:S(2)}, u32[]{:S(2)}) %collective-permute-start) | collective-permute-done | bytes 405536 | tf_op jit(solution)/shard_map/ppermute | solution.py:161
  71.6 8.6 %apply_sweeps.1 = f32[64,4096]{1,0:T(8,128)} custom-call(s32[1]{0:T(128)} %bitcast.base_ref, s32[32]{0:T(128)S(1)} %and_select_fusion.phase_ref, s32[32,2]{1,0:T(8,128)S(1)} %copy.9.ranges_ref, f32[792,128]{1,0:T(8,128)S(1)} %bitcast.14, f32[792,128]{1,0:T(8,128)S(1)} %collective-permute-done.low_ref, f32[792,128]{1,0:T(8,128)S(1)} %collective-permute-done.1.high_ref, ...), custom_call_target="tpu_custom_call" | custom-call | tf_op jit(solution)/shard_map/apply_sweeps/pallas_call | solution.py:164
  (1 shorter events, 0.0 us)
Async XLA Ops:
  31.4 20.8 %all-to-all-start = ((f32[2,32,4096]{2,0,1:T(2,128)}), f32[2,32,4096]{2,0,1:T(2,128)S(1)}, u32[]{:S(2)}, u32[]{:S(2)}) async-start(f32[2,32,4096]{2,0,1:T(2,128)} %bitcast.2), calls=%async_computation | async-start | bytes 2097152 | tf_op jit(solution)/shard_map/all_to_all | solution.py:184
  37.4 0.7 copy-start
  54.9 10.8 %collective-permute-start.1 = (f32[792,128]{1,0:T(8,128)S(1)}, f32[792,128]{1,0:T(8,128)S(1)}, u32[]{:S(2)}, u32[]{:S(2)}) collective-permute-start(f32[792,128]{1,0:T(8,128)S(1)} %bitcast.12), channel_id=1, source_target_pairs={{1,0},{2,1},{3,2},{4,3},{5,4},{6,5},{7,6},{8,7},{9,8},{10,9},{11,1... | collective-permute-start | bytes 1216520 | tf_op jit(solution)/shard_map/ppermute | solution.py:162
  60.2 11.3 %collective-permute-start = (f32[792,128]{1,0:T(8,128)S(1)}, f32[792,128]{1,0:T(8,128)S(1)}, u32[]{:S(2)}, u32[]{:S(2)}) collective-permute-start(f32[792,128]{1,0:T(8,128)S(1)} %bitcast.13), channel_id=1, source_target_pairs={{0,1},{1,2},{2,3},{3,4},{4,5},{5,6},{6,7},{7,8},{8,9},{9,10},{10,1... | collective-permute-start | bytes 1216520 | tf_op jit(solution)/shard_map/ppermute | solution.py:161

commit v2 on v1

--- a/solution.py
+++ b/solution.py
@@ -59,12 +59,15 @@
     return out
 
 
-def inner_kernel(base_ref, ranges_ref, x_ref, v_ref, out_ref):
+def inner_kernel(place_ref, ranges_ref, x_ref, v0, v1, v2, v3, out_ref, v_ref):
+    for k, piece in enumerate((v0, v1, v2, v3)):
+        first = pl.multiple_of(((place_ref[1] + k) & 3) * 8, 8)
+        v_ref[pl.ds(first, 8), :] = piece[...]
     bounds = sweep_bounds(ranges_ref)
     row = lax.broadcasted_iota(jnp.int32, (SWEEPS, NB), 0)
     lane = lax.broadcasted_iota(jnp.int32, (SWEEPS, NB), 1)
     upper = row <= (lane & 31)
-    base = base_ref[0]
+    base = place_ref[0] * OWN
     out_ref[0] = jnp.zeros((24, NB), F32)
     for a in range(OWN):
         cols = pl.ds(a * NB, NB)
@@ -81,13 +84,27 @@
         out_ref[a, 16:24] += fold(gram_tail, 8)
 
 
-def apply_kernel(base_ref, phase_ref, ranges_ref, own_ref, low_ref, high_ref, x_ref, v_ref,
+def apply_kernel(place_ref, phase_ref, ranges_ref, own_ref, pair_ref, other_ref, x_ref, v_ref,
                  out_ref, gather, coef, tau, inner, shifted, rows_t):
-    gather[pl.ds(0, HALO * 24)] = low_ref[pl.ds(24, HALO * 24)]
     gather[pl.ds(HALO * 24, OWN * 24)] = own_ref[pl.ds(24, OWN * 24)]
-    gather[pl.ds((HALO - 1) * 24, 24)] += own_ref[pl.ds(0, 24)]
-    gather[pl.ds((HALO + OWN - 1) * 24, 24)] += high_ref[pl.ds(0, 24)]
-    gather[pl.ds((HALO + OWN) * 24, (HALO - 1) * 24)] = high_ref[pl.ds(24, (HALO - 1) * 24)]
+    gather[pl.ds((HALO - 1) * 24, 24)] = own_ref[pl.ds(0, 24)]
+
+    def take(low_ref, high_ref):
+        gather[pl.ds(0, (HALO - 1) * 24)] = low_ref[pl.ds(24, (HALO - 1) * 24)]
+        gather[pl.ds((HALO - 1) * 24, 24)] += low_ref[pl.ds(HALO * 24, 24)]
+        gather[pl.ds((HALO + OWN - 1) * 24, 24)] += high_ref[pl.ds(0, 24)]
+        gather[pl.ds((HALO + OWN) * 24, (HALO - 1) * 24)] = high_ref[pl.ds(24, (HALO - 1) * 24)]
+
+    odd = place_ref[0] & 1
+
+    @pl.when(odd == 0)
+    def _():
+        take(other_ref, pair_ref)
+
+    @pl.when(odd == 1)
+    def _():
+        take(pair_ref, other_ref)
+
     gather[pl.ds((2 * HALO + OWN - 1) * 24, 33 * 24)] = jnp.zeros((33 * 24, NB), F32)
 
     for q in range(8):
@@ -128,7 +145,7 @@
 
     bounds = sweep_bounds(ranges_ref)
     group = lane_group(16)
-    base = base_ref[0]
+    base = place_ref[0] * OWN
     for a in range(OWN):
         cols = pl.ds(a * NB, NB)
         head, tail = heads_tails(v_ref[:, cols], bounds, base + a)
@@ -141,25 +158,29 @@
         out_ref[:, cols] = x_ref[:, cols] - dot3(left, right, ((1,), (0,)))
 
 
-def back_transform(x, v, sweep_ranges):
+def back_transform(x, pieces, sweep_ranges):
     count = lax.axis_size("row")
-    base = (lax.axis_index("row") * OWN).reshape(1).astype(jnp.int32)
+    place = jnp.stack([lax.axis_index("row"), lax.axis_index("col")]).astype(jnp.int32)
     vmem = pl.BlockSpec(memory_space=pltpu.VMEM)
     smem = pl.BlockSpec(memory_space=pltpu.SMEM)
     params = pltpu.CompilerParams(vmem_limit_bytes=VMEM_LIMIT)
-    own = pl.pallas_call(
+    own, v = pl.pallas_call(
         inner_kernel,
-        out_shape=jax.ShapeDtypeStruct((OWN + 1, 24, NB), F32),
-        in_specs=[smem, vmem, vmem, vmem],
-        out_specs=vmem,
+        out_shape=(
+            jax.ShapeDtypeStruct((OWN + 1, 24, NB), F32),
+            jax.ShapeDtypeStruct((SWEEPS, OWN * NB), F32),
+        ),
+        in_specs=[smem, vmem] + [vmem] * 5,
+        out_specs=(vmem, vmem),
         compiler_params=params,
         name="inner_products",
-    )(base, sweep_ranges, x, v)
+    )(place, sweep_ranges, x, *pieces)
     own = own.reshape((OWN + 1) * 24, NB)
-    forward = [(i, i + 1) for i in range(count - 1)]
-    backward = [(i + 1, i) for i in range(count - 1)]
-    low = lax.ppermute(own, "row", forward)
-    high = lax.ppermute(own, "row", backward)
+    within = [(i, i ^ 1) for i in range(count)]
+    across = [(i, i + 1) for i in range(1, count - 1, 2)]
+    across = across + [(t, s) for s, t in across]
+    pair = lax.ppermute(own, "row", within)
+    other = lax.ppermute(own, "row", across)
     phase = sweep_ranges[:, 0] % NB
     return pl.pallas_call(
         apply_kernel,
@@ -176,14 +197,31 @@
         ],
         compiler_params=params,
         name="apply_sweeps",
-    )(base, phase, sweep_ranges, own, low, high, x, v)
+    )(place, phase, sweep_ranges, own, pair, other, x, v)
+
+
+def sweep_pieces(reflectors):
+    cols, count = lax.axis_size("col"), lax.axis_size("row")
+    width = count // cols
+    groups = [[g * width + q for q in range(width)] for g in range(cols)]
+    mine = lax.all_to_all(
+        reflectors.reshape(width, -1), "row", split_axis=0, concat_axis=0, tiled=True,
+        axis_index_groups=groups,
+    )
+    pieces = []
+    for k in range(cols):
+        pairs = [
+            (c * count + g * width + q, ((g - k) % cols) * count + c * width + q)
+            for c in range(cols) for g in range(cols) for q in range(width)
+        ]
+        pieces.append(lax.ppermute(mine, ("col", "row"), pairs))
+    return pieces
 
 
 def per_device(eigenvectors, reflectors, sweep_ranges):
-    sweep_rows = lax.all_gather(reflectors, "col", axis=1, tiled=True)
+    pieces = sweep_pieces(reflectors)
     x = lax.all_to_all(eigenvectors, "row", split_axis=1, concat_axis=0, tiled=True)
-    v = lax.all_to_all(sweep_rows, "row", split_axis=1, concat_axis=0, tiled=True)
-    return back_transform(x, v, sweep_ranges)
+    return back_transform(x, pieces, sweep_ranges)
 
 
 def solution(mesh):

time: 80.5 us -> 61.7 us (0.77)
  the two profiles are of different devices: /device:TPU:40 before, /device:TPU:15 now
where the time goes in v2:
time: 61.7 us; the launch traced here: 61.4 us
  starting transfers between devices  20.8 us (34%)
  waiting for transfers between devices  19.1 us (31%)
  Pallas kernels  11.1 us (18%)
  blocking collectives  8.65 us (14%)
  local copies, waits for them, and re-layouts  1.56 us (3%)
    all_to_all x1, waiting for transfers between devices, per_device(): lax.all_to_all(eigenvectors, 'row', split_axis=1, concat_axis=0, tiled=True)  11 us
    ppermute x4, starting transfers between devices, sweep_pieces(): pieces.append(lax.ppermute(mine, ('col', 'row'), pairs))  8.92 us
    all_to_all x1, blocking collectives, sweep_pieces(): lax.all_to_all(reflectors.reshape(width, -1), 'row', split_axis=0, concat...  8.65 us
    pallas_call x1, Pallas kernels, back_transform(): pl.pallas_call(apply_kernel, out_shape=jax.ShapeDtypeStruct((EIG, OWN * N...  8.65 us
    all_to_all x1, starting transfers between devices, per_device(): lax.all_to_all(eigenvectors, 'row', split_axis=1, concat_axis=0, tiled=True)  8.64 us
    ppermute x1, waiting for transfers between devices, back_transform(): other = lax.ppermute(own, 'row', across)  8.1 us
    pallas_call x1, Pallas kernels, back_transform(): pl.pallas_call(inner_kernel, out_shape=(jax.ShapeDtypeStruct((OWN + 1, 24...  2.43 us
    ppermute x1, starting transfers between devices, back_transform(): other = lax.ppermute(own, 'row', across)  2.09 us
  transfers between devices with their start and end apart: 7, of which 2 were waited for; matrix products, arithmetic and copies ran while one was open for 0% of the time, Pallas kernels for 0%

profile of v2, /device:TPU:15, one launch (start us, length us, event | category | flops | bytes accessed | tf_op | source)
XLA Modules:
  0.0 61.4 jit_solution(5492126696311528941)
XLA Ops:
  0.0 8.6 %all_to_all.31 = f32[8,1,4096]{2,1,0:T(1,128)S(1)} all-to-all(f32[8,1,4096]{2,1,0:T(1,128)} %bitcast.16), channel_id=1, replica_groups={{0,1,2,3,4,5,6,7},{8,9,10,11,12,13,14,15},{16,17,18,19,20,21,22,23},{24..., dimensions={0} | all-to-all | bytes 262144 | tf_op jit(solution)/shard_map/all_to_all | solution.py:207
  8.7 8.6 %all-to-all-start = ((f32[2,32,4096]{2,0,1:T(2,128)}), f32[2,32,4096]{2,0,1:T(2,128)S(1)}, u32[]{:S(2)}, u32[]{:S(2)}) async-start(f32[2,32,4096]{2,0,1:T(2,128)} %bitcast.15), calls=%async_computation | async-start | bytes 2097152 | tf_op jit(solution)/shard_map/all_to_all | solution.py:223
  17.3 0.1 copy.12
  17.4 1.3 %collective-permute-start.3 = (f32[8,4096]{1,0:T(8,128)S(1)}, f32[8,4096]{1,0:T(8,128)S(1)}, u32[]{:S(2)}, u32[]{:S(2)}) collective-permute-start(f32[8,4096]{1,0:T(8,128)S(1)} %bitcast.17), channel_id=1, source_target_pairs={{0,32},{1,33},{2,34},{3,35},{4,36},{5,37},{6,38},{7,39},{8,64},{9,... | collective-permute-start | bytes 393224 | tf_op jit(solution)/shard_map/ppermute | solution.py:217
  18.6 2.2 %collective-permute-start.2 = (f32[8,4096]{1,0:T(8,128)S(1)}, f32[8,4096]{1,0:T(8,128)S(1)}, u32[]{:S(2)}, u32[]{:S(2)}) collective-permute-start(f32[8,4096]{1,0:T(8,128)S(1)} %bitcast.18), channel_id=1, source_target_pairs={{0,64},{1,65},{2,66},{3,67},{4,68},{5,69},{6,70},{7,71},{8,96},{9,... | collective-permute-start | bytes 393224 | tf_op jit(solution)/shard_map/ppermute | solution.py:217
  20.9 1.6 %collective-permute-start.1 = (f32[8,4096]{1,0:T(8,128)S(1)}, f32[8,4096]{1,0:T(8,128)S(1)}, u32[]{:S(2)}, u32[]{:S(2)}) collective-permute-start(f32[8,4096]{1,0:T(8,128)S(1)} %bitcast.19), channel_id=1, source_target_pairs={{0,96},{1,97},{2,98},{3,99},{4,100},{5,101},{6,102},{7,103},{8,0},... | collective-permute-start | bytes 393224 | tf_op jit(solution)/shard_map/ppermute | solution.py:217
  22.4 3.9 %collective-permute-start = (f32[8,4096]{1,0:T(8,128)S(1)}, f32[8,4096]{1,0:T(8,128)S(1)}, u32[]{:S(2)}, u32[]{:S(2)}) collective-permute-start(f32[8,4096]{1,0:T(8,128)S(1)} %bitcast.20), channel_id=1, source_target_pairs={{0,0},{1,1},{2,2},{3,3},{4,4},{5,5},{6,6},{7,7},{8,32},{9,33},{10,... | collective-permute-start | bytes 393224 | tf_op jit(solution)/shard_map/ppermute | solution.py:217
  26.3 0.0 copy-start
  26.3 0.7 %copy-done = s32[32,2]{0,1:T(2,128)S(1)} copy-done((s32[32,2]{0,1:T(2,128)S(1)}, s32[32,2]{0,1:T(2,128)}, u32[]{:S(2)}) %copy-start) | copy-done | bytes 280
  27.0 0.1 copy.9.ranges_ref
  27.1 0.1 pad_add_fusion.place_ref
  27.2 11.0 %all-to-all-done = f32[2,32,4096]{2,0,1:T(2,128)S(1)} async-done(((f32[2,32,4096]{2,0,1:T(2,128)}), f32[2,32,4096]{2,0,1:T(2,128)S(1)}, u32[]{:S(2)}, u32[]{:S(2)}) %all-to-all-start) | async-done | bytes 1048608 | tf_op jit(solution)/shard_map/all_to_all | solution.py:223
  38.2 0.7 %all_to_all.25.x_ref = f32[64,4096]{1,0:T(8,128)S(1)} reshape(f32[32,2,4096]{2,1,0:T(2,128)S(1)} %bitcast.14) | data formatting | bytes 2097152 | tf_op jit(solution)/shard_map/all_to_all | solution.py:223
  38.9 0.0 collective-permute-done.3.v3
  38.9 0.0 collective-permute-done.2.v2
  38.9 0.0 collective-permute-done.1.v1
  39.0 0.0 collective-permute-done.v0
  39.0 2.4 %inner_products.1 = (f32[33,24,128]{2,1,0:T(8,128)S(1)}, f32[32,4096]{1,0:T(8,128)S(1)}) custom-call(s32[2]{0:T(128)S(1)} %pad_add_fusion.place_ref, s32[32,2]{1,0:T(8,128)S(1)} %copy.9.ranges_ref, f32[64,4096]{1,0:T(8,128)S(1)} %all_to_all.25.x_ref, f32[8,4096]{1,0:T(8,128)S(1)} %collective-permute-done.v0, f32[8,4096]{1,0:T(8,128)S(1)} %collective-permute-done.1.v1, ...), custom_call_target="tpu_custom_call" | custom-call | tf_op jit(solution)/shard_map/inner_products/pallas_call | solution.py:167
  41.4 2.1 %collective-permute-start.5 = (f32[792,128]{1,0:T(8,128)S(1)}, f32[792,128]{1,0:T(8,128)S(1)}, u32[]{:S(2)}, u32[]{:S(2)}) collective-permute-start(f32[792,128]{1,0:T(8,128)S(1)} %bitcast.11), channel_id=1, source_target_pairs={{1,2},{3,4},{5,6},{7,8},{9,10},{11,12},{13,14},{15,16},{17,18},{19... | collective-permute-start | bytes 1216520 | tf_op jit(solution)/shard_map/ppermute | solution.py:183
  43.5 1.1 %collective-permute-start.4 = (f32[792,128]{1,0:T(8,128)S(1)}, f32[792,128]{1,0:T(8,128)S(1)}, u32[]{:S(2)}, u32[]{:S(2)}) collective-permute-start(f32[792,128]{1,0:T(8,128)S(1)} %bitcast.12), channel_id=1, source_target_pairs={{0,1},{1,0},{2,3},{3,2},{4,5},{5,4},{6,7},{7,6},{8,9},{9,8},{10,11... | collective-permute-start | bytes 1216520 | tf_op jit(solution)/shard_map/ppermute | solution.py:182
  44.6 8.1 %collective-permute-done.5.other_ref = f32[792,128]{1,0:T(8,128)S(1)} collective-permute-done((f32[792,128]{1,0:T(8,128)S(1)}, f32[792,128]{1,0:T(8,128)S(1)}, u32[]{:S(2)}, u32[]{:S(2)}) %collective-permute-start.5) | collective-permute-done | bytes 405536 | tf_op jit(solution)/shard_map/ppermute | solution.py:183
  52.7 0.0 collective-permute-done.4.pair_ref
  52.7 8.6 %apply_sweeps.1 = f32[64,4096]{1,0:T(8,128)} custom-call(s32[2]{0:T(128)S(1)} %pad_add_fusion.place_ref, s32[32]{0:T(128)S(1)} %and_select_fusion.phase_ref, s32[32,2]{1,0:T(8,128)S(1)} %copy.9.ranges_ref, f32[792,128]{1,0:T(8,128)S(1)} %bitcast.13, f32[792,128]{1,0:T(8,128)S(1)} %collective-permute-done.4.pair_ref, ...), custom_call_target="tpu_custom_call" | custom-call | tf_op jit(solution)/shard_map/apply_sweeps/pallas_call | solution.py:185
  (1 shorter events, 0.0 us)
Async XLA Ops:
  8.7 29.5 %all-to-all-start = ((f32[2,32,4096]{2,0,1:T(2,128)}), f32[2,32,4096]{2,0,1:T(2,128)S(1)}, u32[]{:S(2)}, u32[]{:S(2)}) async-start(f32[2,32,4096]{2,0,1:T(2,128)} %bitcast.15), calls=%async_computation | async-start | bytes 2097152 | tf_op jit(solution)/shard_map/all_to_all | solution.py:223
  17.4 21.5 %collective-permute-start.3 = (f32[8,4096]{1,0:T(8,128)S(1)}, f32[8,4096]{1,0:T(8,128)S(1)}, u32[]{:S(2)}, u32[]{:S(2)}) collective-permute-start(f32[8,4096]{1,0:T(8,128)S(1)} %bitcast.17), channel_id=1, source_target_pairs={{0,32},{1,33},{2,34},{3,35},{4,36},{5,37},{6,38},{7,39},{8,64},{9,... | collective-permute-start | bytes 393224 | tf_op jit(solution)/shard_map/ppermute | solution.py:217
  18.6 20.3 %collective-permute-start.2 = (f32[8,4096]{1,0:T(8,128)S(1)}, f32[8,4096]{1,0:T(8,128)S(1)}, u32[]{:S(2)}, u32[]{:S(2)}) collective-permute-start(f32[8,4096]{1,0:T(8,128)S(1)} %bitcast.18), channel_id=1, source_target_pairs={{0,64},{1,65},{2,66},{3,67},{4,68},{5,69},{6,70},{7,71},{8,96},{9,... | collective-permute-start | bytes 393224 | tf_op jit(solution)/shard_map/ppermute | solution.py:217
  20.9 18.1 %collective-permute-start.1 = (f32[8,4096]{1,0:T(8,128)S(1)}, f32[8,4096]{1,0:T(8,128)S(1)}, u32[]{:S(2)}, u32[]{:S(2)}) collective-permute-start(f32[8,4096]{1,0:T(8,128)S(1)} %bitcast.19), channel_id=1, source_target_pairs={{0,96},{1,97},{2,98},{3,99},{4,100},{5,101},{6,102},{7,103},{8,0},... | collective-permute-start | bytes 393224 | tf_op jit(solution)/shard_map/ppermute | solution.py:217
  22.4 16.5 %collective-permute-start = (f32[8,4096]{1,0:T(8,128)S(1)}, f32[8,4096]{1,0:T(8,128)S(1)}, u32[]{:S(2)}, u32[]{:S(2)}) collective-permute-start(f32[8,4096]{1,0:T(8,128)S(1)} %bitcast.20), channel_id=1, source_target_pairs={{0,0},{1,1},{2,2},{3,3},{4,4},{5,5},{6,6},{7,7},{8,32},{9,33},{10,... | collective-permute-start | bytes 393224 | tf_op jit(solution)/shard_map/ppermute | solution.py:217
  26.3 0.7 %copy-start = (s32[32,2]{0,1:T(2,128)S(1)}, s32[32,2]{0,1:T(2,128)}, u32[]{:S(2)}) copy-start(s32[32,2]{0,1:T(2,128)} %param.5) | copy-start | bytes 772
  41.4 11.3 %collective-permute-start.5 = (f32[792,128]{1,0:T(8,128)S(1)}, f32[792,128]{1,0:T(8,128)S(1)}, u32[]{:S(2)}, u32[]{:S(2)}) collective-permute-start(f32[792,128]{1,0:T(8,128)S(1)} %bitcast.11), channel_id=1, source_target_pairs={{1,2},{3,4},{5,6},{7,8},{9,10},{11,12},{13,14},{15,16},{17,18},{19... | collective-permute-start | bytes 1216520 | tf_op jit(solution)/shard_map/ppermute | solution.py:183
  43.5 9.2 %collective-permute-start.4 = (f32[792,128]{1,0:T(8,128)S(1)}, f32[792,128]{1,0:T(8,128)S(1)}, u32[]{:S(2)}, u32[]{:S(2)}) collective-permute-start(f32[792,128]{1,0:T(8,128)S(1)} %bitcast.12), channel_id=1, source_target_pairs={{0,1},{1,0},{2,3},{3,2},{4,5},{5,4},{6,7},{7,6},{8,9},{9,8},{10,11... | collective-permute-start | bytes 1216520 | tf_op jit(solution)/shard_map/ppermute | solution.py:182

commit v3 on v2

v3 whole, which is shorter than its diff:
```python
import jax
import jax.numpy as jnp
from jax import lax
from jax.experimental import pallas as pl
from jax.experimental.pallas import tpu as pltpu
from jax.sharding import PartitionSpec as P

NB = 128
SWEEPS = 32
OWN = 32
EIG = 64
HALO = 32
ROWS = 24
F32 = jnp.float32
BF16 = jnp.bfloat16
VMEM_LIMIT = 48 * 1024 * 1024


def split(x):
    high = x.astype(BF16)
    low = (x - high.astype(F32)).astype(BF16)
    return high, low


def lane_group(rows):
    return lax.broadcasted_iota(jnp.int32, (rows, NB), 1) // 32


def sweep_bounds(ranges_ref):
    lower = jnp.broadcast_to(ranges_ref[:, 0:1], (SWEEPS, NB))
    upper = jnp.broadcast_to(ranges_ref[:, 1:2], (SWEEPS, NB))
    phase = lower & (NB - 1)
    first = lower >> 7
    last = (upper - phase - NB) >> 7
    return phase, first, last


def heads_tails(rows, bounds, block):
    phase, first, last = bounds
    lane = lax.broadcasted_iota(jnp.int32, (SWEEPS, NB), 1)
    head_on = (lane >= phase) & (block >= first) & (block <= last)
    tail_on = (lane < phase) & (block - 1 >= first) & (block - 1 <= last)
    return jnp.where(head_on, rows, 0.0), jnp.where(tail_on, rows, 0.0)


def fold(x, rows):
    group = lane_group(rows)
    turned = pltpu.roll(x, 32, 1)
    def keep(even, odd):
        parts = [(even if q % 2 == 0 else odd)[q * rows:(q + 1) * rows] for q in range(4)]
        out = parts[0]
        for q in range(1, 4):
            out = jnp.where(group == q, parts[q], out)
        return out
    return keep(x, turned), keep(turned, x)


def inner_products(x, right_high, right_low):
    left = jnp.concatenate(split(x), axis=1)
    right = jnp.concatenate([right_high] * 2 + [right_low] * 2, axis=0)
    right = jnp.concatenate([right, right], axis=1)
    prod = lax.dot_general(left, right, (((1,), (1,)), ((), ())), preferred_element_type=F32)
    return prod[:, :NB] + prod[:, NB:]


def outer_products(y, right_high, right_low):
    left = jnp.concatenate(split(y), axis=0)
    def four(both):
        return jnp.concatenate([both[:32]] * 4 + [both[32:]] * 4, axis=0)
    right = jnp.concatenate([four(right_high), four(right_low)], axis=1)
    prod = lax.dot_general(left, right, (((1,), (0,)), ((), ())), preferred_element_type=F32)
    prod = prod[:64] + prod[64:]
    return prod[:, :NB] + prod[:, NB:]


def needed(k):
    lane = lax.broadcasted_iota(jnp.int32, (ROWS, NB), 1) & 31
    return lane >= k - 1


def pack(ref, row_of, message):
    def block(k):
        return ref[pl.ds(row_of(k) * ROWS, ROWS)]

    message[pl.ds(0, ROWS)] = block(1)
    for k in range(2, 17):
        other = pltpu.roll(block(34 - k), NB - 33 + k, 1)
        message[pl.ds((k - 1) * ROWS, ROWS)] = jnp.where(needed(k), block(k), other)
    message[pl.ds(16 * ROWS, ROWS)] = block(17)


def unpack(message, valid=None):
    def block(m):
        data = message[pl.ds(m * ROWS, ROWS)]
        return data if valid is None else jnp.where(valid, data, 0.0)

    yield 1, block(0)
    for k in range(2, 17):
        both = block(k - 1)
        yield k, jnp.where(needed(k), both, 0.0)
        yield 34 - k, jnp.where(needed(34 - k), pltpu.roll(both, 33 - k, 1), 0.0)
    yield 17, jnp.where(needed(17), block(16), 0.0)


def inner_kernel(place_ref, ranges_ref, arrived_ref, v0, v1, v2, v3,
                 out_ref, pair_ref, other_ref, high_ref, low_ref, x_ref, v_ref):
    for k, piece in enumerate((v0, v1, v2, v3)):
        first = pl.multiple_of(((place_ref[1] + k) & 3) * 8, 8)
        v_ref[pl.ds(first, 8), :] = piece[...]
    bounds = sweep_bounds(ranges_ref)
    row = lax.broadcasted_iota(jnp.int32, (SWEEPS, NB), 0)
    lane = lax.broadcasted_iota(jnp.int32, (SWEEPS, NB), 1)
    upper = row <= (lane & 31)
    heads = (lane & 32) == 0
    base = place_ref[0] * OWN
    out_ref[pl.ds(0, ROWS)] = jnp.zeros((ROWS, NB), F32)
    for a in range(OWN):
        cols = pl.ds(a * NB, NB)
        head, tail = heads_tails(v_ref[:, cols], bounds, base + a)
        high, low = split(jnp.concatenate([head, tail], axis=0))
        high_ref[pl.ds(a * 64, 64)] = high
        low_ref[pl.ds(a * 64, 64)] = low
        x = arrived_ref[:, :, cols].reshape(EIG, NB)
        x_ref[:, cols] = x
        inner = inner_products(jnp.concatenate([x, head, tail], axis=0), high, low)
        of_head, of_tail = inner[64:96], inner[96:128]
        gram = jnp.where(upper == heads, of_head, of_tail)
        inner_head, inner_tail = fold(inner[:64], 16)
        gram_head, gram_tail = fold(gram, 8)
        out_ref[pl.ds((a + 1) * ROWS, 16)] = inner_head
        out_ref[pl.ds((a + 1) * ROWS + 16, 8)] = gram_head
        out_ref[pl.ds(a * ROWS, 16)] += inner_tail
        out_ref[pl.ds(a * ROWS + 16, 8)] += gram_tail

    def to_next(message):
        pack(out_ref, lambda k: 33 - k, message)

    def to_last(message):
        pack(out_ref, lambda k: k - 1, message)

    odd = place_ref[0] & 1

    @pl.when(odd == 0)
    def _():
        to_next(pair_ref)
        to_last(other_ref)

    @pl.when(odd == 1)
    def _():
        to_last(pair_ref)
        to_next(other_ref)


def apply_kernel(place_ref, phase_ref, own_ref, pair_ref, other_ref, x_ref, high_ref, low_ref,
                 out_ref, gather, coef, inner, rows_t, *shifted):
    def at(place, count=1):
        return pl.ds(place * ROWS, count * ROWS)

    gather[at(HALO, OWN)] = own_ref[at(1, OWN)]
    gather[at(2 * HALO + OWN - 1, 33)] = jnp.zeros((33 * ROWS, NB), F32)
    gather[at(HALO - 1)] = own_ref[at(0)]

    def take(low_blocks, high_blocks):
        for k, block in low_blocks:
            if k == 1:
                gather[at(HALO - 1)] += block
            else:
                gather[at(HALO - k)] = block
        for k, block in high_blocks:
            if k == 1:
                gather[at(HALO + OWN - 1)] += block
            else:
                gather[at(HALO + OWN - 2 + k)] = block

    odd = place_ref[0] & 1

    @pl.when(odd == 0)
    def _():
        take(unpack(other_ref, place_ref[0] > 0), unpack(pair_ref))

    @pl.when(odd == 1)
    def _():
        take(unpack(pair_ref), unpack(other_ref, place_ref[0] < place_ref[2] - 1))

    for q in range(8):
        block = gather[pl.ds(16 + q, NB, stride=ROWS), :].T
        for g in range(4):
            coef[pl.ds((g * 8 + q) * 32, 32)] = block[g * 32:(g + 1) * 32]
    square = coef[pl.ds(0, SWEEPS, stride=33), :]
    all_tau = jnp.where(square > 0, 2.0 / jnp.where(square > 0, square, 1.0), 0.0)
    row = lax.broadcasted_iota(jnp.int32, (SWEEPS, NB), 0)
    for j in range(SWEEPS):
        mine = jnp.broadcast_to(all_tau[j:j + 1], (SWEEPS, NB))
        coef[pl.ds(j * 32, 32)] *= jnp.where(row < j, all_tau, mine)

    for q in range(16):
        block = gather[pl.ds(q, NB, stride=ROWS), :].T
        for g in range(4):
            part = block[g * 32:(g + 1) * 32] * all_tau
            inner[pl.ds(g * 16 + q, 32, stride=64), :] = part

    phases = [phase_ref[j] for j in range(SWEEPS)]
    for j in range(SWEEPS - 1, -1, -1):
        total = inner[pl.ds(j * EIG, EIG)]
        for i in range(SWEEPS - 1, j, -1):
            same = coef[pl.ds(j * 32 + i, 1), :]
            next_to = coef[pl.ds(i * 32 + j, 1), :]
            start = pl.multiple_of(jnp.where(phases[j] < phases[i], 0, EIG), EIG)
            total = total - same * inner[pl.ds(i * EIG, EIG)] - next_to * shifted[i][pl.ds(start, EIG)]
        inner[pl.ds(j * EIG, EIG)] = total
        if j > 0:
            shifted[j][pl.ds(0, EIG)] = pltpu.roll(total, 1, 1)
            shifted[j][pl.ds(EIG, EIG)] = pltpu.roll(total, NB - 1, 1)

    for q in range(16):
        parts = [inner[pl.ds(g * 16 + q, 32, stride=64), :] for g in range(4)]
        block = jnp.concatenate(parts, axis=0).T
        rows_t[pl.ds(q, 40, stride=16), :] = block[24:64]

    group = lane_group(16)
    for a in range(OWN):
        cols = pl.ds(a * NB, NB)
        rows = pl.ds(a * 64, 64)
        of_head = rows_t[pl.ds((a + 8) * 16, 16)]
        of_tail = rows_t[pl.ds((a + 7) * 16, 16)]
        spread = [jnp.concatenate([jnp.where(group == g, y, 0.0) for g in range(4)], axis=0)
                  for y in (of_head, of_tail)]
        update = outer_products(jnp.concatenate(spread, axis=1), high_ref[rows], low_ref[rows])
        out_ref[:, cols] = x_ref[:, cols] - update


def call(kernel, name, out_shape, scratch, operands):
    vmem = pl.BlockSpec(memory_space=pltpu.VMEM)
    smem = pl.BlockSpec(memory_space=pltpu.SMEM)
    specs = [smem if x.ndim == 1 else vmem for x in operands]
    return pl.pallas_call(
        kernel,
        out_shape=tuple(jax.ShapeDtypeStruct(*x) for x in out_shape),
        in_specs=specs,
        out_specs=(vmem,) * len(out_shape),
        scratch_shapes=[pltpu.VMEM(x, F32) for x in scratch],
        compiler_params=pltpu.CompilerParams(vmem_limit_bytes=VMEM_LIMIT),
        name=name,
    )(*operands)


def back_transform(x, pieces, sweep_ranges):
    count = lax.axis_size("row")
    place = jnp.stack([lax.axis_index("row"), lax.axis_index("col"), count]).astype(jnp.int32)
    phase = sweep_ranges[:, 0] % NB
    message = ((17 * ROWS, NB), F32)
    own, to_pair, to_other, high, low, x = call(
        inner_kernel, "inner_products",
        [(((OWN + 1) * ROWS, NB), F32), message, message, ((OWN * 64, NB), BF16), ((OWN * 64, NB), BF16), ((EIG, OWN * NB), F32)],
        [(SWEEPS, OWN * NB)],
        [place, sweep_ranges, x, *pieces],
    )
    within = [(i, i ^ 1) for i in range(count)]
    across = [(i, (i + 1) % count) for i in range(1, count, 2)]
    across = across + [(t, s) for s, t in across]
    pair = lax.ppermute(to_pair, "row", within)
    other = lax.ppermute(to_other, "row", across)
    out, = call(
        apply_kernel, "apply_sweeps",
        [((EIG, OWN * NB), F32)],
        [(NB * ROWS, NB), (SWEEPS * 32, NB), (SWEEPS * EIG, NB), (40 * 16, NB)] + [(2 * EIG, NB)] * SWEEPS,
        [place, phase, own, pair, other, x, high, low],
    )
    return out


def sweep_pieces(reflectors):
    cols, count = lax.axis_size("col"), lax.axis_size("row")
    width = count // cols
    groups = [[g * width + q for q in range(width)] for g in range(cols)]
    mine = lax.all_to_all(
        reflectors.reshape(width, -1), "row", split_axis=0, concat_axis=0, tiled=True,
        axis_index_groups=groups,
    )
    pieces = []
    for k in range(cols):
        pairs = [
            (c * count + g * width + q, ((g - k) % cols) * count + c * width + q)
            for c in range(cols) for g in range(cols) for q in range(width)
        ]
        pieces.append(lax.ppermute(mine, ("col", "row"), pairs))
    return pieces


def per_device(eigenvectors, reflectors, sweep_ranges):
    pieces = sweep_pieces(reflectors)
    x = lax.all_to_all(eigenvectors.reshape(2, -1, OWN * NB), "row", split_axis=1, concat_axis=1, tiled=True)
    x = x.transpose(1, 0, 2)
    return back_transform(x, pieces, sweep_ranges)


def solution(mesh):
    placed = (P(("col", "row"), None), P("row", "col"), P())
    return jax.shard_map(
        per_device, mesh=mesh, in_specs=placed, out_specs=P("col", "row"), check_vma=False
    )
```

time: 61.7 us -> 58.6 us (0.950)
  the two profiles are of different devices: /device:TPU:15 before, /device:TPU:24 now
where the time goes in v3:
time: 58.6 us; the launch traced here: 58.3 us
  starting transfers between devices  19.6 us (33%)
  waiting for transfers between devices  16.9 us (29%)
  Pallas kernels  10.5 us (18%)
  blocking collectives  10.4 us (18%)
  local copies, waits for them, and re-layouts  0.85 us (1%)
    ppermute x4, waiting for transfers between devices, sweep_pieces(): pieces.append(lax.ppermute(mine, ('col', 'row'), pairs))  10.9 us
    pallas_call x2, Pallas kernels, call(): pl.pallas_call(kernel, out_shape=tuple((jax.ShapeDtypeStruct(*x) for x in...  10.5 us
    all_to_all x1, blocking collectives, sweep_pieces(): lax.all_to_all(reflectors.reshape(width, -1), 'row', split_axis=0, concat...  10.4 us
    ppermute x4, starting transfers between devices, sweep_pieces(): pieces.append(lax.ppermute(mine, ('col', 'row'), pairs))  9.48 us
    all_to_all x1, starting transfers between devices, per_device(): lax.all_to_all(eigenvectors.reshape(2, -1, OWN * NB), 'row', split_axis=1...  6.31 us
    ppermute x1, waiting for transfers between devices, back_transform(): other = lax.ppermute(to_other, 'row', across)  4.88 us
    ppermute x1, starting transfers between devices, back_transform(): other = lax.ppermute(to_other, 'row', across)  3.73 us
  transfers between devices with their start and end apart: 7, of which 5 were waited for; matrix products, arithmetic and copies ran while one was open for 0% of the time, Pallas kernels for 0%

profile of v3, /device:TPU:24, one launch (start us, length us, event | category | flops | bytes accessed | tf_op | source)
XLA Modules:
  0.0 58.3 jit_solution(12088832301861149840)
XLA Ops:
  0.0 10.4 %all_to_all.17 = f32[8,1,4096]{2,1,0:T(1,128)S(1)} all-to-all(f32[8,1,4096]{2,1,0:T(1,128)} %bitcast.12), channel_id=1, replica_groups={{0,1,2,3,4,5,6,7},{8,9,10,11,12,13,14,15},{16,17,18,19,20,21,22,23},{24..., dimensions={0} | all-to-all | bytes 262144 | tf_op jit(solution)/shard_map/all_to_all | solution.py:276
  10.4 6.3 %all-to-all-start = ((f32[2,32,4096]{2,0,1:T(2,128)}), f32[2,32,4096]{2,0,1:T(2,128)S(1)}, u32[]{:S(2)}, u32[]{:S(2)}) async-start(f32[2,32,4096]{2,0,1:T(2,128)} %bitcast.11), calls=%async_computation | async-start | bytes 2097152 | tf_op jit(solution)/shard_map/all_to_all | solution.py:292
  16.7 0.1 copy.8
  16.8 4.6 %collective-permute-start = (f32[8,4096]{1,0:T(8,128)S(1)}, f32[8,4096]{1,0:T(8,128)S(1)}, u32[]{:S(2)}, u32[]{:S(2)}) collective-permute-start(f32[8,4096]{1,0:T(8,128)S(1)} %bitcast.13), channel_id=1, source_target_pairs={{0,0},{1,1},{2,2},{3,3},{4,4},{5,5},{6,6},{7,7},{8,32},{9,33},{10,... | collective-permute-start | bytes 393224 | tf_op jit(solution)/shard_map/ppermute | solution.py:286
  21.5 0.1 collective-permute-start.1
  21.5 2.1 %collective-permute-start.2 = (f32[8,4096]{1,0:T(8,128)S(1)}, f32[8,4096]{1,0:T(8,128)S(1)}, u32[]{:S(2)}, u32[]{:S(2)}) collective-permute-start(f32[8,4096]{1,0:T(8,128)S(1)} %bitcast.15), channel_id=1, source_target_pairs={{0,64},{1,65},{2,66},{3,67},{4,68},{5,69},{6,70},{7,71},{8,96},{9,... | collective-permute-start | bytes 393224 | tf_op jit(solution)/shard_map/ppermute | solution.py:286
  23.7 2.7 %collective-permute-start.3 = (f32[8,4096]{1,0:T(8,128)S(1)}, f32[8,4096]{1,0:T(8,128)S(1)}, u32[]{:S(2)}, u32[]{:S(2)}) collective-permute-start(f32[8,4096]{1,0:T(8,128)S(1)} %bitcast.16), channel_id=1, source_target_pairs={{0,32},{1,33},{2,34},{3,35},{4,36},{5,37},{6,38},{7,39},{8,64},{9,... | collective-permute-start | bytes 393224 | tf_op jit(solution)/shard_map/ppermute | solution.py:286
  26.3 0.0 copy-start
  26.3 0.7 %copy-done = s32[32,2]{0,1:T(2,128)S(1)} copy-done((s32[32,2]{0,1:T(2,128)S(1)}, s32[32,2]{0,1:T(2,128)}, u32[]{:S(2)}) %copy-start) | copy-done | bytes 280
  27.0 0.1 copy.5.ranges_ref
  27.1 0.1 pad_add_fusion.place_ref
  27.2 5.1 %collective-permute-done.v0 = f32[8,4096]{1,0:T(8,128)S(1)} collective-permute-done((f32[8,4096]{1,0:T(8,128)S(1)}, f32[8,4096]{1,0:T(8,128)S(1)}, u32[]{:S(2)}, u32[]{:S(2)}) %collective-permute-start) | collective-permute-done | bytes 131104 | tf_op jit(solution)/shard_map/ppermute | solution.py:286
  32.3 0.0 collective-permute-done.1.v1
  32.3 1.2 %collective-permute-done.2.v2 = f32[8,4096]{1,0:T(8,128)S(1)} collective-permute-done((f32[8,4096]{1,0:T(8,128)S(1)}, f32[8,4096]{1,0:T(8,128)S(1)}, u32[]{:S(2)}, u32[]{:S(2)}) %collective-permute-start.2) | collective-permute-done | bytes 131104 | tf_op jit(solution)/shard_map/ppermute | solution.py:286
  33.5 4.6 %collective-permute-done.3.v3 = f32[8,4096]{1,0:T(8,128)S(1)} collective-permute-done((f32[8,4096]{1,0:T(8,128)S(1)}, f32[8,4096]{1,0:T(8,128)S(1)}, u32[]{:S(2)}, u32[]{:S(2)}) %collective-permute-start.3) | collective-permute-done | bytes 131104 | tf_op jit(solution)/shard_map/ppermute | solution.py:286
  38.0 1.1 %all-to-all-done = f32[2,32,4096]{2,0,1:T(2,128)S(1)} async-done(((f32[2,32,4096]{2,0,1:T(2,128)}), f32[2,32,4096]{2,0,1:T(2,128)S(1)}, u32[]{:S(2)}, u32[]{:S(2)}) %all-to-all-start) | async-done | bytes 1048608 | tf_op jit(solution)/shard_map/all_to_all | solution.py:292
  39.1 2.5 %inner_products.1 = (f32[792,128]{1,0:T(8,128)S(1)}, f32[408,128]{1,0:T(8,128)S(1)}, f32[408,128]{1,0:T(8,128)S(1)}, bf16[2048,128]{1,0:T(8,128)(2,1)S(1)}, bf16...) custom-call(s32[3]{0:T(128)S(1)} %pad_add_fusion.place_ref, s32[32,2]{1,0:T(8,128)S(1)} %copy.5.ranges_ref, ...), custom_call_target="tpu_custom_call" | custom-call | tf_op jit(solution)/shard_map/inner_products/pallas_call | solution.py:236
  41.6 0.1 collective-permute-start.4
  41.7 3.7 %collective-permute-start.5 = (f32[408,128]{1,0:T(8,128)S(1)}, f32[408,128]{1,0:T(8,128)S(1)}, u32[]{:S(2)}, u32[]{:S(2)}) collective-permute-start(f32[408,128]{1,0:T(8,128)S(1)} %get-tuple-element.13), channel_id=1, source_target_pairs={{1,2},{3,4},{5,6},{7,8},{9,10},{11,12},{13,14},{15,16},{17,18},{19... | collective-permute-start | bytes 626696 | tf_op jit(solution)/shard_map/ppermute | solution.py:262
  45.4 0.0 collective-permute-done.4.pair_ref
  45.4 4.9 %collective-permute-done.5.other_ref = f32[408,128]{1,0:T(8,128)S(1)} collective-permute-done((f32[408,128]{1,0:T(8,128)S(1)}, f32[408,128]{1,0:T(8,128)S(1)}, u32[]{:S(2)}, u32[]{:S(2)}) %collective-permute-start.5) | collective-permute-done | bytes 208928 | tf_op jit(solution)/shard_map/ppermute | solution.py:262
  50.3 8.0 %apply_sweeps.1 = f32[64,4096]{1,0:T(8,128)} custom-call(s32[3]{0:T(128)S(1)} %pad_add_fusion.place_ref, s32[32]{0:T(128)S(1)} %and_select_fusion.phase_ref, f32[792,128]{1,0:T(8,128)S(1)} %get-tuple-element.11.own_ref, f32[408,128]{1,0:T(8,128)S(1)} %collective-permute-done.4.pair_ref, f32[408,128]{1,0:T(8,128)S(1)} %collective-permute-done.5.other_ref, ...), custom_call_target="tpu_custom_call" | custom-call | tf_op jit(solution)/shard_map/apply_sweeps/pallas_call | solution.py:236
  (1 shorter events, 0.0 us)
Async XLA Ops:
  10.4 28.7 %all-to-all-start = ((f32[2,32,4096]{2,0,1:T(2,128)}), f32[2,32,4096]{2,0,1:T(2,128)S(1)}, u32[]{:S(2)}, u32[]{:S(2)}) async-start(f32[2,32,4096]{2,0,1:T(2,128)} %bitcast.11), calls=%async_computation | async-start | bytes 2097152 | tf_op jit(solution)/shard_map/all_to_all | solution.py:292
  16.8 15.4 %collective-permute-start = (f32[8,4096]{1,0:T(8,128)S(1)}, f32[8,4096]{1,0:T(8,128)S(1)}, u32[]{:S(2)}, u32[]{:S(2)}) collective-permute-start(f32[8,4096]{1,0:T(8,128)S(1)} %bitcast.13), channel_id=1, source_target_pairs={{0,0},{1,1},{2,2},{3,3},{4,4},{5,5},{6,6},{7,7},{8,32},{9,33},{10,... | collective-permute-start | bytes 393224 | tf_op jit(solution)/shard_map/ppermute | solution.py:286
  21.5 10.8 %collective-permute-start.1 = (f32[8,4096]{1,0:T(8,128)S(1)}, f32[8,4096]{1,0:T(8,128)S(1)}, u32[]{:S(2)}, u32[]{:S(2)}) collective-permute-start(f32[8,4096]{1,0:T(8,128)S(1)} %bitcast.14), channel_id=1, source_target_pairs={{0,96},{1,97},{2,98},{3,99},{4,100},{5,101},{6,102},{7,103},{8,0},... | collective-permute-start | bytes 393224 | tf_op jit(solution)/shard_map/ppermute | solution.py:286
  21.5 11.9 %collective-permute-start.2 = (f32[8,4096]{1,0:T(8,128)S(1)}, f32[8,4096]{1,0:T(8,128)S(1)}, u32[]{:S(2)}, u32[]{:S(2)}) collective-permute-start(f32[8,4096]{1,0:T(8,128)S(1)} %bitcast.15), channel_id=1, source_target_pairs={{0,64},{1,65},{2,66},{3,67},{4,68},{5,69},{6,70},{7,71},{8,96},{9,... | collective-permute-start | bytes 393224 | tf_op jit(solution)/shard_map/ppermute | solution.py:286
  23.7 14.4 %collective-permute-start.3 = (f32[8,4096]{1,0:T(8,128)S(1)}, f32[8,4096]{1,0:T(8,128)S(1)}, u32[]{:S(2)}, u32[]{:S(2)}) collective-permute-start(f32[8,4096]{1,0:T(8,128)S(1)} %bitcast.16), channel_id=1, source_target_pairs={{0,32},{1,33},{2,34},{3,35},{4,36},{5,37},{6,38},{7,39},{8,64},{9,... | collective-permute-start | bytes 393224 | tf_op jit(solution)/shard_map/ppermute | solution.py:286
  26.3 0.7 %copy-start = (s32[32,2]{0,1:T(2,128)S(1)}, s32[32,2]{0,1:T(2,128)}, u32[]{:S(2)}) copy-start(s32[32,2]{0,1:T(2,128)} %param.5) | copy-start | bytes 772
  41.6 3.8 %collective-permute-start.4 = (f32[408,128]{1,0:T(8,128)S(1)}, f32[408,128]{1,0:T(8,128)S(1)}, u32[]{:S(2)}, u32[]{:S(2)}) collective-permute-start(f32[408,128]{1,0:T(8,128)S(1)} %get-tuple-element.12), channel_id=1, source_target_pairs={{0,1},{1,0},{2,3},{3,2},{4,5},{5,4},{6,7},{7,6},{8,9},{9,8},{10,11... | collective-permute-start | bytes 626696 | tf_op jit(solution)/shard_map/ppermute | solution.py:261
  41.7 8.6 %collective-permute-start.5 = (f32[408,128]{1,0:T(8,128)S(1)}, f32[408,128]{1,0:T(8,128)S(1)}, u32[]{:S(2)}, u32[]{:S(2)}) collective-permute-start(f32[408,128]{1,0:T(8,128)S(1)} %get-tuple-element.13), channel_id=1, source_target_pairs={{1,2},{3,4},{5,6},{7,8},{9,10},{11,12},{13,14},{15,16},{17,18},{19... | collective-permute-start | bytes 626696 | tf_op jit(solution)/shard_map/ppermute | solution.py:262

commit v4 on v3

--- a/solution.py
+++ b/solution.py
@@ -10,6 +10,8 @@
 OWN = 32
 EIG = 64
 HALO = 32
+PART = 8
+WIDE = 16
 ROWS = 24
 F32 = jnp.float32
 BF16 = jnp.bfloat16
@@ -20,6 +22,11 @@
     high = x.astype(BF16)
     low = (x - high.astype(F32)).astype(BF16)
     return high, low
+
+
+def halves(low, high):
+    lane = lax.broadcasted_iota(jnp.int32, low.shape, 1)
+    return jnp.where(lane < 64, pltpu.roll(low, NB - 16, 1), pltpu.roll(high, 48, 1))
 
 
 def lane_group(rows):
@@ -152,7 +159,7 @@
 
 
 def apply_kernel(place_ref, phase_ref, own_ref, pair_ref, other_ref, x_ref, high_ref, low_ref,
-                 out_ref, gather, coef, inner, rows_t, *shifted):
+                 out_ref, result, sems, gather, coef, coef_half, inner, inner_half, rows_t, *shifted):
     def at(place, count=1):
         return pl.ds(place * ROWS, count * ROWS)
 
@@ -191,45 +198,81 @@
     row = lax.broadcasted_iota(jnp.int32, (SWEEPS, NB), 0)
     for j in range(SWEEPS):
         mine = jnp.broadcast_to(all_tau[j:j + 1], (SWEEPS, NB))
-        coef[pl.ds(j * 32, 32)] *= jnp.where(row < j, all_tau, mine)
+        scaled = coef[pl.ds(j * 32, 32)] * jnp.where(row < j, all_tau, mine)
+        coef[pl.ds(j * 32, 32)] = scaled
+        count = 32 if j < WIDE else 16
+        coef_half[pl.ds(j * 32, count)] = halves(scaled[:count], scaled[:count])
 
     for q in range(16):
         block = gather[pl.ds(q, NB, stride=ROWS), :].T
+        parts = [block[g * 32:(g + 1) * 32] * all_tau for g in range(4)]
         for g in range(4):
-            part = block[g * 32:(g + 1) * 32] * all_tau
-            inner[pl.ds(g * 16 + q, 32, stride=64), :] = part
+            inner[pl.ds(g * 16 + q + 8 * EIG, 24, stride=64), :] = parts[g][8:]
+        for g in range(2):
+            inner_half[pl.ds(g * 16 + q, 16, stride=32), :] = halves(parts[g][:16], parts[g + 2][:16])
 
     phases = [phase_ref[j] for j in range(SWEEPS)]
-    for j in range(SWEEPS - 1, -1, -1):
+    wide, half = shifted[:SWEEPS - WIDE], shifted[SWEEPS - WIDE:]
+    lane = lax.broadcasted_iota(jnp.int32, (EIG // 2, NB), 1) & 63
+
+    def keep_half(j, y):
+        half[j][pl.ds(0, 32)] = jnp.where(lane == 0, 0.0, pltpu.roll(y, 1, 1))
+        half[j][pl.ds(32, 32)] = jnp.where(lane == 63, 0.0, pltpu.roll(y, NB - 1, 1))
+
+    for j in range(SWEEPS - 1, WIDE - 2, -1):
         total = inner[pl.ds(j * EIG, EIG)]
         for i in range(SWEEPS - 1, j, -1):
             same = coef[pl.ds(j * 32 + i, 1), :]
             next_to = coef[pl.ds(i * 32 + j, 1), :]
             start = pl.multiple_of(jnp.where(phases[j] < phases[i], 0, EIG), EIG)
-            total = total - same * inner[pl.ds(i * EIG, EIG)] - next_to * shifted[i][pl.ds(start, EIG)]
+            total = total - same * inner[pl.ds(i * EIG, EIG)] - next_to * wide[i - WIDE][pl.ds(start, EIG)]
         inner[pl.ds(j * EIG, EIG)] = total
+        if j >= WIDE:
+            wide[j - WIDE][pl.ds(0, EIG)] = pltpu.roll(total, 1, 1)
+            wide[j - WIDE][pl.ds(EIG, EIG)] = pltpu.roll(total, NB - 1, 1)
+        both = halves(total[:32], total[32:])
+        inner_half[pl.ds(j * 32, 32)] = both
+        keep_half(j, both)
+
+    for j in range(WIDE - 2, -1, -1):
+        total = inner_half[pl.ds(j * 32, 32)]
+        for i in range(SWEEPS - 1, j, -1):
+            same = coef_half[pl.ds(j * 32 + i, 1), :]
+            next_to = coef_half[pl.ds(i * 32 + j, 1), :]
+            start = pl.multiple_of(jnp.where(phases[j] < phases[i], 0, 32), 32)
+            total = total - same * inner_half[pl.ds(i * 32, 32)] - next_to * half[i][pl.ds(start, 32)]
+        inner_half[pl.ds(j * 32, 32)] = total
         if j > 0:
-            shifted[j][pl.ds(0, EIG)] = pltpu.roll(total, 1, 1)
-            shifted[j][pl.ds(EIG, EIG)] = pltpu.roll(total, NB - 1, 1)
-
-    for q in range(16):
-        parts = [inner[pl.ds(g * 16 + q, 32, stride=64), :] for g in range(4)]
+            keep_half(j, total)
+
+    for t in range(8):
+        parts = [inner_half[pl.ds(g * 16 + q * 8 + t, 32, stride=32), :] for q in range(2) for g in range(2)]
         block = jnp.concatenate(parts, axis=0).T
-        rows_t[pl.ds(q, 40, stride=16), :] = block[24:64]
-
-    group = lane_group(16)
+        for h in range(2):
+            rows_t[pl.ds(h * 8 + t, 40, stride=16), :] = block[h * 64 + 8:h * 64 + 48]
+
+    def copy_out(c):
+        part = pl.ds(c * PART * NB, PART * NB)
+        return pltpu.make_async_copy(result.at[:, part], out_ref.at[:, part], sems.at[c])
+
+    group = lane_group(8)
     for a in range(OWN):
         cols = pl.ds(a * NB, NB)
         rows = pl.ds(a * 64, 64)
         of_head = rows_t[pl.ds((a + 8) * 16, 16)]
         of_tail = rows_t[pl.ds((a + 7) * 16, 16)]
-        spread = [jnp.concatenate([jnp.where(group == g, y, 0.0) for g in range(4)], axis=0)
+        spread = [jnp.concatenate([jnp.where(group == q * 2 + g, y[h * 8:h * 8 + 8], 0.0)
+                                   for h in range(2) for g in range(2) for q in range(2)], axis=0)
                   for y in (of_head, of_tail)]
         update = outer_products(jnp.concatenate(spread, axis=1), high_ref[rows], low_ref[rows])
-        out_ref[:, cols] = x_ref[:, cols] - update
-
-
-def call(kernel, name, out_shape, scratch, operands):
+        result[:, cols] = x_ref[:, cols] - update
+        if (a + 1) % PART == 0:
+            copy_out(a // PART).start()
+    for c in range(OWN // PART):
+        copy_out(c).wait()
+
+
+def call(kernel, name, out_shape, scratch, operands, space=pltpu.VMEM):
     vmem = pl.BlockSpec(memory_space=pltpu.VMEM)
     smem = pl.BlockSpec(memory_space=pltpu.SMEM)
     specs = [smem if x.ndim == 1 else vmem for x in operands]
@@ -237,8 +280,8 @@
         kernel,
         out_shape=tuple(jax.ShapeDtypeStruct(*x) for x in out_shape),
         in_specs=specs,
-        out_specs=(vmem,) * len(out_shape),
-        scratch_shapes=[pltpu.VMEM(x, F32) for x in scratch],
+        out_specs=(pl.BlockSpec(memory_space=space),) * len(out_shape),
+        scratch_shapes=[pltpu.VMEM(x, F32) if isinstance(x, tuple) else x for x in scratch],
         compiler_params=pltpu.CompilerParams(vmem_limit_bytes=VMEM_LIMIT),
         name=name,
     )(*operands)
@@ -263,8 +306,10 @@
     out, = call(
         apply_kernel, "apply_sweeps",
         [((EIG, OWN * NB), F32)],
-        [(NB * ROWS, NB), (SWEEPS * 32, NB), (SWEEPS * EIG, NB), (40 * 16, NB)] + [(2 * EIG, NB)] * SWEEPS,
+        [(EIG, OWN * NB), pltpu.SemaphoreType.DMA((OWN // PART,)), (NB * ROWS, NB), (SWEEPS * 32, NB), (SWEEPS * 32, NB), (SWEEPS * EIG, NB), (SWEEPS * 32, NB), (40 * 16, NB)]
+        + [(2 * EIG, NB)] * (SWEEPS - WIDE) + [(EIG, NB)] * SWEEPS,
         [place, phase, own, pair, other, x, high, low],
+        pl.ANY,
     )
     return out
 

time: 58.6 us -> 56.7 us (0.968)
  Pallas kernels: 10.5 us -> 8.54 us
    pallas_call x2, Pallas kernels: 10.5 us -> 8.54 us  [call(): pl.pallas_call(kernel, out_shape=tuple((jax.ShapeDtypeStruct(*x) for x in...]
where the time goes in v4:
time: 56.7 us; the launch traced here: 56.4 us
  starting transfers between devices  19.6 us (35%)
  waiting for transfers between devices  16.9 us (30%)
  blocking collectives  10.4 us (18%)
  Pallas kernels  8.54 us (15%)
  local copies, waits for them, and re-layouts  0.85 us (1%)
    ppermute x4, waiting for transfers between devices, sweep_pieces(): pieces.append(lax.ppermute(mine, ('col', 'row'), pairs))  10.9 us
    all_to_all x1, blocking collectives, sweep_pieces(): lax.all_to_all(reflectors.reshape(width, -1), 'row', split_axis=0, concat...  10.4 us
    ppermute x4, starting transfers between devices, sweep_pieces(): pieces.append(lax.ppermute(mine, ('col', 'row'), pairs))  9.48 us
    pallas_call x2, Pallas kernels, call(): pl.pallas_call(kernel, out_shape=tuple((jax.ShapeDtypeStruct(*x) for x in...  8.54 us
    all_to_all x1, starting transfers between devices, per_device(): lax.all_to_all(eigenvectors.reshape(2, -1, OWN * NB), 'row', split_axis=1...  6.31 us
    ppermute x1, waiting for transfers between devices, back_transform(): other = lax.ppermute(to_other, 'row', across)  4.88 us
    ppermute x1, starting transfers between devices, back_transform(): other = lax.ppermute(to_other, 'row', across)  3.73 us
  transfers between devices with their start and end apart: 7, of which 5 were waited for; matrix products, arithmetic and copies ran while one was open for 0% of the time, Pallas kernels for 0%

profile of v4, /device:TPU:24, one launch (start us, length us, event | category | flops | bytes accessed | tf_op | source)
XLA Modules:
  0.0 56.4 jit_solution(17587135320353226966)
XLA Ops:
  0.0 10.4 %all_to_all.17 = f32[8,1,4096]{2,1,0:T(1,128)S(1)} all-to-all(f32[8,1,4096]{2,1,0:T(1,128)} %bitcast.12), channel_id=1, replica_groups={{0,1,2,3,4,5,6,7},{8,9,10,11,12,13,14,15},{16,17,18,19,20,21,22,23},{24..., dimensions={0} | all-to-all | bytes 262144 | tf_op jit(solution)/shard_map/all_to_all | solution.py:321
  10.4 6.3 %all-to-all-start = ((f32[2,32,4096]{2,0,1:T(2,128)}), f32[2,32,4096]{2,0,1:T(2,128)S(1)}, u32[]{:S(2)}, u32[]{:S(2)}) async-start(f32[2,32,4096]{2,0,1:T(2,128)} %bitcast.11), calls=%async_computation | async-start | bytes 2097152 | tf_op jit(solution)/shard_map/all_to_all | solution.py:337
  16.7 0.1 copy.8
  16.8 4.6 %collective-permute-start = (f32[8,4096]{1,0:T(8,128)S(1)}, f32[8,4096]{1,0:T(8,128)S(1)}, u32[]{:S(2)}, u32[]{:S(2)}) collective-permute-start(f32[8,4096]{1,0:T(8,128)S(1)} %bitcast.13), channel_id=1, source_target_pairs={{0,0},{1,1},{2,2},{3,3},{4,4},{5,5},{6,6},{7,7},{8,32},{9,33},{10,... | collective-permute-start | bytes 393224 | tf_op jit(solution)/shard_map/ppermute | solution.py:331
  21.5 0.1 collective-permute-start.1
  21.5 2.1 %collective-permute-start.2 = (f32[8,4096]{1,0:T(8,128)S(1)}, f32[8,4096]{1,0:T(8,128)S(1)}, u32[]{:S(2)}, u32[]{:S(2)}) collective-permute-start(f32[8,4096]{1,0:T(8,128)S(1)} %bitcast.15), channel_id=1, source_target_pairs={{0,64},{1,65},{2,66},{3,67},{4,68},{5,69},{6,70},{7,71},{8,96},{9,... | collective-permute-start | bytes 393224 | tf_op jit(solution)/shard_map/ppermute | solution.py:331
  23.7 2.7 %collective-permute-start.3 = (f32[8,4096]{1,0:T(8,128)S(1)}, f32[8,4096]{1,0:T(8,128)S(1)}, u32[]{:S(2)}, u32[]{:S(2)}) collective-permute-start(f32[8,4096]{1,0:T(8,128)S(1)} %bitcast.16), channel_id=1, source_target_pairs={{0,32},{1,33},{2,34},{3,35},{4,36},{5,37},{6,38},{7,39},{8,64},{9,... | collective-permute-start | bytes 393224 | tf_op jit(solution)/shard_map/ppermute | solution.py:331
  26.3 0.0 copy-start
  26.3 0.7 %copy-done = s32[32,2]{0,1:T(2,128)S(1)} copy-done((s32[32,2]{0,1:T(2,128)S(1)}, s32[32,2]{0,1:T(2,128)}, u32[]{:S(2)}) %copy-start) | copy-done | bytes 280
  27.0 0.1 copy.5.ranges_ref
  27.1 0.1 pad_add_fusion.place_ref
  27.2 5.1 %collective-permute-done.v0 = f32[8,4096]{1,0:T(8,128)S(1)} collective-permute-done((f32[8,4096]{1,0:T(8,128)S(1)}, f32[8,4096]{1,0:T(8,128)S(1)}, u32[]{:S(2)}, u32[]{:S(2)}) %collective-permute-start) | collective-permute-done | bytes 131104 | tf_op jit(solution)/shard_map/ppermute | solution.py:331
  32.3 0.0 collective-permute-done.1.v1
  32.3 1.2 %collective-permute-done.2.v2 = f32[8,4096]{1,0:T(8,128)S(1)} collective-permute-done((f32[8,4096]{1,0:T(8,128)S(1)}, f32[8,4096]{1,0:T(8,128)S(1)}, u32[]{:S(2)}, u32[]{:S(2)}) %collective-permute-start.2) | collective-permute-done | bytes 131104 | tf_op jit(solution)/shard_map/ppermute | solution.py:331
  33.5 4.6 %collective-permute-done.3.v3 = f32[8,4096]{1,0:T(8,128)S(1)} collective-permute-done((f32[8,4096]{1,0:T(8,128)S(1)}, f32[8,4096]{1,0:T(8,128)S(1)}, u32[]{:S(2)}, u32[]{:S(2)}) %collective-permute-start.3) | collective-permute-done | bytes 131104 | tf_op jit(solution)/shard_map/ppermute | solution.py:331
  38.0 1.1 %all-to-all-done = f32[2,32,4096]{2,0,1:T(2,128)S(1)} async-done(((f32[2,32,4096]{2,0,1:T(2,128)}), f32[2,32,4096]{2,0,1:T(2,128)S(1)}, u32[]{:S(2)}, u32[]{:S(2)}) %all-to-all-start) | async-done | bytes 1048608 | tf_op jit(solution)/shard_map/all_to_all | solution.py:337
  39.1 2.5 %inner_products.1 = (f32[792,128]{1,0:T(8,128)S(1)}, f32[408,128]{1,0:T(8,128)S(1)}, f32[408,128]{1,0:T(8,128)S(1)}, bf16[2048,128]{1,0:T(8,128)(2,1)S(1)}, bf16...) custom-call(s32[3]{0:T(128)S(1)} %pad_add_fusion.place_ref, s32[32,2]{1,0:T(8,128)S(1)} %copy.5.ranges_ref, ...), custom_call_target="tpu_custom_call" | custom-call | tf_op jit(solution)/shard_map/inner_products/pallas_call | solution.py:279
  41.6 0.1 collective-permute-start.4
  41.7 3.7 %collective-permute-start.5 = (f32[408,128]{1,0:T(8,128)S(1)}, f32[408,128]{1,0:T(8,128)S(1)}, u32[]{:S(2)}, u32[]{:S(2)}) collective-permute-start(f32[408,128]{1,0:T(8,128)S(1)} %get-tuple-element.13), channel_id=1, source_target_pairs={{1,2},{3,4},{5,6},{7,8},{9,10},{11,12},{13,14},{15,16},{17,18},{19... | collective-permute-start | bytes 626696 | tf_op jit(solution)/shard_map/ppermute | solution.py:305
  45.4 0.0 collective-permute-done.4.pair_ref
  45.4 4.9 %collective-permute-done.5.other_ref = f32[408,128]{1,0:T(8,128)S(1)} collective-permute-done((f32[408,128]{1,0:T(8,128)S(1)}, f32[408,128]{1,0:T(8,128)S(1)}, u32[]{:S(2)}, u32[]{:S(2)}) %collective-permute-start.5) | collective-permute-done | bytes 208928 | tf_op jit(solution)/shard_map/ppermute | solution.py:305
  50.3 6.1 %apply_sweeps.1 = f32[64,4096]{1,0:T(8,128)} custom-call(s32[3]{0:T(128)S(1)} %pad_add_fusion.place_ref, s32[32]{0:T(128)S(1)} %and_select_fusion.phase_ref, f32[792,128]{1,0:T(8,128)S(1)} %get-tuple-element.11.own_ref, f32[408,128]{1,0:T(8,128)S(1)} %collective-permute-done.4.pair_ref, f32[408,128]{1,0:T(8,128)S(1)} %collective-permute-done.5.other_ref, ...), custom_call_target="tpu_custom_call" | custom-call | tf_op jit(solution)/shard_map/apply_sweeps/pallas_call | solution.py:279
  (1 shorter events, 0.0 us)
Async XLA Ops:
  10.4 28.7 %all-to-all-start = ((f32[2,32,4096]{2,0,1:T(2,128)}), f32[2,32,4096]{2,0,1:T(2,128)S(1)}, u32[]{:S(2)}, u32[]{:S(2)}) async-start(f32[2,32,4096]{2,0,1:T(2,128)} %bitcast.11), calls=%async_computation | async-start | bytes 2097152 | tf_op jit(solution)/shard_map/all_to_all | solution.py:337
  16.8 15.4 %collective-permute-start = (f32[8,4096]{1,0:T(8,128)S(1)}, f32[8,4096]{1,0:T(8,128)S(1)}, u32[]{:S(2)}, u32[]{:S(2)}) collective-permute-start(f32[8,4096]{1,0:T(8,128)S(1)} %bitcast.13), channel_id=1, source_target_pairs={{0,0},{1,1},{2,2},{3,3},{4,4},{5,5},{6,6},{7,7},{8,32},{9,33},{10,... | collective-permute-start | bytes 393224 | tf_op jit(solution)/shard_map/ppermute | solution.py:331
  21.5 10.8 %collective-permute-start.1 = (f32[8,4096]{1,0:T(8,128)S(1)}, f32[8,4096]{1,0:T(8,128)S(1)}, u32[]{:S(2)}, u32[]{:S(2)}) collective-permute-start(f32[8,4096]{1,0:T(8,128)S(1)} %bitcast.14), channel_id=1, source_target_pairs={{0,96},{1,97},{2,98},{3,99},{4,100},{5,101},{6,102},{7,103},{8,0},... | collective-permute-start | bytes 393224 | tf_op jit(solution)/shard_map/ppermute | solution.py:331
  21.5 11.9 %collective-permute-start.2 = (f32[8,4096]{1,0:T(8,128)S(1)}, f32[8,4096]{1,0:T(8,128)S(1)}, u32[]{:S(2)}, u32[]{:S(2)}) collective-permute-start(f32[8,4096]{1,0:T(8,128)S(1)} %bitcast.15), channel_id=1, source_target_pairs={{0,64},{1,65},{2,66},{3,67},{4,68},{5,69},{6,70},{7,71},{8,96},{9,... | collective-permute-start | bytes 393224 | tf_op jit(solution)/shard_map/ppermute | solution.py:331
  23.7 14.4 %collective-permute-start.3 = (f32[8,4096]{1,0:T(8,128)S(1)}, f32[8,4096]{1,0:T(8,128)S(1)}, u32[]{:S(2)}, u32[]{:S(2)}) collective-permute-start(f32[8,4096]{1,0:T(8,128)S(1)} %bitcast.16), channel_id=1, source_target_pairs={{0,32},{1,33},{2,34},{3,35},{4,36},{5,37},{6,38},{7,39},{8,64},{9,... | collective-permute-start | bytes 393224 | tf_op jit(solution)/shard_map/ppermute | solution.py:331
  26.3 0.7 %copy-start = (s32[32,2]{0,1:T(2,128)S(1)}, s32[32,2]{0,1:T(2,128)}, u32[]{:S(2)}) copy-start(s32[32,2]{0,1:T(2,128)} %param.5) | copy-start | bytes 772
  41.6 3.8 %collective-permute-start.4 = (f32[408,128]{1,0:T(8,128)S(1)}, f32[408,128]{1,0:T(8,128)S(1)}, u32[]{:S(2)}, u32[]{:S(2)}) collective-permute-start(f32[408,128]{1,0:T(8,128)S(1)} %get-tuple-element.12), channel_id=1, source_target_pairs={{0,1},{1,0},{2,3},{3,2},{4,5},{5,4},{6,7},{7,6},{8,9},{9,8},{10,11... | collective-permute-start | bytes 626696 | tf_op jit(solution)/shard_map/ppermute | solution.py:304
  41.7 8.6 %collective-permute-start.5 = (f32[408,128]{1,0:T(8,128)S(1)}, f32[408,128]{1,0:T(8,128)S(1)}, u32[]{:S(2)}, u32[]{:S(2)}) collective-permute-start(f32[408,128]{1,0:T(8,128)S(1)} %get-tuple-element.13), channel_id=1, source_target_pairs={{1,2},{3,4},{5,6},{7,8},{9,10},{11,12},{13,14},{15,16},{17,18},{19... | collective-permute-start | bytes 626696 | tf_op jit(solution)/shard_map/ppermute | solution.py:305

commit v5 on v4

--- a/solution.py
+++ b/solution.py
@@ -109,17 +109,18 @@
     yield 17, jnp.where(needed(17), block(16), 0.0)
 
 
-def inner_kernel(place_ref, ranges_ref, arrived_ref, v0, v1, v2, v3,
+def inner_kernel(ranges_ref, arrived_ref, v0, v1, v2, v3,
                  out_ref, pair_ref, other_ref, high_ref, low_ref, x_ref, v_ref):
     for k, piece in enumerate((v0, v1, v2, v3)):
-        first = pl.multiple_of(((place_ref[1] + k) & 3) * 8, 8)
+        first = pl.multiple_of(((lax.axis_index("col") + k) & 3) * 8, 8)
         v_ref[pl.ds(first, 8), :] = piece[...]
     bounds = sweep_bounds(ranges_ref)
     row = lax.broadcasted_iota(jnp.int32, (SWEEPS, NB), 0)
     lane = lax.broadcasted_iota(jnp.int32, (SWEEPS, NB), 1)
     upper = row <= (lane & 31)
     heads = (lane & 32) == 0
-    base = place_ref[0] * OWN
+    place = lax.axis_index("row")
+    base = place * OWN
     out_ref[pl.ds(0, ROWS)] = jnp.zeros((ROWS, NB), F32)
     for a in range(OWN):
         cols = pl.ds(a * NB, NB)
@@ -145,7 +146,7 @@
     def to_last(message):
         pack(out_ref, lambda k: k - 1, message)
 
-    odd = place_ref[0] & 1
+    odd = place & 1
 
     @pl.when(odd == 0)
     def _():
@@ -158,8 +159,11 @@
         to_next(other_ref)
 
 
-def apply_kernel(place_ref, phase_ref, own_ref, pair_ref, other_ref, x_ref, high_ref, low_ref,
-                 out_ref, result, sems, gather, coef, coef_half, inner, inner_half, rows_t, *shifted):
+def apply_kernel(phase_ref, own_ref, pair_ref, other_ref, x_ref, high_ref, low_ref,
+                 out_ref, result, sems, phase, phase_sem, gather, coef, coef_half, inner, inner_half, rows_t, *shifted):
+    copy_phase = pltpu.make_async_copy(phase_ref, phase, phase_sem)
+    copy_phase.start()
+
     def at(place, count=1):
         return pl.ds(place * ROWS, count * ROWS)
 
@@ -179,15 +183,16 @@
             else:
                 gather[at(HALO + OWN - 2 + k)] = block
 
-    odd = place_ref[0] & 1
+    place = lax.axis_index("row")
+    odd = place & 1
 
     @pl.when(odd == 0)
     def _():
-        take(unpack(other_ref, place_ref[0] > 0), unpack(pair_ref))
+        take(unpack(other_ref, place > 0), unpack(pair_ref))
 
     @pl.when(odd == 1)
     def _():
-        take(unpack(pair_ref), unpack(other_ref, place_ref[0] < place_ref[2] - 1))
+        take(unpack(pair_ref), unpack(other_ref, place < lax.axis_size("row") - 1))
 
     for q in range(8):
         block = gather[pl.ds(16 + q, NB, stride=ROWS), :].T
@@ -211,7 +216,8 @@
         for g in range(2):
             inner_half[pl.ds(g * 16 + q, 16, stride=32), :] = halves(parts[g][:16], parts[g + 2][:16])
 
-    phases = [phase_ref[j] for j in range(SWEEPS)]
+    copy_phase.wait()
+    phases = [phase[j] for j in range(SWEEPS)]
     wide, half = shifted[:SWEEPS - WIDE], shifted[SWEEPS - WIDE:]
     lane = lax.broadcasted_iota(jnp.int32, (EIG // 2, NB), 1) & 63
 
@@ -274,8 +280,8 @@
 
 def call(kernel, name, out_shape, scratch, operands, space=pltpu.VMEM):
     vmem = pl.BlockSpec(memory_space=pltpu.VMEM)
-    smem = pl.BlockSpec(memory_space=pltpu.SMEM)
-    specs = [smem if x.ndim == 1 else vmem for x in operands]
+    any_space = pl.BlockSpec(memory_space=pl.ANY)
+    specs = [any_space if x.ndim == 1 else vmem for x in operands]
     return pl.pallas_call(
         kernel,
         out_shape=tuple(jax.ShapeDtypeStruct(*x) for x in out_shape),
@@ -289,14 +295,13 @@
 
 def back_transform(x, pieces, sweep_ranges):
     count = lax.axis_size("row")
-    place = jnp.stack([lax.axis_index("row"), lax.axis_index("col"), count]).astype(jnp.int32)
     phase = sweep_ranges[:, 0] % NB
     message = ((17 * ROWS, NB), F32)
     own, to_pair, to_other, high, low, x = call(
         inner_kernel, "inner_products",
         [(((OWN + 1) * ROWS, NB), F32), message, message, ((OWN * 64, NB), BF16), ((OWN * 64, NB), BF16), ((EIG, OWN * NB), F32)],
         [(SWEEPS, OWN * NB)],
-        [place, sweep_ranges, x, *pieces],
+        [sweep_ranges, x, *pieces],
     )
     within = [(i, i ^ 1) for i in range(count)]
     across = [(i, (i + 1) % count) for i in range(1, count, 2)]
@@ -306,9 +311,10 @@
     out, = call(
         apply_kernel, "apply_sweeps",
         [((EIG, OWN * NB), F32)],
-        [(EIG, OWN * NB), pltpu.SemaphoreType.DMA((OWN // PART,)), (NB * ROWS, NB), (SWEEPS * 32, NB), (SWEEPS * 32, NB), (SWEEPS * EIG, NB), (SWEEPS * 32, NB), (40 * 16, NB)]
+        [(EIG, OWN * NB), pltpu.SemaphoreType.DMA((OWN // PART,)),
+         pltpu.SMEM((SWEEPS,), jnp.int32), pltpu.SemaphoreType.DMA, (NB * ROWS, NB), (SWEEPS * 32, NB), (SWEEPS * 32, NB), (SWEEPS * EIG, NB), (SWEEPS * 32, NB), (40 * 16, NB)]
         + [(2 * EIG, NB)] * (SWEEPS - WIDE) + [(EIG, NB)] * SWEEPS,
-        [place, phase, own, pair, other, x, high, low],
+        [phase, own, pair, other, x, high, low],
         pl.ANY,
     )
     return out

time: 56.7 us -> 55.8 us (0.984)
  Pallas kernels: 8.54 us -> 7.66 us
  local copies, waits for them, and re-layouts: 0.85 us -> 0.17 us
  waiting for transfers between devices: 16.9 us -> 17.5 us
    pallas_call x2, Pallas kernels: 8.54 us -> 7.66 us  [call(): pl.pallas_call(kernel, out_shape=tuple((jax.ShapeDtypeStruct(*x) for x in...]
    ppermute x4, waiting for transfers between devices: 10.9 us -> 11.6 us  [sweep_pieces(): pieces.append(lax.ppermute(mine, ('col', 'row'), pairs))]
    unnamed x4, local copies, waits for them, and re-layouts: 0.85 us -> 0.17 us
where the time goes in v5:
time: 55.8 us; the launch traced here: 55.5 us
  starting transfers between devices  19.6 us (35%)
  waiting for transfers between devices  17.5 us (31%)
  blocking collectives  10.4 us (19%)
  Pallas kernels  7.66 us (14%)
    ppermute x4, waiting for transfers between devices, sweep_pieces(): pieces.append(lax.ppermute(mine, ('col', 'row'), pairs))  11.6 us
    all_to_all x1, blocking collectives, sweep_pieces(): lax.all_to_all(reflectors.reshape(width, -1), 'row', split_axis=0, concat...  10.4 us
    ppermute x4, starting transfers between devices, sweep_pieces(): pieces.append(lax.ppermute(mine, ('col', 'row'), pairs))  9.48 us
    pallas_call x2, Pallas kernels, call(): pl.pallas_call(kernel, out_shape=tuple((jax.ShapeDtypeStruct(*x) for x in...  7.66 us
    all_to_all x1, starting transfers between devices, per_device(): lax.all_to_all(eigenvectors.reshape(2, -1, OWN * NB), 'row', split_axis=1...  6.31 us
    ppermute x1, waiting for transfers between devices, back_transform(): other = lax.ppermute(to_other, 'row', across)  4.85 us
    ppermute x1, starting transfers between devices, back_transform(): other = lax.ppermute(to_other, 'row', across)  3.76 us
  transfers between devices with their start and end apart: 7, of which 5 were waited for; matrix products, arithmetic and copies ran while one was open for 0% of the time, Pallas kernels for 0%

profile of v5, /device:TPU:24, one launch (start us, length us, event | category | flops | bytes accessed | tf_op | source)
XLA Modules:
  0.0 55.5 jit_solution(14188492561615713045)
XLA Ops:
  0.0 10.4 %all_to_all.17 = f32[8,1,4096]{2,1,0:T(1,128)S(1)} all-to-all(f32[8,1,4096]{2,1,0:T(1,128)} %bitcast.10), channel_id=1, replica_groups={{0,1,2,3,4,5,6,7},{8,9,10,11,12,13,14,15},{16,17,18,19,20,21,22,23},{24..., dimensions={0} | all-to-all | bytes 262144 | tf_op jit(solution)/shard_map/all_to_all | solution.py:327
  10.4 6.3 %all-to-all-start = ((f32[2,32,4096]{2,0,1:T(2,128)}), f32[2,32,4096]{2,0,1:T(2,128)S(1)}, u32[]{:S(2)}, u32[]{:S(2)}) async-start(f32[2,32,4096]{2,0,1:T(2,128)} %bitcast.9), calls=%async_computation | async-start | bytes 2097152 | tf_op jit(solution)/shard_map/all_to_all | solution.py:343
  16.7 0.1 copy.8
  16.8 0.0 copy-start
  16.8 4.6 %collective-permute-start = (f32[8,4096]{1,0:T(8,128)S(1)}, f32[8,4096]{1,0:T(8,128)S(1)}, u32[]{:S(2)}, u32[]{:S(2)}) collective-permute-start(f32[8,4096]{1,0:T(8,128)S(1)} %bitcast.11), channel_id=1, source_target_pairs={{0,0},{1,1},{2,2},{3,3},{4,4},{5,5},{6,6},{7,7},{8,32},{9,33},{10,... | collective-permute-start | bytes 393224 | tf_op jit(solution)/shard_map/ppermute | solution.py:337
  21.5 0.1 collective-permute-start.1
  21.5 2.1 %collective-permute-start.2 = (f32[8,4096]{1,0:T(8,128)S(1)}, f32[8,4096]{1,0:T(8,128)S(1)}, u32[]{:S(2)}, u32[]{:S(2)}) collective-permute-start(f32[8,4096]{1,0:T(8,128)S(1)} %bitcast.13), channel_id=1, source_target_pairs={{0,64},{1,65},{2,66},{3,67},{4,68},{5,69},{6,70},{7,71},{8,96},{9,... | collective-permute-start | bytes 393224 | tf_op jit(solution)/shard_map/ppermute | solution.py:337
  23.7 2.7 %collective-permute-start.3 = (f32[8,4096]{1,0:T(8,128)S(1)}, f32[8,4096]{1,0:T(8,128)S(1)}, u32[]{:S(2)}, u32[]{:S(2)}) collective-permute-start(f32[8,4096]{1,0:T(8,128)S(1)} %bitcast.14), channel_id=1, source_target_pairs={{0,32},{1,33},{2,34},{3,35},{4,36},{5,37},{6,38},{7,39},{8,64},{9,... | collective-permute-start | bytes 393224 | tf_op jit(solution)/shard_map/ppermute | solution.py:337
  26.3 0.0 copy-done
  26.3 0.1 copy.5.ranges_ref
  26.4 5.9 %collective-permute-done.v0 = f32[8,4096]{1,0:T(8,128)S(1)} collective-permute-done((f32[8,4096]{1,0:T(8,128)S(1)}, f32[8,4096]{1,0:T(8,128)S(1)}, u32[]{:S(2)}, u32[]{:S(2)}) %collective-permute-start) | collective-permute-done | bytes 131104 | tf_op jit(solution)/shard_map/ppermute | solution.py:337
  32.3 0.0 collective-permute-done.1.v1
  32.3 1.2 %collective-permute-done.2.v2 = f32[8,4096]{1,0:T(8,128)S(1)} collective-permute-done((f32[8,4096]{1,0:T(8,128)S(1)}, f32[8,4096]{1,0:T(8,128)S(1)}, u32[]{:S(2)}, u32[]{:S(2)}) %collective-permute-start.2) | collective-permute-done | bytes 131104 | tf_op jit(solution)/shard_map/ppermute | solution.py:337
  33.5 4.6 %collective-permute-done.3.v3 = f32[8,4096]{1,0:T(8,128)S(1)} collective-permute-done((f32[8,4096]{1,0:T(8,128)S(1)}, f32[8,4096]{1,0:T(8,128)S(1)}, u32[]{:S(2)}, u32[]{:S(2)}) %collective-permute-start.3) | collective-permute-done | bytes 131104 | tf_op jit(solution)/shard_map/ppermute | solution.py:337
  38.0 1.1 %all-to-all-done = f32[2,32,4096]{2,0,1:T(2,128)S(1)} async-done(((f32[2,32,4096]{2,0,1:T(2,128)}), f32[2,32,4096]{2,0,1:T(2,128)S(1)}, u32[]{:S(2)}, u32[]{:S(2)}) %all-to-all-start) | async-done | bytes 1048608 | tf_op jit(solution)/shard_map/all_to_all | solution.py:343
  39.1 1.9 %inner_products.1 = (f32[792,128]{1,0:T(8,128)S(1)}, f32[408,128]{1,0:T(8,128)S(1)}, f32[408,128]{1,0:T(8,128)S(1)}, bf16[2048,128]{1,0:T(8,128)(2,1)S(1)}, bf16...) custom-call(s32[32,2]{1,0:T(8,128)S(1)} %copy.5.ranges_ref, f32[32,2,4096]{2,1,0:T(2,128)S(1)} %bitcast.8, ...), custom_call_target="tpu_custom_call" | custom-call | tf_op jit(solution)/shard_map/inner_products/pallas_call | solution.py:285
  41.0 0.1 collective-permute-start.4
  41.1 3.8 %collective-permute-start.5 = (f32[408,128]{1,0:T(8,128)S(1)}, f32[408,128]{1,0:T(8,128)S(1)}, u32[]{:S(2)}, u32[]{:S(2)}) collective-permute-start(f32[408,128]{1,0:T(8,128)S(1)} %get-tuple-element.13), channel_id=1, source_target_pairs={{1,2},{3,4},{5,6},{7,8},{9,10},{11,12},{13,14},{15,16},{17,18},{19... | collective-permute-start | bytes 626696 | tf_op jit(solution)/shard_map/ppermute | solution.py:310
  44.9 0.0 collective-permute-done.4.pair_ref
  44.9 4.9 %collective-permute-done.5.other_ref = f32[408,128]{1,0:T(8,128)S(1)} collective-permute-done((f32[408,128]{1,0:T(8,128)S(1)}, f32[408,128]{1,0:T(8,128)S(1)}, u32[]{:S(2)}, u32[]{:S(2)}) %collective-permute-start.5) | collective-permute-done | bytes 208928 | tf_op jit(solution)/shard_map/ppermute | solution.py:310
  49.8 5.8 %apply_sweeps.1 = f32[64,4096]{1,0:T(8,128)} custom-call(s32[32]{0:T(128)S(1)} %and_select_fusion.phase_ref, f32[792,128]{1,0:T(8,128)S(1)} %get-tuple-element.11.own_ref, f32[408,128]{1,0:T(8,128)S(1)} %collective-permute-done.4.pair_ref, f32[408,128]{1,0:T(8,128)S(1)} %collective-permute-done.5.other_ref, f32[64,4096]{1,0:T(8,128)S(1)} %get-tuple-element.14.x_ref, ...), custom_call_target="tpu_custom_call" | custom-call | tf_op jit(solution)/shard_map/apply_sweeps/pallas_call | solution.py:285
  (1 shorter events, 0.0 us)
Async XLA Ops:
  10.4 28.7 %all-to-all-start = ((f32[2,32,4096]{2,0,1:T(2,128)}), f32[2,32,4096]{2,0,1:T(2,128)S(1)}, u32[]{:S(2)}, u32[]{:S(2)}) async-start(f32[2,32,4096]{2,0,1:T(2,128)} %bitcast.9), calls=%async_computation | async-start | bytes 2097152 | tf_op jit(solution)/shard_map/all_to_all | solution.py:343
  16.8 9.5 %copy-start = (s32[32,2]{0,1:T(2,128)S(1)}, s32[32,2]{0,1:T(2,128)}, u32[]{:S(2)}) copy-start(s32[32,2]{0,1:T(2,128)} %param.5) | copy-start | bytes 772
  16.8 15.4 %collective-permute-start = (f32[8,4096]{1,0:T(8,128)S(1)}, f32[8,4096]{1,0:T(8,128)S(1)}, u32[]{:S(2)}, u32[]{:S(2)}) collective-permute-start(f32[8,4096]{1,0:T(8,128)S(1)} %bitcast.11), channel_id=1, source_target_pairs={{0,0},{1,1},{2,2},{3,3},{4,4},{5,5},{6,6},{7,7},{8,32},{9,33},{10,... | collective-permute-start | bytes 393224 | tf_op jit(solution)/shard_map/ppermute | solution.py:337
  21.5 10.8 %collective-permute-start.1 = (f32[8,4096]{1,0:T(8,128)S(1)}, f32[8,4096]{1,0:T(8,128)S(1)}, u32[]{:S(2)}, u32[]{:S(2)}) collective-permute-start(f32[8,4096]{1,0:T(8,128)S(1)} %bitcast.12), channel_id=1, source_target_pairs={{0,96},{1,97},{2,98},{3,99},{4,100},{5,101},{6,102},{7,103},{8,0},... | collective-permute-start | bytes 393224 | tf_op jit(solution)/shard_map/ppermute | solution.py:337
  21.5 11.9 %collective-permute-start.2 = (f32[8,4096]{1,0:T(8,128)S(1)}, f32[8,4096]{1,0:T(8,128)S(1)}, u32[]{:S(2)}, u32[]{:S(2)}) collective-permute-start(f32[8,4096]{1,0:T(8,128)S(1)} %bitcast.13), channel_id=1, source_target_pairs={{0,64},{1,65},{2,66},{3,67},{4,68},{5,69},{6,70},{7,71},{8,96},{9,... | collective-permute-start | bytes 393224 | tf_op jit(solution)/shard_map/ppermute | solution.py:337
  23.7 14.4 %collective-permute-start.3 = (f32[8,4096]{1,0:T(8,128)S(1)}, f32[8,4096]{1,0:T(8,128)S(1)}, u32[]{:S(2)}, u32[]{:S(2)}) collective-permute-start(f32[8,4096]{1,0:T(8,128)S(1)} %bitcast.14), channel_id=1, source_target_pairs={{0,32},{1,33},{2,34},{3,35},{4,36},{5,37},{6,38},{7,39},{8,64},{9,... | collective-permute-start | bytes 393224 | tf_op jit(solution)/shard_map/ppermute | solution.py:337
  41.0 3.9 %collective-permute-start.4 = (f32[408,128]{1,0:T(8,128)S(1)}, f32[408,128]{1,0:T(8,128)S(1)}, u32[]{:S(2)}, u32[]{:S(2)}) collective-permute-start(f32[408,128]{1,0:T(8,128)S(1)} %get-tuple-element.12), channel_id=1, source_target_pairs={{0,1},{1,0},{2,3},{3,2},{4,5},{5,4},{6,7},{7,6},{8,9},{9,8},{10,11... | collective-permute-start | bytes 626696 | tf_op jit(solution)/shard_map/ppermute | solution.py:309
  41.1 8.6 %collective-permute-start.5 = (f32[408,128]{1,0:T(8,128)S(1)}, f32[408,128]{1,0:T(8,128)S(1)}, u32[]{:S(2)}, u32[]{:S(2)}) collective-permute-start(f32[408,128]{1,0:T(8,128)S(1)} %get-tuple-element.13), channel_id=1, source_target_pairs={{1,2},{3,4},{5,6},{7,8},{9,10},{11,12},{13,14},{15,16},{17,18},{19... | collective-permute-start | bytes 626696 | tf_op jit(solution)/shard_map/ppermute | solution.py:310

commit v6 on v5

--- a/solution.py
+++ b/solution.py
@@ -10,7 +10,7 @@
 OWN = 32
 EIG = 64
 HALO = 32
-PART = 8
+ENDS = (10, 18, 24, 28, 31, 32)
 WIDE = 16
 ROWS = 24
 F32 = jnp.float32
@@ -62,11 +62,11 @@
     return keep(x, turned), keep(turned, x)
 
 
-def inner_products(x, right_high, right_low):
+def inner_products(x, both):
     left = jnp.concatenate(split(x), axis=1)
-    right = jnp.concatenate([right_high] * 2 + [right_low] * 2, axis=0)
-    right = jnp.concatenate([right, right], axis=1)
-    prod = lax.dot_general(left, right, (((1,), (1,)), ((), ())), preferred_element_type=F32)
+    right = jnp.concatenate(split(jnp.concatenate([both, both], axis=0).T), axis=1)
+    right = jnp.concatenate([right, right], axis=0)
+    prod = lax.dot_general(left, right, (((1,), (0,)), ((), ())), preferred_element_type=F32)
     return prod[:, :NB] + prod[:, NB:]
 
 
@@ -125,12 +125,13 @@
     for a in range(OWN):
         cols = pl.ds(a * NB, NB)
         head, tail = heads_tails(v_ref[:, cols], bounds, base + a)
-        high, low = split(jnp.concatenate([head, tail], axis=0))
+        both = jnp.concatenate([head, tail], axis=0)
+        high, low = split(both)
         high_ref[pl.ds(a * 64, 64)] = high
         low_ref[pl.ds(a * 64, 64)] = low
         x = arrived_ref[:, :, cols].reshape(EIG, NB)
         x_ref[:, cols] = x
-        inner = inner_products(jnp.concatenate([x, head, tail], axis=0), high, low)
+        inner = inner_products(jnp.concatenate([x, both], axis=0), both)
         of_head, of_tail = inner[64:96], inner[96:128]
         gram = jnp.where(upper == heads, of_head, of_tail)
         inner_head, inner_tail = fold(inner[:64], 16)
@@ -258,7 +259,8 @@
             rows_t[pl.ds(h * 8 + t, 40, stride=16), :] = block[h * 64 + 8:h * 64 + 48]
 
     def copy_out(c):
-        part = pl.ds(c * PART * NB, PART * NB)
+        first = 0 if c == 0 else ENDS[c - 1]
+        part = pl.ds(first * NB, (ENDS[c] - first) * NB)
         return pltpu.make_async_copy(result.at[:, part], out_ref.at[:, part], sems.at[c])
 
     group = lane_group(8)
@@ -272,9 +274,9 @@
                   for y in (of_head, of_tail)]
         update = outer_products(jnp.concatenate(spread, axis=1), high_ref[rows], low_ref[rows])
         result[:, cols] = x_ref[:, cols] - update
-        if (a + 1) % PART == 0:
-            copy_out(a // PART).start()
-    for c in range(OWN // PART):
+        if a + 1 in ENDS:
+            copy_out(ENDS.index(a + 1)).start()
+    for c in range(len(ENDS)):
         copy_out(c).wait()
 
 
@@ -311,7 +313,7 @@
     out, = call(
         apply_kernel, "apply_sweeps",
         [((EIG, OWN * NB), F32)],
-        [(EIG, OWN * NB), pltpu.SemaphoreType.DMA((OWN // PART,)),
+        [(EIG, OWN * NB), pltpu.SemaphoreType.DMA((len(ENDS),)),
          pltpu.SMEM((SWEEPS,), jnp.int32), pltpu.SemaphoreType.DMA, (NB * ROWS, NB), (SWEEPS * 32, NB), (SWEEPS * 32, NB), (SWEEPS * EIG, NB), (SWEEPS * 32, NB), (40 * 16, NB)]
         + [(2 * EIG, NB)] * (SWEEPS - WIDE) + [(EIG, NB)] * SWEEPS,
         [phase, own, pair, other, x, high, low],

time: 55.8 us -> 55.6 us (level)
  no operation moved by 1% of the time
where the time goes in v6:
time: 55.6 us; the launch traced here: 55.3 us
  starting transfers between devices  19.6 us (35%)
  waiting for transfers between devices  17.6 us (32%)
  blocking collectives  10.4 us (19%)
  Pallas kernels  7.46 us (13%)
    ppermute x4, waiting for transfers between devices, sweep_pieces(): pieces.append(lax.ppermute(mine, ('col', 'row'), pairs))  11.6 us
    all_to_all x1, blocking collectives, sweep_pieces(): lax.all_to_all(reflectors.reshape(width, -1), 'row', split_axis=0, concat...  10.4 us
    ppermute x4, starting transfers between devices, sweep_pieces(): pieces.append(lax.ppermute(mine, ('col', 'row'), pairs))  9.48 us
    pallas_call x2, Pallas kernels, call(): pl.pallas_call(kernel, out_shape=tuple((jax.ShapeDtypeStruct(*x) for x in...  7.46 us
    all_to_all x1, starting transfers between devices, per_device(): lax.all_to_all(eigenvectors.reshape(2, -1, OWN * NB), 'row', split_axis=1...  6.31 us
    ppermute x1, waiting for transfers between devices, back_transform(): other = lax.ppermute(to_other, 'row', across)  4.86 us
    ppermute x1, starting transfers between devices, back_transform(): other = lax.ppermute(to_other, 'row', across)  3.76 us
  transfers between devices with their start and end apart: 7, of which 5 were waited for; matrix products, arithmetic and copies ran while one was open for 0% of the time, Pallas kernels for 0%

profile of v6, /device:TPU:24, one launch (start us, length us, event | category | flops | bytes accessed | tf_op | source)
XLA Modules:
  0.0 55.3 jit_solution(4855623434538074026)
XLA Ops:
  0.0 10.4 %all_to_all.17 = f32[8,1,4096]{2,1,0:T(1,128)S(1)} all-to-all(f32[8,1,4096]{2,1,0:T(1,128)} %bitcast.10), channel_id=1, replica_groups={{0,1,2,3,4,5,6,7},{8,9,10,11,12,13,14,15},{16,17,18,19,20,21,22,23},{24..., dimensions={0} | all-to-all | bytes 262144 | tf_op jit(solution)/shard_map/all_to_all | solution.py:329
  10.4 6.3 %all-to-all-start = ((f32[2,32,4096]{2,0,1:T(2,128)}), f32[2,32,4096]{2,0,1:T(2,128)S(1)}, u32[]{:S(2)}, u32[]{:S(2)}) async-start(f32[2,32,4096]{2,0,1:T(2,128)} %bitcast.9), calls=%async_computation | async-start | bytes 2097152 | tf_op jit(solution)/shard_map/all_to_all | solution.py:345
  16.7 0.1 copy.8
  16.8 0.0 copy-start
  16.8 4.6 %collective-permute-start = (f32[8,4096]{1,0:T(8,128)S(1)}, f32[8,4096]{1,0:T(8,128)S(1)}, u32[]{:S(2)}, u32[]{:S(2)}) collective-permute-start(f32[8,4096]{1,0:T(8,128)S(1)} %bitcast.11), channel_id=1, source_target_pairs={{0,0},{1,1},{2,2},{3,3},{4,4},{5,5},{6,6},{7,7},{8,32},{9,33},{10,... | collective-permute-start | bytes 393224 | tf_op jit(solution)/shard_map/ppermute | solution.py:339
  21.5 0.1 collective-permute-start.1
  21.5 2.1 %collective-permute-start.2 = (f32[8,4096]{1,0:T(8,128)S(1)}, f32[8,4096]{1,0:T(8,128)S(1)}, u32[]{:S(2)}, u32[]{:S(2)}) collective-permute-start(f32[8,4096]{1,0:T(8,128)S(1)} %bitcast.13), channel_id=1, source_target_pairs={{0,64},{1,65},{2,66},{3,67},{4,68},{5,69},{6,70},{7,71},{8,96},{9,... | collective-permute-start | bytes 393224 | tf_op jit(solution)/shard_map/ppermute | solution.py:339
  23.7 2.7 %collective-permute-start.3 = (f32[8,4096]{1,0:T(8,128)S(1)}, f32[8,4096]{1,0:T(8,128)S(1)}, u32[]{:S(2)}, u32[]{:S(2)}) collective-permute-start(f32[8,4096]{1,0:T(8,128)S(1)} %bitcast.14), channel_id=1, source_target_pairs={{0,32},{1,33},{2,34},{3,35},{4,36},{5,37},{6,38},{7,39},{8,64},{9,... | collective-permute-start | bytes 393224 | tf_op jit(solution)/shard_map/ppermute | solution.py:339
  26.3 0.0 copy-done
  26.3 0.1 copy.5.ranges_ref
  26.4 5.9 %collective-permute-done.v0 = f32[8,4096]{1,0:T(8,128)S(1)} collective-permute-done((f32[8,4096]{1,0:T(8,128)S(1)}, f32[8,4096]{1,0:T(8,128)S(1)}, u32[]{:S(2)}, u32[]{:S(2)}) %collective-permute-start) | collective-permute-done | bytes 131104 | tf_op jit(solution)/shard_map/ppermute | solution.py:339
  32.3 0.0 collective-permute-done.1.v1
  32.3 1.2 %collective-permute-done.2.v2 = f32[8,4096]{1,0:T(8,128)S(1)} collective-permute-done((f32[8,4096]{1,0:T(8,128)S(1)}, f32[8,4096]{1,0:T(8,128)S(1)}, u32[]{:S(2)}, u32[]{:S(2)}) %collective-permute-start.2) | collective-permute-done | bytes 131104 | tf_op jit(solution)/shard_map/ppermute | solution.py:339
  33.5 4.6 %collective-permute-done.3.v3 = f32[8,4096]{1,0:T(8,128)S(1)} collective-permute-done((f32[8,4096]{1,0:T(8,128)S(1)}, f32[8,4096]{1,0:T(8,128)S(1)}, u32[]{:S(2)}, u32[]{:S(2)}) %collective-permute-start.3) | collective-permute-done | bytes 131104 | tf_op jit(solution)/shard_map/ppermute | solution.py:339
  38.0 1.1 %all-to-all-done = f32[2,32,4096]{2,0,1:T(2,128)S(1)} async-done(((f32[2,32,4096]{2,0,1:T(2,128)}), f32[2,32,4096]{2,0,1:T(2,128)S(1)}, u32[]{:S(2)}, u32[]{:S(2)}) %all-to-all-start) | async-done | bytes 1048608 | tf_op jit(solution)/shard_map/all_to_all | solution.py:345
  39.1 1.8 %inner_products.1 = (f32[792,128]{1,0:T(8,128)S(1)}, f32[408,128]{1,0:T(8,128)S(1)}, f32[408,128]{1,0:T(8,128)S(1)}, bf16[2048,128]{1,0:T(8,128)(2,1)S(1)}, bf16...) custom-call(s32[32,2]{1,0:T(8,128)S(1)} %copy.5.ranges_ref, f32[32,2,4096]{2,1,0:T(2,128)S(1)} %bitcast.8, ...), custom_call_target="tpu_custom_call" | custom-call | tf_op jit(solution)/shard_map/inner_products/pallas_call | solution.py:287
  40.9 0.1 collective-permute-start.4
  41.0 3.8 %collective-permute-start.5 = (f32[408,128]{1,0:T(8,128)S(1)}, f32[408,128]{1,0:T(8,128)S(1)}, u32[]{:S(2)}, u32[]{:S(2)}) collective-permute-start(f32[408,128]{1,0:T(8,128)S(1)} %get-tuple-element.13), channel_id=1, source_target_pairs={{1,2},{3,4},{5,6},{7,8},{9,10},{11,12},{13,14},{15,16},{17,18},{19... | collective-permute-start | bytes 626696 | tf_op jit(solution)/shard_map/ppermute | solution.py:312
  44.7 0.0 collective-permute-done.4.pair_ref
  44.7 4.9 %collective-permute-done.5.other_ref = f32[408,128]{1,0:T(8,128)S(1)} collective-permute-done((f32[408,128]{1,0:T(8,128)S(1)}, f32[408,128]{1,0:T(8,128)S(1)}, u32[]{:S(2)}, u32[]{:S(2)}) %collective-permute-start.5) | collective-permute-done | bytes 208928 | tf_op jit(solution)/shard_map/ppermute | solution.py:312
  49.6 5.7 %apply_sweeps.1 = f32[64,4096]{1,0:T(8,128)} custom-call(s32[32]{0:T(128)S(1)} %and_select_fusion.phase_ref, f32[792,128]{1,0:T(8,128)S(1)} %get-tuple-element.11.own_ref, f32[408,128]{1,0:T(8,128)S(1)} %collective-permute-done.4.pair_ref, f32[408,128]{1,0:T(8,128)S(1)} %collective-permute-done.5.other_ref, f32[64,4096]{1,0:T(8,128)S(1)} %get-tuple-element.14.x_ref, ...), custom_call_target="tpu_custom_call" | custom-call | tf_op jit(solution)/shard_map/apply_sweeps/pallas_call | solution.py:287
  (1 shorter events, 0.0 us)
Async XLA Ops:
  10.4 28.7 %all-to-all-start = ((f32[2,32,4096]{2,0,1:T(2,128)}), f32[2,32,4096]{2,0,1:T(2,128)S(1)}, u32[]{:S(2)}, u32[]{:S(2)}) async-start(f32[2,32,4096]{2,0,1:T(2,128)} %bitcast.9), calls=%async_computation | async-start | bytes 2097152 | tf_op jit(solution)/shard_map/all_to_all | solution.py:345
  16.8 9.5 %copy-start = (s32[32,2]{0,1:T(2,128)S(1)}, s32[32,2]{0,1:T(2,128)}, u32[]{:S(2)}) copy-start(s32[32,2]{0,1:T(2,128)} %param.5) | copy-start | bytes 772
  16.8 15.4 %collective-permute-start = (f32[8,4096]{1,0:T(8,128)S(1)}, f32[8,4096]{1,0:T(8,128)S(1)}, u32[]{:S(2)}, u32[]{:S(2)}) collective-permute-start(f32[8,4096]{1,0:T(8,128)S(1)} %bitcast.11), channel_id=1, source_target_pairs={{0,0},{1,1},{2,2},{3,3},{4,4},{5,5},{6,6},{7,7},{8,32},{9,33},{10,... | collective-permute-start | bytes 393224 | tf_op jit(solution)/shard_map/ppermute | solution.py:339
  21.5 10.8 %collective-permute-start.1 = (f32[8,4096]{1,0:T(8,128)S(1)}, f32[8,4096]{1,0:T(8,128)S(1)}, u32[]{:S(2)}, u32[]{:S(2)}) collective-permute-start(f32[8,4096]{1,0:T(8,128)S(1)} %bitcast.12), channel_id=1, source_target_pairs={{0,96},{1,97},{2,98},{3,99},{4,100},{5,101},{6,102},{7,103},{8,0},... | collective-permute-start | bytes 393224 | tf_op jit(solution)/shard_map/ppermute | solution.py:339
  21.5 11.9 %collective-permute-start.2 = (f32[8,4096]{1,0:T(8,128)S(1)}, f32[8,4096]{1,0:T(8,128)S(1)}, u32[]{:S(2)}, u32[]{:S(2)}) collective-permute-start(f32[8,4096]{1,0:T(8,128)S(1)} %bitcast.13), channel_id=1, source_target_pairs={{0,64},{1,65},{2,66},{3,67},{4,68},{5,69},{6,70},{7,71},{8,96},{9,... | collective-permute-start | bytes 393224 | tf_op jit(solution)/shard_map/ppermute | solution.py:339
  23.7 14.4 %collective-permute-start.3 = (f32[8,4096]{1,0:T(8,128)S(1)}, f32[8,4096]{1,0:T(8,128)S(1)}, u32[]{:S(2)}, u32[]{:S(2)}) collective-permute-start(f32[8,4096]{1,0:T(8,128)S(1)} %bitcast.14), channel_id=1, source_target_pairs={{0,32},{1,33},{2,34},{3,35},{4,36},{5,37},{6,38},{7,39},{8,64},{9,... | collective-permute-start | bytes 393224 | tf_op jit(solution)/shard_map/ppermute | solution.py:339
  40.9 3.9 %collective-permute-start.4 = (f32[408,128]{1,0:T(8,128)S(1)}, f32[408,128]{1,0:T(8,128)S(1)}, u32[]{:S(2)}, u32[]{:S(2)}) collective-permute-start(f32[408,128]{1,0:T(8,128)S(1)} %get-tuple-element.12), channel_id=1, source_target_pairs={{0,1},{1,0},{2,3},{3,2},{4,5},{5,4},{6,7},{7,6},{8,9},{9,8},{10,11... | collective-permute-start | bytes 626696 | tf_op jit(solution)/shard_map/ppermute | solution.py:311
  41.0 8.6 %collective-permute-start.5 = (f32[408,128]{1,0:T(8,128)S(1)}, f32[408,128]{1,0:T(8,128)S(1)}, u32[]{:S(2)}, u32[]{:S(2)}) collective-permute-start(f32[408,128]{1,0:T(8,128)S(1)} %get-tuple-element.13), channel_id=1, source_target_pairs={{1,2},{3,4},{5,6},{7,8},{9,10},{11,12},{13,14},{15,16},{17,18},{19... | collective-permute-start | bytes 626696 | tf_op jit(solution)/shard_map/ppermute | solution.py:312

commit v7 on v6

--- a/solution.py
+++ b/solution.py
@@ -42,12 +42,9 @@
     return phase, first, last
 
 
-def heads_tails(rows, bounds, block):
-    phase, first, last = bounds
-    lane = lax.broadcasted_iota(jnp.int32, (SWEEPS, NB), 1)
-    head_on = (lane >= phase) & (block >= first) & (block <= last)
-    tail_on = (lane < phase) & (block - 1 >= first) & (block - 1 <= last)
-    return jnp.where(head_on, rows, 0.0), jnp.where(tail_on, rows, 0.0)
+def active(bounds, block):
+    _, first, last = bounds
+    return (block >= first) & (block <= last)
 
 
 def fold(x, rows):
@@ -121,10 +118,16 @@
     heads = (lane & 32) == 0
     place = lax.axis_index("row")
     base = place * OWN
+    head_lane, tail_lane = lane >= bounds[0], lane < bounds[0]
+    before = active(bounds, base - 1)
     out_ref[pl.ds(0, ROWS)] = jnp.zeros((ROWS, NB), F32)
     for a in range(OWN):
         cols = pl.ds(a * NB, NB)
-        head, tail = heads_tails(v_ref[:, cols], bounds, base + a)
+        here = active(bounds, base + a)
+        rows = v_ref[:, cols]
+        head = jnp.where(head_lane & here, rows, 0.0)
+        tail = jnp.where(tail_lane & before, rows, 0.0)
+        before = here
         both = jnp.concatenate([head, tail], axis=0)
         high, low = split(both)
         high_ref[pl.ds(a * 64, 64)] = high

time: 55.6 us -> 55.6 us (level)
  no operation moved by 1% of the time
where the time goes in v7:
time: 55.6 us; the launch traced here: 55.3 us
  starting transfers between devices  19.6 us (35%)
  waiting for transfers between devices  17.5 us (31%)
  blocking collectives  10.4 us (19%)
  Pallas kernels  7.41 us (13%)
    ppermute x4, waiting for transfers between devices, sweep_pieces(): pieces.append(lax.ppermute(mine, ('col', 'row'), pairs))  11.6 us
    all_to_all x1, blocking collectives, sweep_pieces(): lax.all_to_all(reflectors.reshape(width, -1), 'row', split_axis=0, concat...  10.4 us
    ppermute x4, starting transfers between devices, sweep_pieces(): pieces.append(lax.ppermute(mine, ('col', 'row'), pairs))  9.48 us
    pallas_call x2, Pallas kernels, call(): pl.pallas_call(kernel, out_shape=tuple((jax.ShapeDtypeStruct(*x) for x in...  7.41 us
    all_to_all x1, starting transfers between devices, per_device(): lax.all_to_all(eigenvectors.reshape(2, -1, OWN * NB), 'row', split_axis=1...  6.31 us
    ppermute x1, waiting for transfers between devices, back_transform(): other = lax.ppermute(to_other, 'row', across)  4.86 us
    ppermute x1, starting transfers between devices, back_transform(): other = lax.ppermute(to_other, 'row', across)  3.76 us
  transfers between devices with their start and end apart: 7, of which 5 were waited for; matrix products, arithmetic and copies ran while one was open for 0% of the time, Pallas kernels for 0%

profile of v7, /device:TPU:24, one launch (start us, length us, event | category | flops | bytes accessed | tf_op | source)
XLA Modules:
  0.0 55.3 jit_solution(18213503050305491442)
XLA Ops:
  0.0 10.4 %all_to_all.17 = f32[8,1,4096]{2,1,0:T(1,128)S(1)} all-to-all(f32[8,1,4096]{2,1,0:T(1,128)} %bitcast.10), channel_id=1, replica_groups={{0,1,2,3,4,5,6,7},{8,9,10,11,12,13,14,15},{16,17,18,19,20,21,22,23},{24..., dimensions={0} | all-to-all | bytes 262144 | tf_op jit(solution)/shard_map/all_to_all | solution.py:332
  10.4 6.3 %all-to-all-start = ((f32[2,32,4096]{2,0,1:T(2,128)}), f32[2,32,4096]{2,0,1:T(2,128)S(1)}, u32[]{:S(2)}, u32[]{:S(2)}) async-start(f32[2,32,4096]{2,0,1:T(2,128)} %bitcast.9), calls=%async_computation | async-start | bytes 2097152 | tf_op jit(solution)/shard_map/all_to_all | solution.py:348
  16.7 0.1 copy.8
  16.8 0.0 copy-start
  16.8 4.6 %collective-permute-start = (f32[8,4096]{1,0:T(8,128)S(1)}, f32[8,4096]{1,0:T(8,128)S(1)}, u32[]{:S(2)}, u32[]{:S(2)}) collective-permute-start(f32[8,4096]{1,0:T(8,128)S(1)} %bitcast.11), channel_id=1, source_target_pairs={{0,0},{1,1},{2,2},{3,3},{4,4},{5,5},{6,6},{7,7},{8,32},{9,33},{10,... | collective-permute-start | bytes 393224 | tf_op jit(solution)/shard_map/ppermute | solution.py:342
  21.5 0.1 collective-permute-start.1
  21.5 2.1 %collective-permute-start.2 = (f32[8,4096]{1,0:T(8,128)S(1)}, f32[8,4096]{1,0:T(8,128)S(1)}, u32[]{:S(2)}, u32[]{:S(2)}) collective-permute-start(f32[8,4096]{1,0:T(8,128)S(1)} %bitcast.13), channel_id=1, source_target_pairs={{0,64},{1,65},{2,66},{3,67},{4,68},{5,69},{6,70},{7,71},{8,96},{9,... | collective-permute-start | bytes 393224 | tf_op jit(solution)/shard_map/ppermute | solution.py:342
  23.7 2.7 %collective-permute-start.3 = (f32[8,4096]{1,0:T(8,128)S(1)}, f32[8,4096]{1,0:T(8,128)S(1)}, u32[]{:S(2)}, u32[]{:S(2)}) collective-permute-start(f32[8,4096]{1,0:T(8,128)S(1)} %bitcast.14), channel_id=1, source_target_pairs={{0,32},{1,33},{2,34},{3,35},{4,36},{5,37},{6,38},{7,39},{8,64},{9,... | collective-permute-start | bytes 393224 | tf_op jit(solution)/shard_map/ppermute | solution.py:342
  26.3 0.0 copy-done
  26.3 0.1 copy.5.ranges_ref
  26.4 5.9 %collective-permute-done.v0 = f32[8,4096]{1,0:T(8,128)S(1)} collective-permute-done((f32[8,4096]{1,0:T(8,128)S(1)}, f32[8,4096]{1,0:T(8,128)S(1)}, u32[]{:S(2)}, u32[]{:S(2)}) %collective-permute-start) | collective-permute-done | bytes 131104 | tf_op jit(solution)/shard_map/ppermute | solution.py:342
  32.3 0.0 collective-permute-done.1.v1
  32.3 1.2 %collective-permute-done.2.v2 = f32[8,4096]{1,0:T(8,128)S(1)} collective-permute-done((f32[8,4096]{1,0:T(8,128)S(1)}, f32[8,4096]{1,0:T(8,128)S(1)}, u32[]{:S(2)}, u32[]{:S(2)}) %collective-permute-start.2) | collective-permute-done | bytes 131104 | tf_op jit(solution)/shard_map/ppermute | solution.py:342
  33.5 4.6 %collective-permute-done.3.v3 = f32[8,4096]{1,0:T(8,128)S(1)} collective-permute-done((f32[8,4096]{1,0:T(8,128)S(1)}, f32[8,4096]{1,0:T(8,128)S(1)}, u32[]{:S(2)}, u32[]{:S(2)}) %collective-permute-start.3) | collective-permute-done | bytes 131104 | tf_op jit(solution)/shard_map/ppermute | solution.py:342
  38.0 1.1 %all-to-all-done = f32[2,32,4096]{2,0,1:T(2,128)S(1)} async-done(((f32[2,32,4096]{2,0,1:T(2,128)}), f32[2,32,4096]{2,0,1:T(2,128)S(1)}, u32[]{:S(2)}, u32[]{:S(2)}) %all-to-all-start) | async-done | bytes 1048608 | tf_op jit(solution)/shard_map/all_to_all | solution.py:348
  39.1 1.7 %inner_products.1 = (f32[792,128]{1,0:T(8,128)S(1)}, f32[408,128]{1,0:T(8,128)S(1)}, f32[408,128]{1,0:T(8,128)S(1)}, bf16[2048,128]{1,0:T(8,128)(2,1)S(1)}, bf16...) custom-call(s32[32,2]{1,0:T(8,128)S(1)} %copy.5.ranges_ref, f32[32,2,4096]{2,1,0:T(2,128)S(1)} %bitcast.8, ...), custom_call_target="tpu_custom_call" | custom-call | tf_op jit(solution)/shard_map/inner_products/pallas_call | solution.py:290
  40.8 0.1 collective-permute-start.4
  40.9 3.8 %collective-permute-start.5 = (f32[408,128]{1,0:T(8,128)S(1)}, f32[408,128]{1,0:T(8,128)S(1)}, u32[]{:S(2)}, u32[]{:S(2)}) collective-permute-start(f32[408,128]{1,0:T(8,128)S(1)} %get-tuple-element.13), channel_id=1, source_target_pairs={{1,2},{3,4},{5,6},{7,8},{9,10},{11,12},{13,14},{15,16},{17,18},{19... | collective-permute-start | bytes 626696 | tf_op jit(solution)/shard_map/ppermute | solution.py:315
  44.7 0.0 collective-permute-done.4.pair_ref
  44.7 4.9 %collective-permute-done.5.other_ref = f32[408,128]{1,0:T(8,128)S(1)} collective-permute-done((f32[408,128]{1,0:T(8,128)S(1)}, f32[408,128]{1,0:T(8,128)S(1)}, u32[]{:S(2)}, u32[]{:S(2)}) %collective-permute-start.5) | collective-permute-done | bytes 208928 | tf_op jit(solution)/shard_map/ppermute | solution.py:315
  49.6 5.7 %apply_sweeps.1 = f32[64,4096]{1,0:T(8,128)} custom-call(s32[32]{0:T(128)S(1)} %and_select_fusion.phase_ref, f32[792,128]{1,0:T(8,128)S(1)} %get-tuple-element.11.own_ref, f32[408,128]{1,0:T(8,128)S(1)} %collective-permute-done.4.pair_ref, f32[408,128]{1,0:T(8,128)S(1)} %collective-permute-done.5.other_ref, f32[64,4096]{1,0:T(8,128)S(1)} %get-tuple-element.14.x_ref, ...), custom_call_target="tpu_custom_call" | custom-call | tf_op jit(solution)/shard_map/apply_sweeps/pallas_call | solution.py:290
  (1 shorter events, 0.0 us)
Async XLA Ops:
  10.4 28.7 %all-to-all-start = ((f32[2,32,4096]{2,0,1:T(2,128)}), f32[2,32,4096]{2,0,1:T(2,128)S(1)}, u32[]{:S(2)}, u32[]{:S(2)}) async-start(f32[2,32,4096]{2,0,1:T(2,128)} %bitcast.9), calls=%async_computation | async-start | bytes 2097152 | tf_op jit(solution)/shard_map/all_to_all | solution.py:348
  16.8 9.5 %copy-start = (s32[32,2]{0,1:T(2,128)S(1)}, s32[32,2]{0,1:T(2,128)}, u32[]{:S(2)}) copy-start(s32[32,2]{0,1:T(2,128)} %param.5) | copy-start | bytes 772
  16.8 15.4 %collective-permute-start = (f32[8,4096]{1,0:T(8,128)S(1)}, f32[8,4096]{1,0:T(8,128)S(1)}, u32[]{:S(2)}, u32[]{:S(2)}) collective-permute-start(f32[8,4096]{1,0:T(8,128)S(1)} %bitcast.11), channel_id=1, source_target_pairs={{0,0},{1,1},{2,2},{3,3},{4,4},{5,5},{6,6},{7,7},{8,32},{9,33},{10,... | collective-permute-start | bytes 393224 | tf_op jit(solution)/shard_map/ppermute | solution.py:342
  21.5 10.8 %collective-permute-start.1 = (f32[8,4096]{1,0:T(8,128)S(1)}, f32[8,4096]{1,0:T(8,128)S(1)}, u32[]{:S(2)}, u32[]{:S(2)}) collective-permute-start(f32[8,4096]{1,0:T(8,128)S(1)} %bitcast.12), channel_id=1, source_target_pairs={{0,96},{1,97},{2,98},{3,99},{4,100},{5,101},{6,102},{7,103},{8,0},... | collective-permute-start | bytes 393224 | tf_op jit(solution)/shard_map/ppermute | solution.py:342
  21.5 11.9 %collective-permute-start.2 = (f32[8,4096]{1,0:T(8,128)S(1)}, f32[8,4096]{1,0:T(8,128)S(1)}, u32[]{:S(2)}, u32[]{:S(2)}) collective-permute-start(f32[8,4096]{1,0:T(8,128)S(1)} %bitcast.13), channel_id=1, source_target_pairs={{0,64},{1,65},{2,66},{3,67},{4,68},{5,69},{6,70},{7,71},{8,96},{9,... | collective-permute-start | bytes 393224 | tf_op jit(solution)/shard_map/ppermute | solution.py:342
  23.7 14.4 %collective-permute-start.3 = (f32[8,4096]{1,0:T(8,128)S(1)}, f32[8,4096]{1,0:T(8,128)S(1)}, u32[]{:S(2)}, u32[]{:S(2)}) collective-permute-start(f32[8,4096]{1,0:T(8,128)S(1)} %bitcast.14), channel_id=1, source_target_pairs={{0,32},{1,33},{2,34},{3,35},{4,36},{5,37},{6,38},{7,39},{8,64},{9,... | collective-permute-start | bytes 393224 | tf_op jit(solution)/shard_map/ppermute | solution.py:342
  40.8 3.9 %collective-permute-start.4 = (f32[408,128]{1,0:T(8,128)S(1)}, f32[408,128]{1,0:T(8,128)S(1)}, u32[]{:S(2)}, u32[]{:S(2)}) collective-permute-start(f32[408,128]{1,0:T(8,128)S(1)} %get-tuple-element.12), channel_id=1, source_target_pairs={{0,1},{1,0},{2,3},{3,2},{4,5},{5,4},{6,7},{7,6},{8,9},{9,8},{10,11... | collective-permute-start | bytes 626696 | tf_op jit(solution)/shard_map/ppermute | solution.py:314
  40.9 8.6 %collective-permute-start.5 = (f32[408,128]{1,0:T(8,128)S(1)}, f32[408,128]{1,0:T(8,128)S(1)}, u32[]{:S(2)}, u32[]{:S(2)}) collective-permute-start(f32[408,128]{1,0:T(8,128)S(1)} %get-tuple-element.13), channel_id=1, source_target_pairs={{1,2},{3,4},{5,6},{7,8},{9,10},{11,12},{13,14},{15,16},{17,18},{19... | collective-permute-start | bytes 626696 | tf_op jit(solution)/shard_map/ppermute | solution.py:315

commit v8 on v7

--- a/solution.py
+++ b/solution.py
@@ -208,7 +208,8 @@
     for j in range(SWEEPS):
         mine = jnp.broadcast_to(all_tau[j:j + 1], (SWEEPS, NB))
         scaled = coef[pl.ds(j * 32, 32)] * jnp.where(row < j, all_tau, mine)
-        coef[pl.ds(j * 32, 32)] = scaled
+        if j >= WIDE - 1:
+            coef[pl.ds(j * 32, 32)] = scaled
         count = 32 if j < WIDE else 16
         coef_half[pl.ds(j * 32, count)] = halves(scaled[:count], scaled[:count])
 

time: 55.6 us -> 55.6 us (level)
  no operation moved by 1% of the time
where the time goes in v8:
time: 55.6 us; the launch traced here: 55.3 us
  starting transfers between devices  19.6 us (35%)
  waiting for transfers between devices  17.5 us (31%)
  blocking collectives  10.4 us (19%)
  Pallas kernels  7.41 us (13%)
    ppermute x4, waiting for transfers between devices, sweep_pieces(): pieces.append(lax.ppermute(mine, ('col', 'row'), pairs))  11.6 us
    all_to_all x1, blocking collectives, sweep_pieces(): lax.all_to_all(reflectors.reshape(width, -1), 'row', split_axis=0, concat...  10.4 us
    ppermute x4, starting transfers between devices, sweep_pieces(): pieces.append(lax.ppermute(mine, ('col', 'row'), pairs))  9.48 us
    pallas_call x2, Pallas kernels, call(): pl.pallas_call(kernel, out_shape=tuple((jax.ShapeDtypeStruct(*x) for x in...  7.41 us
    all_to_all x1, starting transfers between devices, per_device(): lax.all_to_all(eigenvectors.reshape(2, -1, OWN * NB), 'row', split_axis=1...  6.31 us
    ppermute x1, waiting for transfers between devices, back_transform(): other = lax.ppermute(to_other, 'row', across)  4.86 us
    ppermute x1, starting transfers between devices, back_transform(): other = lax.ppermute(to_other, 'row', across)  3.76 us
  transfers between devices with their start and end apart: 7, of which 5 were waited for; matrix products, arithmetic and copies ran while one was open for 0% of the time, Pallas kernels for 0%

profile of v8, /device:TPU:24, one launch (start us, length us, event | category | flops | bytes accessed | tf_op | source)
XLA Modules:
  0.0 55.3 jit_solution(17701118201247970203)
XLA Ops:
  0.0 10.4 %all_to_all.17 = f32[8,1,4096]{2,1,0:T(1,128)S(1)} all-to-all(f32[8,1,4096]{2,1,0:T(1,128)} %bitcast.10), channel_id=1, replica_groups={{0,1,2,3,4,5,6,7},{8,9,10,11,12,13,14,15},{16,17,18,19,20,21,22,23},{24..., dimensions={0} | all-to-all | bytes 262144 | tf_op jit(solution)/shard_map/all_to_all | solution.py:333
  10.4 6.3 %all-to-all-start = ((f32[2,32,4096]{2,0,1:T(2,128)}), f32[2,32,4096]{2,0,1:T(2,128)S(1)}, u32[]{:S(2)}, u32[]{:S(2)}) async-start(f32[2,32,4096]{2,0,1:T(2,128)} %bitcast.9), calls=%async_computation | async-start | bytes 2097152 | tf_op jit(solution)/shard_map/all_to_all | solution.py:349
  16.7 0.1 copy.8
  16.8 0.0 copy-start
  16.8 4.6 %collective-permute-start = (f32[8,4096]{1,0:T(8,128)S(1)}, f32[8,4096]{1,0:T(8,128)S(1)}, u32[]{:S(2)}, u32[]{:S(2)}) collective-permute-start(f32[8,4096]{1,0:T(8,128)S(1)} %bitcast.11), channel_id=1, source_target_pairs={{0,0},{1,1},{2,2},{3,3},{4,4},{5,5},{6,6},{7,7},{8,32},{9,33},{10,... | collective-permute-start | bytes 393224 | tf_op jit(solution)/shard_map/ppermute | solution.py:343
  21.5 0.1 collective-permute-start.1
  21.5 2.1 %collective-permute-start.2 = (f32[8,4096]{1,0:T(8,128)S(1)}, f32[8,4096]{1,0:T(8,128)S(1)}, u32[]{:S(2)}, u32[]{:S(2)}) collective-permute-start(f32[8,4096]{1,0:T(8,128)S(1)} %bitcast.13), channel_id=1, source_target_pairs={{0,64},{1,65},{2,66},{3,67},{4,68},{5,69},{6,70},{7,71},{8,96},{9,... | collective-permute-start | bytes 393224 | tf_op jit(solution)/shard_map/ppermute | solution.py:343
  23.7 2.7 %collective-permute-start.3 = (f32[8,4096]{1,0:T(8,128)S(1)}, f32[8,4096]{1,0:T(8,128)S(1)}, u32[]{:S(2)}, u32[]{:S(2)}) collective-permute-start(f32[8,4096]{1,0:T(8,128)S(1)} %bitcast.14), channel_id=1, source_target_pairs={{0,32},{1,33},{2,34},{3,35},{4,36},{5,37},{6,38},{7,39},{8,64},{9,... | collective-permute-start | bytes 393224 | tf_op jit(solution)/shard_map/ppermute | solution.py:343
  26.3 0.0 copy-done
  26.3 0.1 copy.5.ranges_ref
  26.4 5.9 %collective-permute-done.v0 = f32[8,4096]{1,0:T(8,128)S(1)} collective-permute-done((f32[8,4096]{1,0:T(8,128)S(1)}, f32[8,4096]{1,0:T(8,128)S(1)}, u32[]{:S(2)}, u32[]{:S(2)}) %collective-permute-start) | collective-permute-done | bytes 131104 | tf_op jit(solution)/shard_map/ppermute | solution.py:343
  32.3 0.0 collective-permute-done.1.v1
  32.3 1.2 %collective-permute-done.2.v2 = f32[8,4096]{1,0:T(8,128)S(1)} collective-permute-done((f32[8,4096]{1,0:T(8,128)S(1)}, f32[8,4096]{1,0:T(8,128)S(1)}, u32[]{:S(2)}, u32[]{:S(2)}) %collective-permute-start.2) | collective-permute-done | bytes 131104 | tf_op jit(solution)/shard_map/ppermute | solution.py:343
  33.5 4.6 %collective-permute-done.3.v3 = f32[8,4096]{1,0:T(8,128)S(1)} collective-permute-done((f32[8,4096]{1,0:T(8,128)S(1)}, f32[8,4096]{1,0:T(8,128)S(1)}, u32[]{:S(2)}, u32[]{:S(2)}) %collective-permute-start.3) | collective-permute-done | bytes 131104 | tf_op jit(solution)/shard_map/ppermute | solution.py:343
  38.0 1.1 %all-to-all-done = f32[2,32,4096]{2,0,1:T(2,128)S(1)} async-done(((f32[2,32,4096]{2,0,1:T(2,128)}), f32[2,32,4096]{2,0,1:T(2,128)S(1)}, u32[]{:S(2)}, u32[]{:S(2)}) %all-to-all-start) | async-done | bytes 1048608 | tf_op jit(solution)/shard_map/all_to_all | solution.py:349
  39.1 1.7 %inner_products.1 = (f32[792,128]{1,0:T(8,128)S(1)}, f32[408,128]{1,0:T(8,128)S(1)}, f32[408,128]{1,0:T(8,128)S(1)}, bf16[2048,128]{1,0:T(8,128)(2,1)S(1)}, bf16...) custom-call(s32[32,2]{1,0:T(8,128)S(1)} %copy.5.ranges_ref, f32[32,2,4096]{2,1,0:T(2,128)S(1)} %bitcast.8, ...), custom_call_target="tpu_custom_call" | custom-call | tf_op jit(solution)/shard_map/inner_products/pallas_call | solution.py:291
  40.8 0.1 collective-permute-start.4
  40.9 3.8 %collective-permute-start.5 = (f32[408,128]{1,0:T(8,128)S(1)}, f32[408,128]{1,0:T(8,128)S(1)}, u32[]{:S(2)}, u32[]{:S(2)}) collective-permute-start(f32[408,128]{1,0:T(8,128)S(1)} %get-tuple-element.13), channel_id=1, source_target_pairs={{1,2},{3,4},{5,6},{7,8},{9,10},{11,12},{13,14},{15,16},{17,18},{19... | collective-permute-start | bytes 626696 | tf_op jit(solution)/shard_map/ppermute | solution.py:316
  44.7 0.0 collective-permute-done.4.pair_ref
  44.7 4.9 %collective-permute-done.5.other_ref = f32[408,128]{1,0:T(8,128)S(1)} collective-permute-done((f32[408,128]{1,0:T(8,128)S(1)}, f32[408,128]{1,0:T(8,128)S(1)}, u32[]{:S(2)}, u32[]{:S(2)}) %collective-permute-start.5) | collective-permute-done | bytes 208928 | tf_op jit(solution)/shard_map/ppermute | solution.py:316
  49.6 5.7 %apply_sweeps.1 = f32[64,4096]{1,0:T(8,128)} custom-call(s32[32]{0:T(128)S(1)} %and_select_fusion.phase_ref, f32[792,128]{1,0:T(8,128)S(1)} %get-tuple-element.11.own_ref, f32[408,128]{1,0:T(8,128)S(1)} %collective-permute-done.4.pair_ref, f32[408,128]{1,0:T(8,128)S(1)} %collective-permute-done.5.other_ref, f32[64,4096]{1,0:T(8,128)S(1)} %get-tuple-element.14.x_ref, ...), custom_call_target="tpu_custom_call" | custom-call | tf_op jit(solution)/shard_map/apply_sweeps/pallas_call | solution.py:291
  (1 shorter events, 0.0 us)
Async XLA Ops:
  10.4 28.7 %all-to-all-start = ((f32[2,32,4096]{2,0,1:T(2,128)}), f32[2,32,4096]{2,0,1:T(2,128)S(1)}, u32[]{:S(2)}, u32[]{:S(2)}) async-start(f32[2,32,4096]{2,0,1:T(2,128)} %bitcast.9), calls=%async_computation | async-start | bytes 2097152 | tf_op jit(solution)/shard_map/all_to_all | solution.py:349
  16.8 9.5 %copy-start = (s32[32,2]{0,1:T(2,128)S(1)}, s32[32,2]{0,1:T(2,128)}, u32[]{:S(2)}) copy-start(s32[32,2]{0,1:T(2,128)} %param.5) | copy-start | bytes 772
  16.8 15.4 %collective-permute-start = (f32[8,4096]{1,0:T(8,128)S(1)}, f32[8,4096]{1,0:T(8,128)S(1)}, u32[]{:S(2)}, u32[]{:S(2)}) collective-permute-start(f32[8,4096]{1,0:T(8,128)S(1)} %bitcast.11), channel_id=1, source_target_pairs={{0,0},{1,1},{2,2},{3,3},{4,4},{5,5},{6,6},{7,7},{8,32},{9,33},{10,... | collective-permute-start | bytes 393224 | tf_op jit(solution)/shard_map/ppermute | solution.py:343
  21.5 10.8 %collective-permute-start.1 = (f32[8,4096]{1,0:T(8,128)S(1)}, f32[8,4096]{1,0:T(8,128)S(1)}, u32[]{:S(2)}, u32[]{:S(2)}) collective-permute-start(f32[8,4096]{1,0:T(8,128)S(1)} %bitcast.12), channel_id=1, source_target_pairs={{0,96},{1,97},{2,98},{3,99},{4,100},{5,101},{6,102},{7,103},{8,0},... | collective-permute-start | bytes 393224 | tf_op jit(solution)/shard_map/ppermute | solution.py:343
  21.5 11.9 %collective-permute-start.2 = (f32[8,4096]{1,0:T(8,128)S(1)}, f32[8,4096]{1,0:T(8,128)S(1)}, u32[]{:S(2)}, u32[]{:S(2)}) collective-permute-start(f32[8,4096]{1,0:T(8,128)S(1)} %bitcast.13), channel_id=1, source_target_pairs={{0,64},{1,65},{2,66},{3,67},{4,68},{5,69},{6,70},{7,71},{8,96},{9,... | collective-permute-start | bytes 393224 | tf_op jit(solution)/shard_map/ppermute | solution.py:343
  23.7 14.4 %collective-permute-start.3 = (f32[8,4096]{1,0:T(8,128)S(1)}, f32[8,4096]{1,0:T(8,128)S(1)}, u32[]{:S(2)}, u32[]{:S(2)}) collective-permute-start(f32[8,4096]{1,0:T(8,128)S(1)} %bitcast.14), channel_id=1, source_target_pairs={{0,32},{1,33},{2,34},{3,35},{4,36},{5,37},{6,38},{7,39},{8,64},{9,... | collective-permute-start | bytes 393224 | tf_op jit(solution)/shard_map/ppermute | solution.py:343
  40.8 3.9 %collective-permute-start.4 = (f32[408,128]{1,0:T(8,128)S(1)}, f32[408,128]{1,0:T(8,128)S(1)}, u32[]{:S(2)}, u32[]{:S(2)}) collective-permute-start(f32[408,128]{1,0:T(8,128)S(1)} %get-tuple-element.12), channel_id=1, source_target_pairs={{0,1},{1,0},{2,3},{3,2},{4,5},{5,4},{6,7},{7,6},{8,9},{9,8},{10,11... | collective-permute-start | bytes 626696 | tf_op jit(solution)/shard_map/ppermute | solution.py:315
  40.9 8.6 %collective-permute-start.5 = (f32[408,128]{1,0:T(8,128)S(1)}, f32[408,128]{1,0:T(8,128)S(1)}, u32[]{:S(2)}, u32[]{:S(2)}) collective-permute-start(f32[408,128]{1,0:T(8,128)S(1)} %get-tuple-element.13), channel_id=1, source_target_pairs={{1,2},{3,4},{5,6},{7,8},{9,10},{11,12},{13,14},{15,16},{17,18},{19... | collective-permute-start | bytes 626696 | tf_op jit(solution)/shard_map/ppermute | solution.py:316
